TPU v7x, 128 devices: a whole 4x4x4 slice. The times are simulated.
128 devices in a mesh: wide: 16 (over x, z), narrow: 8 (over y, core).
Axes of the slice: x: 4, y: 4, z: 4, core: 2. Of those that a mesh axis runs over, the one named last changes fastest.
Arguments:
- pressure: float32 [128, 128, 1024], P('wide', 'narrow'), may hold values from -6 to 6
- divergence: float32 [128, 128, 1024], P('wide', 'narrow'), may hold values from -6 to 6
- mobility: float32 [128, 128, 1024], P('wide', 'narrow'), may hold values from 0.1 to 10
Outputs:
- pressure_out: float32 [128, 128, 1024], P('wide', 'narrow')
- residual_out: float32 [128, 128, 1024], P('wide', 'narrow')
All inputs are finite; a program needn't handle non-finite values.
Results may differ from a plain program's by a relative error of at most 0.00004.
Values sent between devices are 32-bit elements; how exact they have to be, the bound alone decides.
No kernel may reach another device: no remote copies, remote signals or barrier semaphores. Data moves between devices by JAX's collectives and lax.ppermute only.
A program may use at most 128 MiB of HBM per device.

v0:
```python
import jax
import jax.numpy as jnp
from jax import lax
from jax.experimental import pallas as pl
from jax.experimental.pallas import tpu as pltpu
from jax.sharding import Mesh, PartitionSpec as P

OMEGA = 0.8
AX = ("wide", "ny", "core")
F32 = jnp.float32
LIMIT = 48 * 1024 * 1024


def iota(shape, dim):
    return lax.broadcasted_iota(jnp.int32, shape, dim)


def following(x, dim):
    return pltpu.roll(x, x.shape[dim] - 1, dim)


def preceding(x, dim):
    return pltpu.roll(x, 1, dim)


def add_z_ends(out, c, v):
    length = out.shape[1]
    lane = iota((out.shape[0], 128), 1)
    if length == 128:
        return out + jnp.where((lane == 0) | (lane == 127), 0.5 * c * v, 0.0)
    low = out[:, :128] + jnp.where(lane == 0, 0.5 * c[:, :128] * v[:, :128], 0.0)
    high = out[:, -128:] + jnp.where(lane == 127, 0.5 * c[:, -128:] * v[:, -128:], 0.0)
    parts = [low, high] if length == 256 else [low, out[:, 128:-128], high]
    return jnp.concatenate(parts, axis=1)


def row_operator(v, below, above, c, fa_below, fa_above, fb, fz):
    gb = fb * (following(v, 0) - v)
    gz = fz * (following(v, 1) - v)
    out = fa_above * (v - above) + fa_below * (v - below)
    out = out + (preceding(gb, 0) - gb) + (preceding(gz, 1) - gz)
    return add_z_ends(out, c, v)


def row_diagonal(c, fa_below, fa_above, fb, fz):
    out = fa_above + fa_below + (fb + preceding(fb, 0)) + (fz + preceding(fz, 1))
    return add_z_ends(out, c, jnp.ones_like(c))


def half_compress(low, high, dim):
    length = low.shape[dim]
    at = iota(low.shape, dim)
    index = (2 * at) % length
    first = jnp.take_along_axis(low, index, axis=dim)
    if high is None:
        return jnp.where(at < length // 2, first, 0.0)
    return jnp.where(at < length // 2, first, jnp.take_along_axis(high, index, axis=dim))


def pair_sums(x, dim, tile):
    x = x + following(x, dim)
    count = x.shape[dim] // tile

    def piece(r, l, t):
        if dim == 0:
            return x[8 * t : 8 * t + 8, 128 * l : 128 * l + 128]
        return x[8 * r : 8 * r + 8, 128 * t : 128 * t + 128]

    rows, lanes = x.shape[0] // 8, x.shape[1] // 128
    half = max(count // 2, 1)
    if dim == 0:
        out = [
            [half_compress(piece(0, l, 2 * t), piece(0, l, 2 * t + 1) if count > 1 else None, 0) for l in range(lanes)]
            for t in range(half)
        ]
    else:
        out = [
            [half_compress(piece(r, 0, 2 * t), piece(r, 0, 2 * t + 1) if count > 1 else None, 1) for t in range(half)]
            for r in range(rows)
        ]
    joined = [line[0] if len(line) == 1 else jnp.concatenate(line, axis=1) for line in out]
    return joined[0] if len(joined) == 1 else jnp.concatenate(joined, axis=0)


def coarse_sum(first, second):
    return pair_sums(pair_sums(first + second, 0, 8), 1, 128)


def repeat_lanes(x, block):
    source = block // 2
    index = iota((8, 128), 1) // 2 + 64 * (block % 2)
    return jnp.take_along_axis(x[:, 128 * source : 128 * source + 128], index, axis=1)


def take_rows(x, index):
    pieces = [
        jnp.take_along_axis(x[:, k : k + 128], index, axis=0) for k in range(0, x.shape[1], 128)
    ]
    return pieces[0] if len(pieces) == 1 else jnp.concatenate(pieces, axis=1)


def widen(x, blocks):
    pieces = [repeat_lanes(x, k) for k in range(blocks)]
    return pieces[0] if len(pieces) == 1 else jnp.concatenate(pieces, axis=1)


def scalars():
    wide, ny, core = lax.axis_index("wide"), lax.axis_index("ny"), lax.axis_index("core")
    sizes = [lax.axis_size(name) for name in AX]
    narrow = ny * sizes[2] + core
    inside = [
        jnp.where(flag, 1.0, 0.0).astype(F32)
        for flag in (wide > 0, wide < sizes[0] - 1, narrow > 0, narrow < sizes[1] * sizes[2] - 1)
    ]
    return wide, narrow, core, inside


def call(kernel, outs, scratch, *args, flops=1_000_000):
    vmem = pl.BlockSpec(memory_space=pltpu.VMEM)
    size = 4 * sum(a.size for a in args)
    return pl.pallas_call(
        kernel,
        out_shape=[jax.ShapeDtypeStruct(s, F32) for s in outs],
        in_specs=[vmem] * len(args),
        out_specs=[vmem] * len(outs),
        scratch_shapes=[pltpu.VMEM(s, F32) for s in scratch],
        compiler_params=pltpu.CompilerParams(vmem_limit_bytes=LIMIT),
        cost_estimate=pl.CostEstimate(flops=flops, bytes_accessed=size, transcendentals=0),
    )(*args)


def pack_zero(p, d, m, left, right, to_left, to_right):
    _, _, _, (low, high, _, _) = scalars()
    at = iota((8, 1024), 0)
    for r in range(14):
        a = r - 3
        for side, out in ((0, to_left), (1, to_right)):
            tile = slice(8 * side, 8 * side + 8)
            if a < 0:
                vp, vm = left[r, tile] * low, left[3 + r, tile] * low
                vd = left[5 + r, tile] * low if r > 0 else jnp.zeros_like(vp)
            elif a < 8:
                vp, vm, vd = p[a, tile], m[a, tile], d[a, tile]
            else:
                vp, vm = right[a - 8, tile] * high, right[a - 5, tile] * high
                vd = right[a - 2, tile] * high if a < 10 else jnp.zeros_like(vp)
            if side == 0:
                vm, vd = pltpu.roll(vm, 3, 0), pltpu.roll(vd, 6, 0)
                out[r] = jnp.where(at < 3, vp, jnp.where(at < 6, vm, vd))
            else:
                vm, vd = pltpu.roll(vm, 5, 0), pltpu.roll(vd, 2, 0)
                out[r] = jnp.where(at >= 5, vp, jnp.where(at >= 2, vm, vd))


def faces(c, rows, fa, fb, fz, w, cols, mask_b):
    lo, hi = rows
    length = c.shape[2]
    last = iota((cols, length), 1) == length - 1

    def one_face(r, carry):
        fa[r] = 0.5 * (c[r] + c[r + 1])
        return carry

    lax.fori_loop(lo - 1, hi, one_face, 0)

    def one(r, carry):
        here = c[r]
        b = 0.5 * (here + following(here, 0))
        z = jnp.where(last, 0.0, 0.5 * (here + following(here, 1)))
        fb[r], fz[r] = b, z
        diagonal = row_diagonal(here, fa[r - 1], fa[r], b, z)
        w[r] = jnp.where(here > 0.0, OMEGA / diagonal, 0.0)
        return carry

    lax.fori_loop(lo, hi, one, 0)


def sweep(source, target, s, c, fa, fb, fz, w, rows):
    def one(r, carry):
        v = source[r]
        a = row_operator(v, source[r - 1], source[r + 1], c[r], fa[r - 1], fa[r], fb[r], fz[r])
        target[r] = v + w[r] * (s[r] - a)
        return carry

    lax.fori_loop(rows[0], rows[1], one, 0)


def residual_row(v, s, c, fa, fb, fz, r):
    return s[r] - row_operator(v[r], v[r - 1], v[r + 1], c[r], fa[r - 1], fa[r], fb[r], fz[r])


def level_zero(p, d, m, left, right, nleft, nright, field, me, de, s1, c1, up, down, v, u, fa, fb, fz, w):
    _, _, _, (low, high, nlow, nhigh) = scalars()
    at = iota((8, 1024), 0)
    for r in range(14):
        a = r - 3
        if a < 0:
            v[r, 0:16], me[r, 0:16] = left[r] * low, left[3 + r] * low
            de[r, 0:16] = left[5 + r] * low if r > 0 else jnp.zeros((16, 1024), F32)
        elif a < 8:
            v[r, 0:16], me[r, 0:16], de[r, 0:16] = p[a], m[a], d[a]
        else:
            v[r, 0:16], me[r, 0:16] = right[a - 8] * high, right[a - 5] * high
            de[r, 0:16] = right[a - 2] * high if a < 10 else jnp.zeros((16, 1024), F32)
        x, y = nright[r] * nhigh, nleft[r] * nlow
        v[r, 16:24] = jnp.where(at < 3, x, jnp.where(at >= 5, y, 0.0))
        x3, y3 = pltpu.roll(x, 5, 0), pltpu.roll(y, 3, 0)
        me[r, 16:24] = jnp.where(at < 3, x3, jnp.where(at >= 5, y3, 0.0))
        x6, y6 = pltpu.roll(x, 2, 0), pltpu.roll(y, 6, 0)
        de[r, 16:24] = jnp.where(at < 2, x6, jnp.where(at >= 6, y6, 0.0))
    faces(me, (1, 13), fa, fb, fz, w, 24, None)
    u[0], u[13] = v[0], v[13]
    sweep(v, u, de, me, fa, fb, fz, w, (1, 13))
    sweep(u, v, de, me, fa, fb, fz, w, (2, 12))
    field[...] = v[3:11, 0:16]

    def coarse(i, carry):
        r = 2 * i + 3
        x = residual_row(v, de, me, fa, fb, fz, r)[0:16]
        y = residual_row(v, de, me, fa, fb, fz, r + 1)[0:16]
        s1[i] = 0.5 * coarse_sum(x, y)
        c1[i] = 0.125 * coarse_sum(me[r, 0:16], me[r + 1, 0:16])
        return carry

    lax.fori_loop(0, 4, coarse, 0)
    up[0:3], down[0:3] = s1[1:4], s1[0:3]
    up[3:7], down[3:7] = c1[...], c1[...]


def pack_one(s, c, left, right, to_left, to_right):
    _, _, _, (low, high, _, _) = scalars()
    at = iota((8, 512), 0)
    for r in range(12):
        a = r - 4
        if a < 0:
            vc = left[3 + r] * low
            vs = left[r - 1] * low if r > 0 else jnp.zeros_like(vc)
        elif a < 4:
            vs, vc = s[a], c[a]
        else:
            vc = right[a - 1] * high
            vs = right[a - 4] * high if a < 7 else jnp.zeros_like(vc)
        to_left[r] = jnp.where(at < 4, vc, pltpu.roll(vs, 4, 0))
        to_right[r] = jnp.where(at >= 4, vc, pltpu.roll(vs, 4, 0))


def level_one(s, c, left, right, nleft, nright, f0, se, ce, field, send, keep, up, down, v, u, fa, fb, fz, w):
    _, _, core, (low, high, nlow, nhigh) = scalars()
    at = iota((8, 512), 0)
    for r in range(12):
        a = r - 4
        if a < 0:
            ce[r, 0:8] = left[3 + r] * low
            se[r, 0:8] = left[r - 1] * low if r > 0 else jnp.zeros((8, 512), F32)
        elif a < 4:
            se[r, 0:8], ce[r, 0:8] = s[a], c[a]
        else:
            ce[r, 0:8] = right[a - 1] * high
            se[r, 0:8] = right[a - 4] * high if a < 7 else jnp.zeros((8, 512), F32)
        x, y = nright[r] * nhigh, nleft[r] * nlow
        ce[r, 8:16] = jnp.where(at < 4, x, y)
        se[r, 8:16] = jnp.where(at < 4, pltpu.roll(x, 4, 0), pltpu.roll(y, 4, 0))
    faces(ce, (2, 10), fa, fb, fz, w, 16, None)

    def first(r, carry):
        u[r] = w[r] * se[r]
        return carry

    lax.fori_loop(2, 10, first, 0)
    sweep(u, v, se, ce, fa, fb, fz, w, (3, 9))
    field[...] = v[4:8, 0:8]
    rows = iota((8, 256), 0)
    index = iota((8, 256), 0) % 4
    mine = rows // 4 == core
    for i in range(2):
        r = 2 * i + 4
        x = residual_row(v, se, ce, fa, fb, fz, r)[0:8]
        y = residual_row(v, se, ce, fa, fb, fz, r + 1)[0:8]
        s2 = 0.5 * coarse_sum(x, y)
        c2 = 0.125 * coarse_sum(ce[r, 0:8], ce[r + 1, 0:8])
        s2 = jnp.where(mine, take_rows(s2, index[:, :128]), 0.0)
        c2 = jnp.where(mine, take_rows(c2, index[:, :128]), 0.0)
        send[i] = jnp.where(core == 0, c2, s2)
        keep[i] = jnp.where(core == 0, s2, c2)
    for r in range(3):
        for t in range(2):
            up[2 * r + t] = f0[5 + r, 8 * t : 8 * t + 8]
            down[2 * r + t] = f0[r, 8 * t : 8 * t + 8]
    for r in range(2):
        both = jnp.concatenate([field[2 * r], field[2 * r + 1]], axis=1)
        up[6 + r] = both
        down[6 + r] = both


def pack_up(f0, f1, left, right, to_left, to_right):
    _, _, _, (low, high, _, _) = scalars()
    at = iota((8, 1024), 0)
    for r in range(14):
        for side, out in ((0, to_left), (1, to_right)):
            tile = slice(8 * side, 8 * side + 8)
            if r < 3:
                x = left[2 * r + side] * low
            elif r < 11:
                x = f0[r - 3, tile]
            else:
                x = right[2 * (r - 11) + side] * high
            if r < 2:
                y = left[6 + r] * low
            elif r < 4:
                y = jnp.concatenate([f1[2 * r - 4], f1[2 * r - 3]], axis=1)
            elif r < 6:
                y = right[2 + r] * high
            else:
                y = None
            if y is not None:
                y = pltpu.roll(y, 4, 0)
                x = jnp.where(at < 4, x, y) if side == 0 else jnp.where(at >= 4, x, y)
            out[r] = x


def level_up(me, de, w, f0, left, right, nleft, nright, se, ce, f1, e2, out, res, v, u, fa, fb, fz, v1, u1, fa1, fb1, fz1, w1):
    _, _, _, (low, high, nlow, nhigh) = scalars()
    at = iota((8, 512), 0)
    half = iota((8, 128), 0)
    for r in range(12):
        if r < 4:
            f = left[6 + r // 2][:, 512 * (r % 2) : 512 * (r % 2) + 512] * low
        elif r < 8:
            f = f1[r - 4]
        else:
            f = right[2 + r // 2][:, 512 * (r % 2) : 512 * (r % 2) + 512] * high
        x = nright[r // 2][:, 512 * (r % 2) : 512 * (r % 2) + 512] * nhigh
        y = nleft[r // 2][:, 512 * (r % 2) : 512 * (r % 2) + 512] * nlow
        g = jnp.where(at < 4, pltpu.roll(x, 4, 0), pltpu.roll(y, 4, 0))
        e = e2[r // 2]
        own = widen(take_rows(e, 2 + half // 2), 4)
        beside = widen(take_rows(e, jnp.where(half < 4, 6 + half // 2, (half - 4) // 2)), 4)
        v1[r, 0:8] = f + jnp.where(ce[r, 0:8] > 0.0, own, 0.0)
        v1[r, 8:16] = g + jnp.where(ce[r, 8:16] > 0.0, beside, 0.0)
    faces(ce, (1, 11), fa1, fb1, fz1, w1, 16, None)
    sweep(v1, u1, se, ce, fa1, fb1, fz1, w1, (1, 11))
    sweep(u1, v1, se, ce, fa1, fb1, fz1, w1, (2, 10))
    zero = iota((8, 1024), 0)
    for r in range(14):
        if r < 3:
            f = [left[2 * r] * low, left[2 * r + 1] * low]
        elif r < 11:
            f = [f0[r - 3, 0:8], f0[r - 3, 8:16]]
        else:
            f = [right[2 * (r - 11)] * high, right[2 * (r - 11) + 1] * high]
        x, y = nright[r] * nhigh, nleft[r] * nlow
        f.append(jnp.where(zero < 3, x, jnp.where(zero >= 5, y, 0.0)))
        e = v1[(r + 5) // 2]
        pieces = (
            (e[0:8], half // 2),
            (e[0:8], 4 + half // 2),
            (e[8:16], jnp.where(half < 4, half // 2, 4 + half // 2)),
        )
        for t, (part, index) in enumerate(pieces):
            fine = widen(take_rows(part, index), 8)
            tile = slice(8 * t, 8 * t + 8)
            v[r, tile] = f[t] + jnp.where(me[r, tile] > 0.0, fine, 0.0)

    def one_face(r, carry):
        fa[r] = 0.5 * (me[r] + me[r + 1])
        return carry

    lax.fori_loop(0, 13, one_face, 0)
    last = iota((24, 1024), 1) == 1023

    def one(r, carry):
        here = me[r]
        fb[r] = 0.5 * (here + following(here, 0))
        fz[r] = jnp.where(last, 0.0, 0.5 * (here + following(here, 1)))
        return carry

    lax.fori_loop(1, 13, one, 0)
    sweep(v, u, de, me, fa, fb, fz, w, (1, 13))
    sweep(u, v, de, me, fa, fb, fz, w, (2, 12))
    out[...] = v[3:11, 0:16]

    def final(r, carry):
        res[r] = residual_row(v, de, me, fa, fb, fz, r + 3)[0:16]
        return carry

    lax.fori_loop(0, 8, final, 0)


def shifted(x, step):
    zero = jnp.zeros((1,) + x.shape[1:], F32)
    return jnp.concatenate([x[1:], zero] if step > 0 else [zero, x[:-1]], axis=0)


class Whole:
    def __init__(self, c, cols, length):
        b, z = iota(c.shape, 1), iota(c.shape, 2)
        valid = (b < cols) & (z < length)
        self.fa = 0.5 * (c + shifted(c, 1))
        self.fa_below = 0.5 * (c + shifted(c, -1))
        self.fb = jnp.where(b < cols - 1, 0.5 * (c + following(c, 1)), 0.0)
        self.fz = jnp.where(z < length - 1, 0.5 * (c + following(c, 2)), 0.0)
        half = 0.5 * c
        self.ends = jnp.where(b == 0, half, 0.0) + jnp.where(b == cols - 1, half, 0.0)
        self.ends = self.ends + jnp.where(z == 0, half, 0.0) + jnp.where(z == length - 1, half, 0.0)
        diagonal = self.fa + self.fa_below + self.fb + preceding(self.fb, 1)
        diagonal = diagonal + self.fz + preceding(self.fz, 2) + self.ends
        self.w = jnp.where(valid, OMEGA / diagonal, 0.0)

    def operator(self, v):
        gb = self.fb * (following(v, 1) - v)
        gz = self.fz * (following(v, 2) - v)
        out = self.fa * (v - shifted(v, 1)) + self.fa_below * (v - shifted(v, -1)) + self.ends * v
        return out + (preceding(gb, 1) - gb) + (preceding(gz, 2) - gz)

    def sweep(self, v, s):
        return v + self.w * (s - self.operator(v))


def coarsen_whole(x):
    return jnp.stack([coarse_sum(x[a], x[a + 1]) for a in range(0, x.shape[0], 2)])


def refine_row(x, cols_tiles, blocks):
    half = iota((8, 128), 0)
    tiles = []
    for t in range(cols_tiles):
        source = x[8 * (t // 2) : 8 * (t // 2) + 8]
        tiles.append(widen(take_rows(source, half // 2 + 4 * (t % 2)), blocks))
    return tiles[0] if cols_tiles == 1 else jnp.concatenate(tiles, axis=0)


def refine_whole(x, cols_tiles):
    rows = [refine_row(x[a], cols_tiles, 1) for a in range(x.shape[0])]
    return jnp.stack([rows[a // 2] for a in range(2 * x.shape[0])])


def multiply(x, y):
    out = [[None] * 4 for _ in range(4)]
    for i in range(4):
        for j in range(4):
            for k in range(4):
                if x[i][k] is not None and y[k][j] is not None:
                    term = x[i][k] * y[k][j]
                    out[i][j] = term if out[i][j] is None else out[i][j] + term
    return out


def apply(x, y):
    out = []
    for i in range(4):
        total = None
        for k in range(4):
            if x[i][k] is not None:
                term = x[i][k] * y[k]
                total = term if total is None else total + term
        out.append(total)
    return out


def inverse(x):
    x = [[jnp.zeros((8, 128), F32) if e is None else e for e in line] for line in x]
    for k in range(4):
        pivot = 1.0 / x[k][k]
        line = [pivot if j == k else x[k][j] * pivot for j in range(4)]
        for i in range(4):
            if i != k:
                factor = x[i][k]
                x[i] = [-factor * pivot if j == k else x[i][j] - factor * line[j] for j in range(4)]
        x[k] = line
    return x


def each(x, move):
    return [[None if e is None else move(e) for e in line] for line in x]


def exact(s, c):
    length = 16
    lane = iota((8, 128), 1)
    row = iota((8, 128), 0)
    valid = lane < length

    def line(x, a, b):
        picked = jnp.take_along_axis(x[a], jnp.full((8, 128), b, jnp.int32), axis=0)
        return jnp.where(valid, picked, 0.0)

    cs = [line(c, k // 2, k % 2) for k in range(4)]
    rhs = [line(s, k // 2, k % 2) for k in range(4)]
    below = [[None] * 4 for _ in range(4)]
    above = [[None] * 4 for _ in range(4)]
    centre = [[None] * 4 for _ in range(4)]
    for k in range(4):
        here = cs[k]
        upper = 0.5 * (here + following(here, 1))
        lower = 0.5 * (here + preceding(here, 1))
        fa, fb = 0.5 * (here + cs[k ^ 2]), 0.5 * (here + cs[k ^ 1])
        diagonal = upper + lower + fa + fb + here
        centre[k][k] = jnp.where(valid, diagonal, 1.0)
        centre[k][k ^ 2], centre[k][k ^ 1] = -fa, -fb
        above[k][k] = jnp.where(lane < length - 1, -upper, 0.0)
        below[k][k] = jnp.where((lane > 0) & valid, -lower, 0.0)
    step = 1
    while step < length:
        ahead = lambda e, step=step: pltpu.roll(e, 128 - step, 1)
        behind = lambda e, step=step: pltpu.roll(e, step, 1)
        solved = inverse(centre)
        t, u, q = multiply(solved, below), multiply(solved, above), apply(solved, rhs)
        t_ahead, u_behind = each(t, ahead), each(u, behind)
        x, y = multiply(below, u_behind), multiply(above, t_ahead)
        centre = [
            [jnp.zeros((8, 128), F32) if centre[i][j] is None else centre[i][j] for j in range(4)]
            for i in range(4)
        ]
        centre = [[centre[i][j] - x[i][j] - y[i][j] for j in range(4)] for i in range(4)]
        x, y = apply(below, [behind(e) for e in q]), apply(above, [ahead(e) for e in q])
        rhs = [rhs[i] - x[i] - y[i] for i in range(4)]
        if 2 * step < length:
            below = each(multiply(below, each(t, behind)), lambda e: -e)
            above = each(multiply(above, each(u, ahead)), lambda e: -e)
        step *= 2
    solved = [jnp.where(valid, e, 0.0) for e in apply(inverse(centre), rhs)]
    return jnp.stack(
        [
            jnp.where(row == 0, solved[2 * a], jnp.where(row == 1, solved[2 * a + 1], 0.0))
            for a in range(2)
        ]
    )


def descend(s, c, cols, length):
    if c.shape[0] == 2:
        return exact(s, c)
    level = Whole(c, cols, length)
    v = level.w * s
    v = level.sweep(v, s)
    r = s - level.operator(v)
    e = descend(0.5 * coarsen_whole(r), 0.125 * coarsen_whole(c), cols // 2, length // 2)
    v = v + refine_whole(e, c.shape[1] // 8)
    v = level.sweep(v, s)
    return level.sweep(v, s)


def coarse_levels(mine, other, e2, s, c, v, u, fa, fb, fz, w, ends):
    wide, narrow, core, _ = scalars()
    devices, strips = mine.shape[0], mine.shape[0] // 16
    rows, cols, length = 2 * (devices // strips), 8 * strips, 256
    edge = jnp.zeros((cols, length), F32)
    for x in (c, v, u):
        x[0], x[rows + 1] = edge, edge

    def load(k, carry):
        for y in range(strips):
            for i in range(2):
                x, z = mine[k * strips + y, i], other[k * strips + y, i]
                s[2 * k + i + 1, 8 * y : 8 * y + 8] = jnp.where(core == 0, x, z)
                c[2 * k + i + 1, 8 * y : 8 * y + 8] = jnp.where(core == 0, z, x)
        return carry

    lax.fori_loop(0, rows // 2, load, 0)
    b, z = iota((cols, length), 0), iota((cols, length), 1)

    def one_face(r, carry):
        fa[r] = 0.5 * (c[r] + c[r + 1])
        return carry

    lax.fori_loop(0, rows + 1, one_face, 0)

    def one(r, carry):
        here = c[r]
        half = 0.5 * here
        yb = jnp.where(b == cols - 1, 0.0, 0.5 * (here + following(here, 0)))
        yz = jnp.where(z == length - 1, 0.0, 0.5 * (here + following(here, 1)))
        e = jnp.where((b == 0) | (b == cols - 1), half, 0.0) + jnp.where((z == 0) | (z == length - 1), half, 0.0)
        diagonal = fa[r - 1] + fa[r] + (yb + preceding(yb, 0)) + (yz + preceding(yz, 1)) + e
        factor = OMEGA / diagonal
        fb[r], fz[r], ends[r], w[r] = yb, yz, e, factor
        u[r] = factor * s[r]
        return carry

    lax.fori_loop(1, rows + 1, one, 0)

    def operator(x, r):
        here = x[r]
        gb = fb[r] * (following(here, 0) - here)
        gz = fz[r] * (following(here, 1) - here)
        out = fa[r] * (here - x[r + 1]) + fa[r - 1] * (here - x[r - 1]) + ends[r] * here
        return out + (preceding(gb, 0) - gb) + (preceding(gz, 1) - gz)

    def smooth(source, target, lo, hi):
        def body(r, carry):
            target[r] = source[r] + w[r] * (s[r] - operator(source, r))
            return carry

        lax.fori_loop(lo, hi, body, 0)

    smooth(u, v, 1, rows + 1)
    def coarse(i, carry):
        r = 2 * i + 1
        x, y = s[r] - operator(v, r), s[r + 1] - operator(v, r + 1)
        u[i + 1, 0 : cols // 2, 0:128] = 0.5 * coarse_sum(x, y)
        u[i + 1, 0 : cols // 2, 128:256] = 0.125 * coarse_sum(c[r], c[r + 1])
        return carry

    lax.fori_loop(0, rows // 2, coarse, 0)
    s3 = u[1 : rows // 2 + 1, 0 : cols // 2, 0:128]
    c3 = u[1 : rows // 2 + 1, 0 : cols // 2, 128:256]
    e3 = descend(s3, c3, cols // 2, 128)
    u[1 : rows // 2 + 1, 0 : cols // 2, 0:128] = e3

    def refine(i, carry):
        e = refine_row(u[i + 1, 0 : cols // 2, 0:128], cols // 8, 2)
        v[2 * i + 1] = v[2 * i + 1] + e
        v[2 * i + 2] = v[2 * i + 2] + e
        return carry

    lax.fori_loop(0, rows // 2, refine, 0)
    smooth(v, u, 1, rows + 1)
    smooth(u, v, 1, rows + 1)
    for i in range(6):
        r = lax.rem(2 * wide - 2 + i + rows, rows)
        moved = pltpu.roll(v[r + 1], lax.rem(cols + 2 - 4 * narrow, cols), 0)
        e2[i] = moved[0:8]


def moved(x, wide_step, narrow_step):
    w, y, k = [lax.axis_size(name) for name in AX]
    n = y * k
    pairs = [
        (i * n + j, ((i + wide_step) % w) * n + (j + narrow_step) % n)
        for i in range(w)
        for j in range(n)
    ]
    return lax.ppermute(x, AX, pairs)


def other_core(x):
    w, y, k = [lax.axis_size(name) for name in AX]
    return lax.ppermute(x, AX, [(i, i ^ 1) for i in range(w * y * k)])


def per_device(p, d, m):
    up = jnp.concatenate([p[5:8], m[5:8], d[6:8]], axis=0)
    down = jnp.concatenate([p[0:3], m[0:3], d[0:2]], axis=0)
    left, right = moved(up, 1, 0), moved(down, -1, 0)
    to_left, to_right = call(pack_zero, [(14, 8, 1024)] * 2, [], p, d, m, left, right)
    nleft, nright = moved(to_right, 0, 1), moved(to_left, 0, -1)
    big = (14, 24, 1024)
    f0, me, de, s1, c1, up, down, w0 = call(
        lambda *refs: level_zero(*refs[:14], *refs[15:], refs[14]),
        [(8, 16, 1024), big, big, (4, 8, 512), (4, 8, 512), (7, 8, 512), (7, 8, 512), big],
        [big] * 5,
        p, d, m, left, right, nleft, nright,
        flops=30_000_000,
    )
    left1, right1 = moved(up, 1, 0), moved(down, -1, 0)
    to_left, to_right = call(pack_one, [(12, 8, 512)] * 2, [], s1, c1, left1, right1)
    nleft1, nright1 = moved(to_right, 0, 1), moved(to_left, 0, -1)
    mid = (12, 16, 512)
    se, ce, f1, send, keep, up, down = call(
        level_one,
        [mid, mid, (4, 8, 512), (2, 8, 256), (2, 8, 256), (8, 8, 1024), (8, 8, 1024)],
        [mid] * 6,
        s1, c1, left1, right1, nleft1, nright1, f0,
        flops=10_000_000,
    )
    hleft, hright = moved(up, 1, 0), moved(down, -1, 0)
    pair = keep + other_core(send)
    chips = lax.axis_size("wide") * lax.axis_size("ny")
    mine = lax.all_to_all(jnp.broadcast_to(pair[None], (chips,) + pair.shape), ("wide", "ny"), 0, 0, tiled=True)
    other = other_core(mine)
    to_left, to_right = call(pack_up, [(14, 8, 1024)] * 2, [], f0, f1, hleft, hright)
    nhleft, nhright = moved(to_right, 0, 1), moved(to_left, 0, -1)
    whole = (34, 32, 256)
    (e2,) = call(coarse_levels, [(6, 8, 256)], [whole] * 9, mine, other, flops=60_000_000)
    return call(
        level_up,
        [(8, 16, 1024)] * 2,
        [big] * 5 + [mid] * 6,
        me, de, w0, f0, hleft, hright, nhleft, nhright, se, ce, f1, e2,
        flops=30_000_000,
    )


def solution(mesh):
    wide, narrow = mesh.axis_names
    devices = mesh.devices.reshape(mesh.shape[wide], mesh.shape[narrow] // 2, 2)
    spec = P("wide", ("ny", "core"), None)
    return jax.shard_map(
        lambda p, d, m: tuple(per_device(p, d, m)),
        mesh=Mesh(devices, AX),
        in_specs=(spec,) * 3,
        out_specs=(spec,) * 2,
        check_vma=False,
    )
```

profile of v0, /device:TPU:1, one launch (start us, length us, event | category | flops | bytes accessed | tf_op | source)
XLA Modules:
  0.0 151.0 jit_solution(15003872309220268867)
XLA Ops:
  0.6 1.0 fusion.2
  1.6 1.3 fusion
  3.0 6.8 %collective-permute-start.1 = (f32[8,16,1024]{2,1,0:T(8,128)S(1)}, f32[8,16,1024]{2,1,0:T(8,128)S(1)}, u32[]{:S(2)}, u32[]{:S(2)}) collective-permute-start(f32[8,16,1024]{2,1,0:T(8,128)S(1)} %pad_maximum_fusion.1), channel_id=1, source_target_pairs={{0,120},{1,121},{2,122},{3,123},{4,124},{5,125},{6,126},{7,127},{8... | collective-permute-start | bytes 1572872 | tf_op jit(solution)/shard_map/ppermute | solution.py:633
  10.0 10.5 %collective-permute-done.1.right.refs_4_ = f32[8,16,1024]{2,1,0:T(8,128)S(1)} collective-permute-done((f32[8,16,1024]{2,1,0:T(8,128)S(1)}, f32[8,16,1024]{2,1,0:T(8,128)S(1)}, u32[]{:S(2)}, u32[]{:S(2)}) %collective-permute-start.1) | collective-permute-done | bytes 524320 | tf_op jit(solution)/shard_map/ppermute | solution.py:633
  20.4 5.3 %collective-permute-done.left.refs_3_ = f32[8,16,1024]{2,1,0:T(8,128)S(1)} collective-permute-done((f32[8,16,1024]{2,1,0:T(8,128)S(1)}, f32[8,16,1024]{2,1,0:T(8,128)S(1)}, u32[]{:S(2)}, u32[]{:S(2)}) %collective-permute-start) | collective-permute-done | bytes 524320 | tf_op jit(solution)/shard_map/ppermute | solution.py:633
  25.9 3.1 %collective-permute-start.2 = (f32[14,8,1024]{2,1,0:T(8,128)S(1)}, f32[14,8,1024]{2,1,0:T(8,128)S(1)}, u32[]{:S(2)}, u32[]{:S(2)}) collective-permute-start(f32[14,8,1024]{2,1,0:T(8,128)S(1)} %get-tuple-element.23), channel_id=1, source_target_pairs={{0,1},{1,2},{2,3},{3,4},{4,5},{5,6},{6,7},{7,0},{8,9},{9,10},{10,1... | collective-permute-start | bytes 1376264 | tf_op jit(solution)/shard_map/ppermute | solution.py:633
  29.0 5.4 %collective-permute-done.2.refs_5_ = f32[14,8,1024]{2,1,0:T(8,128)S(1)} collective-permute-done((f32[14,8,1024]{2,1,0:T(8,128)S(1)}, f32[14,8,1024]{2,1,0:T(8,128)S(1)}, u32[]{:S(2)}, u32[]{:S(2)}) %collective-permute-start.2) | collective-permute-done | bytes 458784 | tf_op jit(solution)/shard_map/ppermute | solution.py:633
  34.4 2.5 %collective-permute-done.3.refs_6_ = f32[14,8,1024]{2,1,0:T(8,128)S(1)} collective-permute-done((f32[14,8,1024]{2,1,0:T(8,128)S(1)}, f32[14,8,1024]{2,1,0:T(8,128)S(1)}, u32[]{:S(2)}, u32[]{:S(2)}) %collective-permute-start.3) | collective-permute-done | bytes 458784 | tf_op jit(solution)/shard_map/ppermute | solution.py:633
  36.9 9.3 %shard_map.51 = (f32[8,16,1024]{2,1,0:T(8,128)S(1)}, f32[14,24,1024]{2,1,0:T(8,128)S(1)}, f32[14,24,1024]{2,1,0:T(8,128)}, f32[4,8,512]{2,1,0:T(8,128)S(1)}, f32...) custom-call(f32[8,16,1024]{2,1,0:T(8,128)S(1)} %copy-done, ...), custom_call_target="tpu_custom_call" | custom-call | flops 30000000 | bytes 3538944 | tf_op jit(solution)/shard_map/pallas_call | solution.py:121
  46.2 4.8 %collective-permute-start.5 = (f32[7,8,512]{2,1,0:T(8,128)S(1)}, f32[7,8,512]{2,1,0:T(8,128)S(1)}, u32[]{:S(2)}, u32[]{:S(2)}) collective-permute-start(f32[7,8,512]{2,1,0:T(8,128)S(1)} %get-tuple-element.32), channel_id=1, source_target_pairs={{0,120},{1,121},{2,122},{3,123},{4,124},{5,125},{6,126},{7,127},{8... | collective-permute-start | bytes 344072 | tf_op jit(solution)/shard_map/ppermute | solution.py:633
  51.0 3.3 %collective-permute-done.4.left = f32[7,8,512]{2,1,0:T(8,128)S(1)} collective-permute-done((f32[7,8,512]{2,1,0:T(8,128)S(1)}, f32[7,8,512]{2,1,0:T(8,128)S(1)}, u32[]{:S(2)}, u32[]{:S(2)}) %collective-permute-start.4) | collective-permute-done | bytes 114720 | tf_op jit(solution)/shard_map/ppermute | solution.py:633
  54.3 0.6 collective-permute-start.6
  55.2 2.4 %collective-permute-done.6.nleft = f32[12,8,512]{2,1,0:T(8,128)S(1)} collective-permute-done((f32[12,8,512]{2,1,0:T(8,128)S(1)}, f32[12,8,512]{2,1,0:T(8,128)S(1)}, u32[]{:S(2)}, u32[]{:S(2)}) %collective-permute-start.6) | collective-permute-done | bytes 196640 | tf_op jit(solution)/shard_map/ppermute | solution.py:633
  57.5 2.8 %collective-permute-done.7.nright = f32[12,8,512]{2,1,0:T(8,128)S(1)} collective-permute-done((f32[12,8,512]{2,1,0:T(8,128)S(1)}, f32[12,8,512]{2,1,0:T(8,128)S(1)}, u32[]{:S(2)}, u32[]{:S(2)}) %collective-permute-start.7) | collective-permute-done | bytes 196640 | tf_op jit(solution)/shard_map/ppermute | solution.py:633
  60.3 2.8 %shard_map.53 = (f32[12,16,512]{2,1,0:T(8,128)S(1)}, f32[12,16,512]{2,1,0:T(8,128)S(1)}, f32[4,8,512]{2,1,0:T(8,128)S(1)}, f32[2,8,256]{2,1,0:T(8,128)S(1)}, f32...) custom-call(f32[4,8,512]{2,1,0:T(8,128)S(1)} %get-tuple-element.29.s, ...), custom_call_target="tpu_custom_call" | custom-call | flops 10000000 | bytes 1277952 | tf_op jit(solution)/shard_map/pallas_call | solution.py:121
  63.1 1.2 collective-permute-start.12
  64.3 0.8 collective-permute-done.12
  65.2 26.7 %all_to_all.5.mine = f32[64,2,8,256]{3,2,1,0:T(8,128)S(1)} all-to-all(f32[64,2,8,256]{3,2,1,0:T(8,128)S(1)} %broadcast_in_dim.2), channel_id=1, replica_groups=mesh['wide'=16,'ny'=4,'core'=2] {'wide','ny'}, dimensions={0} | all-to-all | bytes 2097152 | tf_op jit(solution)/shard_map/all_to_all | solution.py:669
  92.0 2.2 %collective-permute-start.13 = (f32[64,2,8,256]{3,2,1,0:T(8,128)S(1)}, f32[64,2,8,256]{3,2,1,0:T(8,128)S(1)}, u32[]{:S(2)}, u32[]{:S(2)}) collective-permute-start(f32[64,2,8,256]{3,2,1,0:T(8,128)S(1)} %all_to_all.5.mine), channel_id=1, source_target_pairs={{0,1},{1,0},{2,3},{3,2},{4,5},{5,4},{6,7},{7,6},{8,9},{9,8},{10,11... | collective-permute-start | bytes 3145736 | tf_op jit(solution)/shard_map/ppermute | solution.py:638
  94.4 4.7 %collective-permute-start.9 = (f32[8,8,1024]{2,1,0:T(8,128)S(1)}, f32[8,8,1024]{2,1,0:T(8,128)S(1)}, u32[]{:S(2)}, u32[]{:S(2)}) collective-permute-start(f32[8,8,1024]{2,1,0:T(8,128)S(1)} %get-tuple-element.36), channel_id=1, source_target_pairs={{0,120},{1,121},{2,122},{3,123},{4,124},{5,125},{6,126},{7,127},{8... | collective-permute-start | bytes 786440 | tf_op jit(solution)/shard_map/ppermute | solution.py:633
  99.0 6.5 %collective-permute-done.8.left = f32[8,8,1024]{2,1,0:T(8,128)S(1)} collective-permute-done((f32[8,8,1024]{2,1,0:T(8,128)S(1)}, f32[8,8,1024]{2,1,0:T(8,128)S(1)}, u32[]{:S(2)}, u32[]{:S(2)}) %collective-permute-start.8) | collective-permute-done | bytes 262176 | tf_op jit(solution)/shard_map/ppermute | solution.py:633
  105.6 1.1 collective-permute-start.10
  106.7 30.4 %shard_map.55.e2 = f32[6,8,256]{2,1,0:T(8,128)S(1)} custom-call(f32[64,2,8,256]{3,2,1,0:T(8,128)S(1)} %all_to_all.5.mine, f32[64,2,8,256]{3,2,1,0:T(8,128)S(1)} %collective-permute-done.13.other), custom_call_target="tpu_custom_call" | custom-call | flops 60000000 | bytes 2097152 | tf_op jit(solution)/shard_map/pallas_call | solution.py:121
  137.1 13.8 %shard_map.56 = (f32[8,16,1024]{2,1,0:T(8,128)}, f32[8,16,1024]{2,1,0:T(8,128)}) custom-call(f32[14,24,1024]{2,1,0:T(8,128)S(1)} %get-tuple-element.25.me, f32[14,24,1024]{2,1,0:T(8,128)S(1)} %copy-done.3, f32[14,24,1024]{2,1,0:T(8,128)} %get-tuple-element.27.w, f32[8,16,1024]{2,1,0:T(8,128)S(1)} %get-tuple-element.28.f0, ...), custom_call_target="tpu_custom_call" | custom-call | flops 30000000 | bytes 6995968 | tf_op jit(solution)/shard_map/pallas_call | solution.py:121
  (26 shorter events, 1.0 us)
Async XLA Ops:
  2.9 22.9 %copy-start = (f32[8,16,1024]{2,1,0:T(8,128)S(1)}, f32[8,16,1024]{2,1,0:T(8,128)}, u32[]{:S(2)}) copy-start(f32[8,16,1024]{2,1,0:T(8,128)} %refs_0_.1) | copy-start | bytes 1572868
  2.9 22.8 %copy-start.1 = (f32[8,16,1024]{2,1,0:T(8,128)S(1)}, f32[8,16,1024]{2,1,0:T(8,128)}, u32[]{:S(2)}) copy-start(f32[8,16,1024]{2,1,0:T(8,128)} %refs_2_.1) | copy-start | bytes 1572868
  2.9 22.8 %copy-start.2 = (f32[8,16,1024]{2,1,0:T(8,128)S(1)}, f32[8,16,1024]{2,1,0:T(8,128)}, u32[]{:S(2)}) copy-start(f32[8,16,1024]{2,1,0:T(8,128)} %refs_1_.1) | copy-start | bytes 1572868
  3.0 17.4 %collective-permute-start.1 = (f32[8,16,1024]{2,1,0:T(8,128)S(1)}, f32[8,16,1024]{2,1,0:T(8,128)S(1)}, u32[]{:S(2)}, u32[]{:S(2)}) collective-permute-start(f32[8,16,1024]{2,1,0:T(8,128)S(1)} %pad_maximum_fusion.1), channel_id=1, source_target_pairs={{0,120},{1,121},{2,122},{3,123},{4,124},{5,125},{6,126},{7,127},{8... | collective-permute-start | bytes 1572872 | tf_op jit(solution)/shard_map/ppermute | solution.py:633
  9.9 15.9 %collective-permute-start = (f32[8,16,1024]{2,1,0:T(8,128)S(1)}, f32[8,16,1024]{2,1,0:T(8,128)S(1)}, u32[]{:S(2)}, u32[]{:S(2)}) collective-permute-start(f32[8,16,1024]{2,1,0:T(8,128)S(1)} %pad_maximum_fusion), channel_id=1, source_target_pairs={{0,8},{1,9},{2,10},{3,11},{4,12},{5,13},{6,14},{7,15},{8,16},{9,17... | collective-permute-start | bytes 1572872 | tf_op jit(solution)/shard_map/ppermute | solution.py:633
  25.9 8.5 %collective-permute-start.2 = (f32[14,8,1024]{2,1,0:T(8,128)S(1)}, f32[14,8,1024]{2,1,0:T(8,128)S(1)}, u32[]{:S(2)}, u32[]{:S(2)}) collective-permute-start(f32[14,8,1024]{2,1,0:T(8,128)S(1)} %get-tuple-element.23), channel_id=1, source_target_pairs={{0,1},{1,2},{2,3},{3,4},{4,5},{5,6},{6,7},{7,0},{8,9},{9,10},{10,1... | collective-permute-start | bytes 1376264 | tf_op jit(solution)/shard_map/ppermute | solution.py:633
  29.0 7.9 %collective-permute-start.3 = (f32[14,8,1024]{2,1,0:T(8,128)S(1)}, f32[14,8,1024]{2,1,0:T(8,128)S(1)}, u32[]{:S(2)}, u32[]{:S(2)}) collective-permute-start(f32[14,8,1024]{2,1,0:T(8,128)S(1)} %get-tuple-element.24), channel_id=1, source_target_pairs={{0,7},{1,0},{2,1},{3,2},{4,3},{5,4},{6,5},{7,6},{8,15},{9,8},{10,9... | collective-permute-start | bytes 1376264 | tf_op jit(solution)/shard_map/ppermute | solution.py:633
  46.2 8.1 %collective-permute-start.4 = (f32[7,8,512]{2,1,0:T(8,128)S(1)}, f32[7,8,512]{2,1,0:T(8,128)S(1)}, u32[]{:S(2)}, u32[]{:S(2)}) collective-permute-start(f32[7,8,512]{2,1,0:T(8,128)S(1)} %get-tuple-element.31), channel_id=1, source_target_pairs={{0,8},{1,9},{2,10},{3,11},{4,12},{5,13},{6,14},{7,15},{8,16},{9,17... | collective-permute-start | bytes 344072 | tf_op jit(solution)/shard_map/ppermute | solution.py:633
  46.2 8.1 %collective-permute-start.5 = (f32[7,8,512]{2,1,0:T(8,128)S(1)}, f32[7,8,512]{2,1,0:T(8,128)S(1)}, u32[]{:S(2)}, u32[]{:S(2)}) collective-permute-start(f32[7,8,512]{2,1,0:T(8,128)S(1)} %get-tuple-element.32), channel_id=1, source_target_pairs={{0,120},{1,121},{2,122},{3,123},{4,124},{5,125},{6,126},{7,127},{8... | collective-permute-start | bytes 344072 | tf_op jit(solution)/shard_map/ppermute | solution.py:633
  54.3 3.2 %collective-permute-start.6 = (f32[12,8,512]{2,1,0:T(8,128)S(1)}, f32[12,8,512]{2,1,0:T(8,128)S(1)}, u32[]{:S(2)}, u32[]{:S(2)}) collective-permute-start(f32[12,8,512]{2,1,0:T(8,128)S(1)} %get-tuple-element.33), channel_id=1, source_target_pairs={{0,1},{1,2},{2,3},{3,4},{4,5},{5,6},{6,7},{7,0},{8,9},{9,10},{10,1... | collective-permute-start | bytes 589832 | tf_op jit(solution)/shard_map/ppermute | solution.py:633
  54.9 5.4 %collective-permute-start.7 = (f32[12,8,512]{2,1,0:T(8,128)S(1)}, f32[12,8,512]{2,1,0:T(8,128)S(1)}, u32[]{:S(2)}, u32[]{:S(2)}) collective-permute-start(f32[12,8,512]{2,1,0:T(8,128)S(1)} %get-tuple-element.34), channel_id=1, source_target_pairs={{0,7},{1,0},{2,1},{3,2},{4,3},{5,4},{6,5},{7,6},{8,15},{9,8},{10,9... | collective-permute-start | bytes 589832 | tf_op jit(solution)/shard_map/ppermute | solution.py:633
  63.1 2.0 %collective-permute-start.12 = (f32[2,8,256]{2,1,0:T(8,128)S(1)}, f32[2,8,256]{2,1,0:T(8,128)S(1)}, u32[]{:S(2)}, u32[]{:S(2)}) collective-permute-start(f32[2,8,256]{2,1,0:T(8,128)S(1)} %get-tuple-element.43), channel_id=1, source_target_pairs={{0,1},{1,0},{2,3},{3,2},{4,5},{5,4},{6,7},{7,6},{8,9},{9,8},{10,11... | collective-permute-start | bytes 49160 | tf_op jit(solution)/shard_map/ppermute | solution.py:638
  92.0 14.7 %collective-permute-start.13 = (f32[64,2,8,256]{3,2,1,0:T(8,128)S(1)}, f32[64,2,8,256]{3,2,1,0:T(8,128)S(1)}, u32[]{:S(2)}, u32[]{:S(2)}) collective-permute-start(f32[64,2,8,256]{3,2,1,0:T(8,128)S(1)} %all_to_all.5.mine), channel_id=1, source_target_pairs={{0,1},{1,0},{2,3},{3,2},{4,5},{5,4},{6,7},{7,6},{8,9},{9,8},{10,11... | collective-permute-start | bytes 3145736 | tf_op jit(solution)/shard_map/ppermute | solution.py:638
  94.2 11.3 %collective-permute-start.8 = (f32[8,8,1024]{2,1,0:T(8,128)S(1)}, f32[8,8,1024]{2,1,0:T(8,128)S(1)}, u32[]{:S(2)}, u32[]{:S(2)}) collective-permute-start(f32[8,8,1024]{2,1,0:T(8,128)S(1)} %get-tuple-element.35), channel_id=1, source_target_pairs={{0,8},{1,9},{2,10},{3,11},{4,12},{5,13},{6,14},{7,15},{8,16},{9,17... | collective-permute-start | bytes 786440 | tf_op jit(solution)/shard_map/ppermute | solution.py:633
  94.4 11.1 %collective-permute-start.9 = (f32[8,8,1024]{2,1,0:T(8,128)S(1)}, f32[8,8,1024]{2,1,0:T(8,128)S(1)}, u32[]{:S(2)}, u32[]{:S(2)}) collective-permute-start(f32[8,8,1024]{2,1,0:T(8,128)S(1)} %get-tuple-element.36), channel_id=1, source_target_pairs={{0,120},{1,121},{2,122},{3,123},{4,124},{5,125},{6,126},{7,127},{8... | collective-permute-start | bytes 786440 | tf_op jit(solution)/shard_map/ppermute | solution.py:633
  105.5 31.6 %copy-start.3 = (f32[14,24,1024]{2,1,0:T(8,128)S(1)}, f32[14,24,1024]{2,1,0:T(8,128)}, u32[]{:S(2)}) copy-start(f32[14,24,1024]{2,1,0:T(8,128)} %get-tuple-element.26.de) | copy-start | bytes 4128772
  105.6 31.5 %collective-permute-start.10 = (f32[14,8,1024]{2,1,0:T(8,128)S(1)}, f32[14,8,1024]{2,1,0:T(8,128)S(1)}, u32[]{:S(2)}, u32[]{:S(2)}) collective-permute-start(f32[14,8,1024]{2,1,0:T(8,128)S(1)} %get-tuple-element.38), channel_id=1, source_target_pairs={{0,1},{1,2},{2,3},{3,4},{4,5},{5,6},{6,7},{7,0},{8,9},{9,10},{10,1... | collective-permute-start | bytes 1376264 | tf_op jit(solution)/shard_map/ppermute | solution.py:633
  106.7 30.4 %collective-permute-start.11 = (f32[14,8,1024]{2,1,0:T(8,128)S(1)}, f32[14,8,1024]{2,1,0:T(8,128)S(1)}, u32[]{:S(2)}, u32[]{:S(2)}) collective-permute-start(f32[14,8,1024]{2,1,0:T(8,128)S(1)} %get-tuple-element.39), channel_id=1, source_target_pairs={{0,7},{1,0},{2,1},{3,2},{4,3},{5,4},{6,5},{7,6},{8,15},{9,8},{10,9... | collective-permute-start | bytes 1376264 | tf_op jit(solution)/shard_map/ppermute | solution.py:633
where the time goes:
time: 152 us; the launch traced here: 151 us
  Pallas kernels  56.5 us (37%)
  waiting for transfers between devices  39.4 us (26%)
  blocking collectives  26.7 us (18%)
  starting transfers between devices  25 us (16%)
  local copies, waits for them, and re-layouts  2.42 us (2%)
    pallas_call x7, Pallas kernels, call(): pl.pallas_call(kernel, out_shape=[jax.ShapeDtypeStruct(s, F32) for s in o...  56.5 us
    ppermute x12, waiting for transfers between devices, moved(): return lax.ppermute(x, AX, pairs)  38.6 us
    all_to_all x1, blocking collectives, per_device(): lax.all_to_all(jnp.broadcast_to(pair[None], (chips,) + pair.shape), ('wid...  26.7 us
    ppermute x12, starting transfers between devices, moved(): return lax.ppermute(x, AX, pairs)  21.5 us
    ppermute x2, starting transfers between devices, other_core(): return lax.ppermute(x, AX, [(i, i ^ 1) for i in range(w * y * k)])  3.45 us
  transfers between devices with their start and end apart: 14, of which 9 were waited for; matrix products, arithmetic and copies ran while one was open for 0% of the time, Pallas kernels for 20%

commit v1 on v0

--- a/solution.py
+++ b/solution.py
@@ -1,3 +1,5 @@
+import math
+
 import jax
 import jax.numpy as jnp
 from jax import lax
@@ -8,7 +10,7 @@
 OMEGA = 0.8
 AX = ("wide", "ny", "core")
 F32 = jnp.float32
-LIMIT = 48 * 1024 * 1024
+SPARE = 4 * 1024 * 1024
 
 
 def iota(shape, dim):
@@ -23,28 +25,73 @@
     return pltpu.roll(x, 1, dim)
 
 
-def add_z_ends(out, c, v):
-    length = out.shape[1]
-    lane = iota((out.shape[0], 128), 1)
-    if length == 128:
-        return out + jnp.where((lane == 0) | (lane == 127), 0.5 * c * v, 0.0)
-    low = out[:, :128] + jnp.where(lane == 0, 0.5 * c[:, :128] * v[:, :128], 0.0)
-    high = out[:, -128:] + jnp.where(lane == 127, 0.5 * c[:, -128:] * v[:, -128:], 0.0)
-    parts = [low, high] if length == 256 else [low, out[:, 128:-128], high]
-    return jnp.concatenate(parts, axis=1)
-
-
-def row_operator(v, below, above, c, fa_below, fa_above, fb, fz):
-    gb = fb * (following(v, 0) - v)
-    gz = fz * (following(v, 1) - v)
-    out = fa_above * (v - above) + fa_below * (v - below)
-    out = out + (preceding(gb, 0) - gb) + (preceding(gz, 1) - gz)
-    return add_z_ends(out, c, v)
-
-
-def row_diagonal(c, fa_below, fa_above, fb, fz):
-    out = fa_above + fa_below + (fb + preceding(fb, 0)) + (fz + preceding(fz, 1))
-    return add_z_ends(out, c, jnp.ones_like(c))
+def lanes(x, r, k):
+    return x[r, :, 128 * k : 128 * k + 128]
+
+
+def row_operator(v, r, c, fa, fb, fz):
+    count = v.shape[2] // 128
+    lane = iota((v.shape[1], 128), 1)
+    here = lanes(v, r, 0)
+    turned = pltpu.roll(here, 127, 1)
+    out = []
+    for k in range(count):
+        if k + 1 < count:
+            later = lanes(v, r, k + 1)
+            later_turned = pltpu.roll(later, 127, 1)
+        else:
+            later, later_turned = None, 0.0
+        gz = lanes(fz, r, k) * (jnp.where(lane == 127, later_turned, turned) - here)
+        gz_turned = pltpu.roll(gz, 1, 1)
+        if k == 0:
+            gz_before = 0.5 * lanes(c, r, 0) * here
+        gb = lanes(fb, r, k) * (following(here, 0) - here)
+        a = lanes(fa, r, k) * (here - lanes(v, r + 1, k)) + lanes(fa, r - 1, k) * (here - lanes(v, r - 1, k))
+        a = a + (preceding(gb, 0) - gb) + (jnp.where(lane == 0, gz_before, gz_turned) - gz)
+        out.append(a)
+        here, turned, gz_before = later, later_turned, gz_turned
+    return out
+
+
+def row_faces(r, c, fa, fb, fz, w):
+    count = c.shape[2] // 128
+    cols = c.shape[1]
+    lane = iota((cols, 128), 1)
+    here = lanes(c, r, 0)
+    turned = pltpu.roll(here, 127, 1)
+    for k in range(count):
+        if k + 1 < count:
+            later = lanes(c, r, k + 1)
+            later_turned = pltpu.roll(later, 127, 1)
+        else:
+            later, later_turned = None, 0.0
+        at = slice(128 * k, 128 * k + 128)
+        z = 0.5 * (here + jnp.where(lane == 127, later_turned, turned))
+        z_turned = pltpu.roll(z, 1, 1)
+        if k == 0:
+            z_before = 0.5 * here
+        y = 0.5 * (here + following(here, 0))
+        diagonal = 0.5 * (here + lanes(c, r - 1, k)) + 0.5 * (here + lanes(c, r + 1, k))
+        diagonal = diagonal + (y + preceding(y, 0)) + (z + jnp.where(lane == 0, z_before, z_turned))
+        fa[r, :, at] = 0.5 * (here + lanes(c, r + 1, k))
+        fb[r, :, at], fz[r, :, at] = y, z
+        w[r, :, at] = jnp.where(here > 0.0, OMEGA / diagonal, 0.0)
+        here, turned, z_before = later, later_turned, z_turned
+
+
+def over_rows(lo, hi, step, body):
+    whole = (hi - lo) // step
+
+    def some(i, carry):
+        for j in range(step):
+            body(lo + i * step + j)
+        return carry
+
+    if whole > 1:
+        lax.fori_loop(0, whole, some, 0)
+        lo = lo + whole * step
+    for r in range(lo, hi):
+        body(r)
 
 
 def half_compress(low, high, dim):
@@ -57,33 +104,44 @@
     return jnp.where(at < length // 2, first, jnp.take_along_axis(high, index, axis=dim))
 
 
-def pair_sums(x, dim, tile):
-    x = x + following(x, dim)
-    count = x.shape[dim] // tile
-
-    def piece(r, l, t):
-        if dim == 0:
-            return x[8 * t : 8 * t + 8, 128 * l : 128 * l + 128]
-        return x[8 * r : 8 * r + 8, 128 * t : 128 * t + 128]
-
-    rows, lanes = x.shape[0] // 8, x.shape[1] // 128
-    half = max(count // 2, 1)
-    if dim == 0:
-        out = [
-            [half_compress(piece(0, l, 2 * t), piece(0, l, 2 * t + 1) if count > 1 else None, 0) for l in range(lanes)]
-            for t in range(half)
-        ]
-    else:
-        out = [
-            [half_compress(piece(r, 0, 2 * t), piece(r, 0, 2 * t + 1) if count > 1 else None, 1) for t in range(half)]
-            for r in range(rows)
-        ]
-    joined = [line[0] if len(line) == 1 else jnp.concatenate(line, axis=1) for line in out]
-    return joined[0] if len(joined) == 1 else jnp.concatenate(joined, axis=0)
-
-
-def coarse_sum(first, second):
-    return pair_sums(pair_sums(first + second, 0, 8), 1, 128)
+def half_columns(x):
+    x = x + following(x, 0)
+    tiles = x.shape[0] // 8
+    part = lambda t: x[8 * t : 8 * t + 8]
+    if tiles == 1:
+        return half_compress(x, None, 0)
+    x = [half_compress(part(2 * t), part(2 * t + 1), 0) for t in range(tiles // 2)]
+    return x[0] if len(x) == 1 else jnp.concatenate(x, axis=0)
+
+
+def coarse_sum(first, second, split=False):
+    halves = [half_columns(x + y) for x, y in zip(first, second)]
+    halves = [x + following(x, 1) for x in halves]
+    if split:
+        lane = iota((8, 128), 1)
+        out = []
+        for odd in range(2):
+            index = (4 * lane + 2 * odd) % 128
+            picked = jnp.take_along_axis(halves[0], index, axis=1)
+            for k in range(1, 4):
+                picked = jnp.where(lane >= 32 * k, jnp.take_along_axis(halves[k], index, axis=1), picked)
+            out.append(picked)
+        return out
+    if len(halves) == 1:
+        return [by_tile(halves[0], None)]
+    return [by_tile(halves[k], halves[k + 1]) for k in range(0, len(halves), 2)]
+
+
+def by_tile(low, high):
+    tiles = [
+        half_compress(low[8 * t : 8 * t + 8], None if high is None else high[8 * t : 8 * t + 8], 1)
+        for t in range(low.shape[0] // 8)
+    ]
+    return tiles[0] if len(tiles) == 1 else jnp.concatenate(tiles, axis=0)
+
+
+def blocks_of(x):
+    return [x[:, 128 * k : 128 * k + 128] for k in range(x.shape[1] // 128)]
 
 
 def repeat_lanes(x, block):
@@ -102,6 +160,17 @@
 def widen(x, blocks):
     pieces = [repeat_lanes(x, k) for k in range(blocks)]
     return pieces[0] if len(pieces) == 1 else jnp.concatenate(pieces, axis=1)
+
+
+def widen_split(x):
+    lane = iota((8, 128), 1)
+    pieces = []
+    for k in range(4):
+        index = 32 * k + lane // 4
+        even = jnp.take_along_axis(x[:, :128], index, axis=1)
+        odd = jnp.take_along_axis(x[:, 128:], index, axis=1)
+        pieces.append(jnp.where(lane // 2 % 2 == 0, even, odd))
+    return jnp.concatenate(pieces, axis=1)
 
 
 def scalars():
@@ -118,14 +187,15 @@
 def call(kernel, outs, scratch, *args, flops=1_000_000):
     vmem = pl.BlockSpec(memory_space=pltpu.VMEM)
     size = 4 * sum(a.size for a in args)
+    held = size + 4 * sum(math.prod(s) for s in outs + scratch)
     return pl.pallas_call(
         kernel,
         out_shape=[jax.ShapeDtypeStruct(s, F32) for s in outs],
         in_specs=[vmem] * len(args),
         out_specs=[vmem] * len(outs),
         scratch_shapes=[pltpu.VMEM(s, F32) for s in scratch],
-        compiler_params=pltpu.CompilerParams(vmem_limit_bytes=LIMIT),
-        cost_estimate=pl.CostEstimate(flops=flops, bytes_accessed=size, transcendentals=0),
+        compiler_params=pltpu.CompilerParams(vmem_limit_bytes=held + SPARE),
+        cost_estimate=pl.CostEstimate(flops=flops, bytes_accessed=0 if flops == 1000 else size, transcendentals=0),
     )(*args)
 
 
@@ -152,44 +222,30 @@
                 out[r] = jnp.where(at >= 5, vp, jnp.where(at >= 2, vm, vd))
 
 
-def faces(c, rows, fa, fb, fz, w, cols, mask_b):
-    lo, hi = rows
-    length = c.shape[2]
-    last = iota((cols, length), 1) == length - 1
-
-    def one_face(r, carry):
-        fa[r] = 0.5 * (c[r] + c[r + 1])
-        return carry
-
-    lax.fori_loop(lo - 1, hi, one_face, 0)
-
-    def one(r, carry):
-        here = c[r]
-        b = 0.5 * (here + following(here, 0))
-        z = jnp.where(last, 0.0, 0.5 * (here + following(here, 1)))
-        fb[r], fz[r] = b, z
-        diagonal = row_diagonal(here, fa[r - 1], fa[r], b, z)
-        w[r] = jnp.where(here > 0.0, OMEGA / diagonal, 0.0)
-        return carry
-
-    lax.fori_loop(lo, hi, one, 0)
-
-
-def sweep(source, target, s, c, fa, fb, fz, w, rows):
-    def one(r, carry):
-        v = source[r]
-        a = row_operator(v, source[r - 1], source[r + 1], c[r], fa[r - 1], fa[r], fb[r], fz[r])
-        target[r] = v + w[r] * (s[r] - a)
-        return carry
-
-    lax.fori_loop(rows[0], rows[1], one, 0)
-
-
-def residual_row(v, s, c, fa, fb, fz, r):
-    return s[r] - row_operator(v[r], v[r - 1], v[r + 1], c[r], fa[r - 1], fa[r], fb[r], fz[r])
-
-
-def level_zero(p, d, m, left, right, nleft, nright, field, me, de, s1, c1, up, down, v, u, fa, fb, fz, w):
+def faces(c, rows, fa, fb, fz, w, step):
+    for k in range(c.shape[2] // 128):
+        at = slice(128 * k, 128 * k + 128)
+        fa[rows[0] - 1, :, at] = 0.5 * (c[rows[0] - 1, :, at] + c[rows[0], :, at])
+    over_rows(rows[0], rows[1], step, lambda r: row_faces(r, c, fa, fb, fz, w))
+
+
+def sweep(source, target, s, c, fa, fb, fz, w, rows, step):
+    def one(r):
+        for k, a in enumerate(row_operator(source, r, c, fa, fb, fz)):
+            at = slice(128 * k, 128 * k + 128)
+            target[r, :, at] = source[r, :, at] + w[r, :, at] * (s[r, :, at] - a)
+
+    over_rows(rows[0], rows[1], step, one)
+
+
+def residual_row(v, s, c, fa, fb, fz, r, cols):
+    return [
+        (lanes(s, r, k) - a)[0:cols]
+        for k, a in enumerate(row_operator(v, r, c, fa, fb, fz))
+    ]
+
+
+def level_zero(p, d, m, left, right, nleft, nright, field, s1, c1, up, down, me, de, w, fa, fb, fz, v, u):
     _, _, _, (low, high, nlow, nhigh) = scalars()
     at = iota((8, 1024), 0)
     for r in range(14):
@@ -208,18 +264,20 @@
         me[r, 16:24] = jnp.where(at < 3, x3, jnp.where(at >= 5, y3, 0.0))
         x6, y6 = pltpu.roll(x, 2, 0), pltpu.roll(y, 6, 0)
         de[r, 16:24] = jnp.where(at < 2, x6, jnp.where(at >= 6, y6, 0.0))
-    faces(me, (1, 13), fa, fb, fz, w, 24, None)
+    faces(me, (1, 13), fa, fb, fz, w, 2)
     u[0], u[13] = v[0], v[13]
-    sweep(v, u, de, me, fa, fb, fz, w, (1, 13))
-    sweep(u, v, de, me, fa, fb, fz, w, (2, 12))
+    sweep(v, u, de, me, fa, fb, fz, w, (1, 13), 2)
+    sweep(u, v, de, me, fa, fb, fz, w, (2, 12), 2)
     field[...] = v[3:11, 0:16]
 
     def coarse(i, carry):
         r = 2 * i + 3
-        x = residual_row(v, de, me, fa, fb, fz, r)[0:16]
-        y = residual_row(v, de, me, fa, fb, fz, r + 1)[0:16]
-        s1[i] = 0.5 * coarse_sum(x, y)
-        c1[i] = 0.125 * coarse_sum(me[r, 0:16], me[r + 1, 0:16])
+        x = residual_row(v, de, me, fa, fb, fz, r, 16)
+        y = residual_row(v, de, me, fa, fb, fz, r + 1, 16)
+        mx, my = blocks_of(me[r, 0:16]), blocks_of(me[r + 1, 0:16])
+        for k, (a, b) in enumerate(zip(coarse_sum(x, y), coarse_sum(mx, my))):
+            s1[i, :, 128 * k : 128 * k + 128] = 0.5 * a
+            c1[i, :, 128 * k : 128 * k + 128] = 0.125 * b
         return carry
 
     lax.fori_loop(0, 4, coarse, 0)
@@ -260,24 +318,22 @@
         x, y = nright[r] * nhigh, nleft[r] * nlow
         ce[r, 8:16] = jnp.where(at < 4, x, y)
         se[r, 8:16] = jnp.where(at < 4, pltpu.roll(x, 4, 0), pltpu.roll(y, 4, 0))
-    faces(ce, (2, 10), fa, fb, fz, w, 16, None)
-
-    def first(r, carry):
+    faces(ce, (2, 10), fa, fb, fz, w, 4)
+
+    for r in range(2, 10):
         u[r] = w[r] * se[r]
-        return carry
-
-    lax.fori_loop(2, 10, first, 0)
-    sweep(u, v, se, ce, fa, fb, fz, w, (3, 9))
+    sweep(u, v, se, ce, fa, fb, fz, w, (3, 9), 3)
     field[...] = v[4:8, 0:8]
     rows = iota((8, 256), 0)
     index = iota((8, 256), 0) % 4
     mine = rows // 4 == core
     for i in range(2):
         r = 2 * i + 4
-        x = residual_row(v, se, ce, fa, fb, fz, r)[0:8]
-        y = residual_row(v, se, ce, fa, fb, fz, r + 1)[0:8]
-        s2 = 0.5 * coarse_sum(x, y)
-        c2 = 0.125 * coarse_sum(ce[r, 0:8], ce[r + 1, 0:8])
+        x = residual_row(v, se, ce, fa, fb, fz, r, 8)
+        y = residual_row(v, se, ce, fa, fb, fz, r + 1, 8)
+        mx, my = blocks_of(ce[r, 0:8]), blocks_of(ce[r + 1, 0:8])
+        s2 = 0.5 * jnp.concatenate(coarse_sum(x, y, True), axis=1)
+        c2 = 0.125 * jnp.concatenate(coarse_sum(mx, my, True), axis=1)
         s2 = jnp.where(mine, take_rows(s2, index[:, :128]), 0.0)
         c2 = jnp.where(mine, take_rows(c2, index[:, :128]), 0.0)
         send[i] = jnp.where(core == 0, c2, s2)
@@ -318,7 +374,7 @@
             out[r] = x
 
 
-def level_up(me, de, w, f0, left, right, nleft, nright, se, ce, f1, e2, out, res, v, u, fa, fb, fz, v1, u1, fa1, fb1, fz1, w1):
+def level_up(me, de, w, fa, fb, fz, f0, left, right, nleft, nright, se, ce, f1, e2, out, res, v, u, v1, u1, fa1, fb1, fz1, w1):
     _, _, _, (low, high, nlow, nhigh) = scalars()
     at = iota((8, 512), 0)
     half = iota((8, 128), 0)
@@ -333,13 +389,13 @@
         y = nleft[r // 2][:, 512 * (r % 2) : 512 * (r % 2) + 512] * nlow
         g = jnp.where(at < 4, pltpu.roll(x, 4, 0), pltpu.roll(y, 4, 0))
         e = e2[r // 2]
-        own = widen(take_rows(e, 2 + half // 2), 4)
-        beside = widen(take_rows(e, jnp.where(half < 4, 6 + half // 2, (half - 4) // 2)), 4)
+        own = widen_split(take_rows(e, 2 + half // 2))
+        beside = widen_split(take_rows(e, jnp.where(half < 4, 6 + half // 2, (half - 4) // 2)))
         v1[r, 0:8] = f + jnp.where(ce[r, 0:8] > 0.0, own, 0.0)
         v1[r, 8:16] = g + jnp.where(ce[r, 8:16] > 0.0, beside, 0.0)
-    faces(ce, (1, 11), fa1, fb1, fz1, w1, 16, None)
-    sweep(v1, u1, se, ce, fa1, fb1, fz1, w1, (1, 11))
-    sweep(u1, v1, se, ce, fa1, fb1, fz1, w1, (2, 10))
+    faces(ce, (1, 11), fa1, fb1, fz1, w1, 5)
+    sweep(v1, u1, se, ce, fa1, fb1, fz1, w1, (1, 11), 5)
+    sweep(u1, v1, se, ce, fa1, fb1, fz1, w1, (2, 10), 4)
     zero = iota((8, 1024), 0)
     for r in range(14):
         if r < 3:
@@ -361,29 +417,15 @@
             tile = slice(8 * t, 8 * t + 8)
             v[r, tile] = f[t] + jnp.where(me[r, tile] > 0.0, fine, 0.0)
 
-    def one_face(r, carry):
-        fa[r] = 0.5 * (me[r] + me[r + 1])
-        return carry
-
-    lax.fori_loop(0, 13, one_face, 0)
-    last = iota((24, 1024), 1) == 1023
-
-    def one(r, carry):
-        here = me[r]
-        fb[r] = 0.5 * (here + following(here, 0))
-        fz[r] = jnp.where(last, 0.0, 0.5 * (here + following(here, 1)))
-        return carry
-
-    lax.fori_loop(1, 13, one, 0)
-    sweep(v, u, de, me, fa, fb, fz, w, (1, 13))
-    sweep(u, v, de, me, fa, fb, fz, w, (2, 12))
+    sweep(v, u, de, me, fa, fb, fz, w, (1, 13), 2)
+    sweep(u, v, de, me, fa, fb, fz, w, (2, 12), 2)
     out[...] = v[3:11, 0:16]
 
-    def final(r, carry):
-        res[r] = residual_row(v, de, me, fa, fb, fz, r + 3)[0:16]
-        return carry
-
-    lax.fori_loop(0, 8, final, 0)
+    def final(r):
+        for k, x in enumerate(residual_row(v, de, me, fa, fb, fz, r, 16)):
+            res[r - 3, :, 128 * k : 128 * k + 128] = x
+
+    over_rows(3, 11, 2, final)
 
 
 def shifted(x, step):
@@ -417,20 +459,21 @@
 
 
 def coarsen_whole(x):
-    return jnp.stack([coarse_sum(x[a], x[a + 1]) for a in range(0, x.shape[0], 2)])
-
-
-def refine_row(x, cols_tiles, blocks):
+    return jnp.stack([coarse_sum([x[a]], [x[a + 1]])[0] for a in range(0, x.shape[0], 2)])
+
+
+def refine_row(x, cols_tiles, lanes_too):
     half = iota((8, 128), 0)
     tiles = []
     for t in range(cols_tiles):
         source = x[8 * (t // 2) : 8 * (t // 2) + 8]
-        tiles.append(widen(take_rows(source, half // 2 + 4 * (t % 2)), blocks))
+        tile = take_rows(source, half // 2 + 4 * (t % 2))
+        tiles.append(widen(tile, 1) if lanes_too else tile)
     return tiles[0] if cols_tiles == 1 else jnp.concatenate(tiles, axis=0)
 
 
 def refine_whole(x, cols_tiles):
-    rows = [refine_row(x[a], cols_tiles, 1) for a in range(x.shape[0])]
+    rows = [refine_row(x[a], cols_tiles, True) for a in range(x.shape[0])]
     return jnp.stack([rows[a // 2] for a in range(2 * x.shape[0])])
 
 
@@ -540,86 +583,107 @@
     return level.sweep(v, s)
 
 
-def coarse_levels(mine, other, e2, s, c, v, u, fa, fb, fz, w, ends):
-    wide, narrow, core, _ = scalars()
-    devices, strips = mine.shape[0], mine.shape[0] // 16
-    rows, cols, length = 2 * (devices // strips), 8 * strips, 256
-    edge = jnp.zeros((cols, length), F32)
+def split_before(last, first_lane):
+    lane = iota(last.shape, 1)
+    return jnp.where(lane == 0, first_lane, pltpu.roll(last, 1, 1))
+
+
+def split_after(first):
+    lane = iota(first.shape, 1)
+    return jnp.where(lane == 127, 0.0, pltpu.roll(first, 127, 1))
+
+
+def split_operator(v, r, c, fa, fb, fz, ends):
+    here = [lanes(v, r, k) for k in range(2)]
+    after = [here[1], split_after(here[0])]
+    gz = [lanes(fz, r, k) * (after[k] - here[k]) for k in range(2)]
+    before = [split_before(gz[1], 0.5 * lanes(c, r, 0) * here[0]), gz[0]]
+    out = []
+    for k in range(2):
+        gb = lanes(fb, r, k) * (following(here[k], 0) - here[k])
+        a = lanes(fa, r, k) * (here[k] - lanes(v, r + 1, k)) + lanes(fa, r - 1, k) * (here[k] - lanes(v, r - 1, k))
+        a = a + lanes(ends, r, k) * here[k]
+        out.append(a + (preceding(gb, 0) - gb) + (before[k] - gz[k]))
+    return out
+
+
+def split_sweep(source, target, s, c, fa, fb, fz, ends, w, r):
+    for k, a in enumerate(split_operator(source, r, c, fa, fb, fz, ends)):
+        at = slice(128 * k, 128 * k + 128)
+        target[r, :, at] = source[r, :, at] + w[r, :, at] * (s[r, :, at] - a)
+
+
+def level_two(mine, other, s, c, v, fa, fb, fz, ends, w, s3, c3, u):
+    _, _, core, _ = scalars()
+    strips = mine.shape[0] // 16
+    rows, cols = 32, 8 * strips
+    edge = jnp.zeros((cols, 256), F32)
     for x in (c, v, u):
         x[0], x[rows + 1] = edge, edge
 
-    def load(k, carry):
+    def load(k):
         for y in range(strips):
             for i in range(2):
                 x, z = mine[k * strips + y, i], other[k * strips + y, i]
                 s[2 * k + i + 1, 8 * y : 8 * y + 8] = jnp.where(core == 0, x, z)
                 c[2 * k + i + 1, 8 * y : 8 * y + 8] = jnp.where(core == 0, z, x)
-        return carry
-
-    lax.fori_loop(0, rows // 2, load, 0)
-    b, z = iota((cols, length), 0), iota((cols, length), 1)
-
-    def one_face(r, carry):
-        fa[r] = 0.5 * (c[r] + c[r + 1])
-        return carry
-
-    lax.fori_loop(0, rows + 1, one_face, 0)
-
-    def one(r, carry):
-        here = c[r]
-        half = 0.5 * here
-        yb = jnp.where(b == cols - 1, 0.0, 0.5 * (here + following(here, 0)))
-        yz = jnp.where(z == length - 1, 0.0, 0.5 * (here + following(here, 1)))
-        e = jnp.where((b == 0) | (b == cols - 1), half, 0.0) + jnp.where((z == 0) | (z == length - 1), half, 0.0)
-        diagonal = fa[r - 1] + fa[r] + (yb + preceding(yb, 0)) + (yz + preceding(yz, 1)) + e
-        factor = OMEGA / diagonal
-        fb[r], fz[r], ends[r], w[r] = yb, yz, e, factor
-        u[r] = factor * s[r]
-        return carry
-
-    lax.fori_loop(1, rows + 1, one, 0)
-
-    def operator(x, r):
-        here = x[r]
-        gb = fb[r] * (following(here, 0) - here)
-        gz = fz[r] * (following(here, 1) - here)
-        out = fa[r] * (here - x[r + 1]) + fa[r - 1] * (here - x[r - 1]) + ends[r] * here
-        return out + (preceding(gb, 0) - gb) + (preceding(gz, 1) - gz)
-
-    def smooth(source, target, lo, hi):
-        def body(r, carry):
-            target[r] = source[r] + w[r] * (s[r] - operator(source, r))
-            return carry
-
-        lax.fori_loop(lo, hi, body, 0)
-
-    smooth(u, v, 1, rows + 1)
-    def coarse(i, carry):
-        r = 2 * i + 1
-        x, y = s[r] - operator(v, r), s[r + 1] - operator(v, r + 1)
-        u[i + 1, 0 : cols // 2, 0:128] = 0.5 * coarse_sum(x, y)
-        u[i + 1, 0 : cols // 2, 128:256] = 0.125 * coarse_sum(c[r], c[r + 1])
-        return carry
-
-    lax.fori_loop(0, rows // 2, coarse, 0)
-    s3 = u[1 : rows // 2 + 1, 0 : cols // 2, 0:128]
-    c3 = u[1 : rows // 2 + 1, 0 : cols // 2, 128:256]
-    e3 = descend(s3, c3, cols // 2, 128)
-    u[1 : rows // 2 + 1, 0 : cols // 2, 0:128] = e3
-
-    def refine(i, carry):
-        e = refine_row(u[i + 1, 0 : cols // 2, 0:128], cols // 8, 2)
-        v[2 * i + 1] = v[2 * i + 1] + e
-        v[2 * i + 2] = v[2 * i + 2] + e
-        return carry
-
-    lax.fori_loop(0, rows // 2, refine, 0)
-    smooth(v, u, 1, rows + 1)
-    smooth(u, v, 1, rows + 1)
+
+    over_rows(0, rows // 2, 2, load)
+    fa[0] = 0.5 * c[1]
+    b = iota((cols, 128), 0)
+
+    def one(r):
+        here = [lanes(c, r, k) for k in range(2)]
+        z = [0.5 * (here[0] + here[1]), 0.5 * (here[1] + split_after(here[0]))]
+        before = [split_before(z[1], 0.5 * here[0]), z[0]]
+        for k in range(2):
+            at = slice(128 * k, 128 * k + 128)
+            x, h = here[k], 0.5 * here[k]
+            y = jnp.where(b == cols - 1, 0.0, 0.5 * (x + following(x, 0)))
+            e = jnp.where((b == 0) | (b == cols - 1), h, 0.0)
+            above = h + 0.5 * lanes(c, r + 1, k)
+            diagonal = above + (h + 0.5 * lanes(c, r - 1, k)) + (y + preceding(y, 0)) + (z[k] + before[k]) + e
+            factor = OMEGA / diagonal
+            fa[r, :, at], fb[r, :, at], fz[r, :, at] = above, y, z[k]
+            ends[r, :, at], w[r, :, at] = e, factor
+            u[r, :, at] = factor * s[r, :, at]
+
+    over_rows(1, rows + 1, 4, one)
+    over_rows(1, rows + 1, 4, lambda r: split_sweep(u, v, s, c, fa, fb, fz, ends, w, r))
+
+    def coarse(i):
+        total = None
+        for r in (2 * i + 1, 2 * i + 2):
+            for k, a in enumerate(split_operator(v, r, c, fa, fb, fz, ends)):
+                x = lanes(s, r, k) - a
+                total = x if total is None else total + x
+        s3[i] = 0.5 * half_columns(total)
+        total = (lanes(c, 2 * i + 1, 0) + lanes(c, 2 * i + 1, 1)) + (lanes(c, 2 * i + 2, 0) + lanes(c, 2 * i + 2, 1))
+        c3[i] = 0.125 * half_columns(total)
+
+    over_rows(0, rows // 2, 2, coarse)
+
+
+def coarse_levels(s3, c3, s, c, v, fa, fb, fz, ends, w, e2, e3, u, t):
+    wide, narrow, _, _ = scalars()
+    rows, cols = s.shape[0] - 2, s.shape[1]
+    e3[...] = descend(s3[...], c3[...], cols // 2, 128)
+    row = lambda step: jnp.clip(2 * wide + step, 0, rows - 1) + 1
+    u[0], u[rows + 1], t[0], t[rows + 1] = v[0], v[0], v[0], v[0]
+    for i in range(-2, 3):
+        k = jnp.clip(wide + i, 0, rows // 2 - 1)
+        e = refine_row(e3[k], cols // 8, False)
+        for r in (2 * k + 1, 2 * k + 2):
+            for half in range(2):
+                at = slice(128 * half, 128 * half + 128)
+                u[r, :, at] = v[r, :, at] + e
+    for i in range(-3, 5):
+        split_sweep(u, t, s, c, fa, fb, fz, ends, w, row(i))
+    for i in range(-2, 4):
+        split_sweep(t, u, s, c, fa, fb, fz, ends, w, row(i))
     for i in range(6):
-        r = lax.rem(2 * wide - 2 + i + rows, rows)
-        moved = pltpu.roll(v[r + 1], lax.rem(cols + 2 - 4 * narrow, cols), 0)
-        e2[i] = moved[0:8]
+        turned = pltpu.roll(u[row(i - 2)], lax.rem(cols + 2 - 4 * narrow, cols), 0)
+        e2[i] = turned[0:8]
 
 
 def moved(x, wide_step, narrow_step):
@@ -638,6 +702,11 @@
     return lax.ppermute(x, AX, [(i, i ^ 1) for i in range(w * y * k)])
 
 
+def gathered(x):
+    chips = lax.axis_size("wide") * lax.axis_size("ny")
+    return lax.all_to_all(jnp.broadcast_to(x[None], (chips,) + x.shape), ("wide", "ny"), 0, 0, tiled=True)
+
+
 def per_device(p, d, m):
     up = jnp.concatenate([p[5:8], m[5:8], d[6:8]], axis=0)
     down = jnp.concatenate([p[0:3], m[0:3], d[0:2]], axis=0)
@@ -645,10 +714,10 @@
     to_left, to_right = call(pack_zero, [(14, 8, 1024)] * 2, [], p, d, m, left, right)
     nleft, nright = moved(to_right, 0, 1), moved(to_left, 0, -1)
     big = (14, 24, 1024)
-    f0, me, de, s1, c1, up, down, w0 = call(
-        lambda *refs: level_zero(*refs[:14], *refs[15:], refs[14]),
-        [(8, 16, 1024), big, big, (4, 8, 512), (4, 8, 512), (7, 8, 512), (7, 8, 512), big],
-        [big] * 5,
+    f0, s1, c1, up, down, *zero = call(
+        level_zero,
+        [(8, 16, 1024), (4, 8, 512), (4, 8, 512), (7, 8, 512), (7, 8, 512)] + [big] * 6,
+        [big] * 2,
         p, d, m, left, right, nleft, nright,
         flops=30_000_000,
     )
@@ -665,18 +734,19 @@
     )
     hleft, hright = moved(up, 1, 0), moved(down, -1, 0)
     pair = keep + other_core(send)
-    chips = lax.axis_size("wide") * lax.axis_size("ny")
-    mine = lax.all_to_all(jnp.broadcast_to(pair[None], (chips,) + pair.shape), ("wide", "ny"), 0, 0, tiled=True)
+    mine = gathered(pair)
     other = other_core(mine)
+    whole, small = (34, 32, 256), (16, 16, 128)
+    *two, s3, c3 = call(level_two, [whole] * 8 + [small] * 2, [whole], mine, other, flops=1000)
+    s3, hleft, hright = lax.optimization_barrier((s3, hleft, hright))
     to_left, to_right = call(pack_up, [(14, 8, 1024)] * 2, [], f0, f1, hleft, hright)
     nhleft, nhright = moved(to_right, 0, 1), moved(to_left, 0, -1)
-    whole = (34, 32, 256)
-    (e2,) = call(coarse_levels, [(6, 8, 256)], [whole] * 9, mine, other, flops=60_000_000)
+    (e2,) = call(coarse_levels, [(6, 8, 256)], [small] + [whole] * 2, s3, c3, *two, flops=1000)
     return call(
         level_up,
         [(8, 16, 1024)] * 2,
-        [big] * 5 + [mid] * 6,
-        me, de, w0, f0, hleft, hright, nhleft, nhright, se, ce, f1, e2,
+        [big] * 2 + [mid] * 6,
+        *zero, f0, hleft, hright, nhleft, nhright, se, ce, f1, e2,
         flops=30_000_000,
     )
 

time: 152 us -> 112 us (0.74)
  Pallas kernels: 56.5 us -> 21.1 us
  waiting for transfers between devices: 39.4 us -> 35.4 us
    pallas_call x7 -> x8, Pallas kernels: 56.5 us -> 21.1 us  [call(): pl.pallas_call(kernel, out_shape=[jax.ShapeDtypeStruct(s, F32) for s in o...]
    ppermute x12, waiting for transfers between devices: 38.6 us -> 34.6 us  [moved(): return lax.ppermute(x, AX, pairs)]
  transfers between devices with their start and end apart: 14 -> 14, of which waited for: 9 -> 10; matrix products, arithmetic and copies ran while one was open for 0% -> 0% of each run, Pallas kernels for 20% -> 7%
where the time goes in v1:
time: 112 us; the launch traced here: 111 us
  waiting for transfers between devices  35.4 us (32%)
  blocking collectives  26.8 us (24%)
  starting transfers between devices  24.7 us (22%)
  Pallas kernels  21.1 us (19%)
  local copies, waits for them, and re-layouts  2.41 us (2%)
    ppermute x12, waiting for transfers between devices, moved(): return lax.ppermute(x, AX, pairs)  34.6 us
    all_to_all x1, blocking collectives, gathered(): lax.all_to_all(jnp.broadcast_to(x[None], (chips,) + x.shape), ('wide', 'n...  26.8 us
    pallas_call x8, Pallas kernels, call(): pl.pallas_call(kernel, out_shape=[jax.ShapeDtypeStruct(s, F32) for s in o...  21.1 us
    ppermute x12, starting transfers between devices, moved(): return lax.ppermute(x, AX, pairs)  21 us
    ppermute x2, starting transfers between devices, other_core(): return lax.ppermute(x, AX, [(i, i ^ 1) for i in range(w * y * k)])  3.71 us
    slice x2, local copies, waits for them, and re-layouts, per_device(): down = jnp.concatenate([p[0:3], m[0:3], d[0:2]], axis=0)  2.28 us
  transfers between devices with their start and end apart: 14, of which 10 were waited for; matrix products, arithmetic and copies ran while one was open for 0% of the time, Pallas kernels for 7%

profile of v1, /device:TPU:1, one launch (start us, length us, event | category | flops | bytes accessed | tf_op | source)
XLA Modules:
  0.0 111.3 jit_solution(9220340145075467580)
XLA Ops:
  1.6 1.3 %fusion = (f32[3,16,1024]{2,1,0:T(8,128)S(1)}, f32[3,16,1024]{2,1,0:T(8,128)S(1)}, f32[3,16,1024]{2,1,0:T(8,128)S(1)}, f32[3,16,1024]{2,1,0:T(8,128)S(1)}) fusion(f32[8,16,1024]{2,1,0:T(8,128)} %p.3, f32[8,16,1024]{2,1,0:T(8,128)} %m.3), kind=kLoop, calls=%fused_computation.2 | loop fusion | bytes 1572864 | tf_op jit(solution)/shard_map/slice | solution.py:712
  3.0 2.5 %collective-permute-start = (f32[8,16,1024]{2,1,0:T(8,128)S(1)}, f32[8,16,1024]{2,1,0:T(8,128)S(1)}, u32[]{:S(2)}, u32[]{:S(2)}) collective-permute-start(f32[8,16,1024]{2,1,0:T(8,128)S(1)} %pad_maximum_fusion), channel_id=1, source_target_pairs={{0,8},{1,9},{2,10},{3,11},{4,12},{5,13},{6,14},{7,15},{8,16},{9,17... | collective-permute-start | bytes 1572872 | tf_op jit(solution)/shard_map/ppermute | solution.py:697
  5.6 4.4 %collective-permute-start.1 = (f32[8,16,1024]{2,1,0:T(8,128)S(1)}, f32[8,16,1024]{2,1,0:T(8,128)S(1)}, u32[]{:S(2)}, u32[]{:S(2)}) collective-permute-start(f32[8,16,1024]{2,1,0:T(8,128)S(1)} %pad_maximum_fusion.1), channel_id=1, source_target_pairs={{0,120},{1,121},{2,122},{3,123},{4,124},{5,125},{6,126},{7,127},{8... | collective-permute-start | bytes 1572872 | tf_op jit(solution)/shard_map/ppermute | solution.py:697
  10.0 11.5 %collective-permute-done.left = f32[8,16,1024]{2,1,0:T(8,128)S(1)} collective-permute-done((f32[8,16,1024]{2,1,0:T(8,128)S(1)}, f32[8,16,1024]{2,1,0:T(8,128)S(1)}, u32[]{:S(2)}, u32[]{:S(2)}) %collective-permute-start) | collective-permute-done | bytes 524320 | tf_op jit(solution)/shard_map/ppermute | solution.py:697
  21.7 2.4 %collective-permute-start.2 = (f32[14,8,1024]{2,1,0:T(8,128)S(1)}, f32[14,8,1024]{2,1,0:T(8,128)S(1)}, u32[]{:S(2)}, u32[]{:S(2)}) collective-permute-start(f32[14,8,1024]{2,1,0:T(8,128)S(1)} %get-tuple-element.39), channel_id=1, source_target_pairs={{0,1},{1,2},{2,3},{3,4},{4,5},{5,6},{6,7},{7,0},{8,9},{9,10},{10,1... | collective-permute-start | bytes 1376264 | tf_op jit(solution)/shard_map/ppermute | solution.py:697
  24.1 5.4 %collective-permute-done.2.nleft = f32[14,8,1024]{2,1,0:T(8,128)S(1)} collective-permute-done((f32[14,8,1024]{2,1,0:T(8,128)S(1)}, f32[14,8,1024]{2,1,0:T(8,128)S(1)}, u32[]{:S(2)}, u32[]{:S(2)}) %collective-permute-start.2) | collective-permute-done | bytes 458784 | tf_op jit(solution)/shard_map/ppermute | solution.py:697
  29.5 2.5 %collective-permute-done.3.nright = f32[14,8,1024]{2,1,0:T(8,128)S(1)} collective-permute-done((f32[14,8,1024]{2,1,0:T(8,128)S(1)}, f32[14,8,1024]{2,1,0:T(8,128)S(1)}, u32[]{:S(2)}, u32[]{:S(2)}) %collective-permute-start.3) | collective-permute-done | bytes 458784 | tf_op jit(solution)/shard_map/ppermute | solution.py:697
  32.0 5.6 %shard_map.51 = (f32[8,16,1024]{2,1,0:T(8,128)S(1)}, f32[4,8,512]{2,1,0:T(8,128)S(1)}, f32[4,8,512]{2,1,0:T(8,128)S(1)}, f32[7,8,512]{2,1,0:T(8,128)S(1)}, f32[7...) custom-call(f32[8,16,1024]{2,1,0:T(8,128)S(1)} %copy-done, ...), custom_call_target="tpu_custom_call" | custom-call | flops 30000000 | bytes 3538944 | tf_op jit(solution)/shard_map/pallas_call | solution.py:191
  37.7 5.0 %collective-permute-start.5 = (f32[7,8,512]{2,1,0:T(8,128)S(1)}, f32[7,8,512]{2,1,0:T(8,128)S(1)}, u32[]{:S(2)}, u32[]{:S(2)}) collective-permute-start(f32[7,8,512]{2,1,0:T(8,128)S(1)} %get-tuple-element.51), channel_id=1, source_target_pairs={{0,120},{1,121},{2,122},{3,123},{4,124},{5,125},{6,126},{7,127},{8... | collective-permute-start | bytes 344072 | tf_op jit(solution)/shard_map/ppermute | solution.py:697
  42.6 3.3 %collective-permute-done.4.left = f32[7,8,512]{2,1,0:T(8,128)S(1)} collective-permute-done((f32[7,8,512]{2,1,0:T(8,128)S(1)}, f32[7,8,512]{2,1,0:T(8,128)S(1)}, u32[]{:S(2)}, u32[]{:S(2)}) %collective-permute-start.4) | collective-permute-done | bytes 114720 | tf_op jit(solution)/shard_map/ppermute | solution.py:697
  46.7 2.1 %collective-permute-done.6.nleft = f32[12,8,512]{2,1,0:T(8,128)S(1)} collective-permute-done((f32[12,8,512]{2,1,0:T(8,128)S(1)}, f32[12,8,512]{2,1,0:T(8,128)S(1)}, u32[]{:S(2)}, u32[]{:S(2)}) %collective-permute-start.6) | collective-permute-done | bytes 196640 | tf_op jit(solution)/shard_map/ppermute | solution.py:697
  48.9 2.8 %collective-permute-done.7.nright = f32[12,8,512]{2,1,0:T(8,128)S(1)} collective-permute-done((f32[12,8,512]{2,1,0:T(8,128)S(1)}, f32[12,8,512]{2,1,0:T(8,128)S(1)}, u32[]{:S(2)}, u32[]{:S(2)}) %collective-permute-start.7) | collective-permute-done | bytes 196640 | tf_op jit(solution)/shard_map/ppermute | solution.py:697
  51.6 1.1 %shard_map.53 = (f32[12,16,512]{2,1,0:T(8,128)S(1)}, f32[12,16,512]{2,1,0:T(8,128)S(1)}, f32[4,8,512]{2,1,0:T(8,128)S(1)}, f32[2,8,256]{2,1,0:T(8,128)S(1)}, f32...) custom-call(f32[4,8,512]{2,1,0:T(8,128)S(1)} %get-tuple-element.48.s, ...), custom_call_target="tpu_custom_call" | custom-call | flops 10000000 | bytes 1277952 | tf_op jit(solution)/shard_map/pallas_call | solution.py:191
  52.8 1.5 %collective-permute-start.8 = (f32[2,8,256]{2,1,0:T(8,128)S(1)}, f32[2,8,256]{2,1,0:T(8,128)S(1)}, u32[]{:S(2)}, u32[]{:S(2)}) collective-permute-start(f32[2,8,256]{2,1,0:T(8,128)S(1)} %get-tuple-element.55), channel_id=1, source_target_pairs={{0,1},{1,0},{2,3},{3,2},{4,5},{5,4},{6,7},{7,6},{8,9},{9,8},{10,11... | collective-permute-start | bytes 49160 | tf_op jit(solution)/shard_map/ppermute | solution.py:702
  55.2 26.8 %all_to_all.5.mine = f32[64,2,8,256]{3,2,1,0:T(8,128)S(1)} all-to-all(f32[64,2,8,256]{3,2,1,0:T(8,128)S(1)} %broadcast_in_dim.2), channel_id=1, replica_groups=mesh['wide'=16,'ny'=4,'core'=2] {'wide','ny'}, dimensions={0} | all-to-all | bytes 2097152 | tf_op jit(solution)/shard_map/all_to_all | solution.py:707
  82.0 2.2 %collective-permute-start.9 = (f32[64,2,8,256]{3,2,1,0:T(8,128)S(1)}, f32[64,2,8,256]{3,2,1,0:T(8,128)S(1)}, u32[]{:S(2)}, u32[]{:S(2)}) collective-permute-start(f32[64,2,8,256]{3,2,1,0:T(8,128)S(1)} %all_to_all.5.mine), channel_id=1, source_target_pairs={{0,1},{1,0},{2,3},{3,2},{4,5},{5,4},{6,7},{7,6},{8,9},{9,8},{10,11... | collective-permute-start | bytes 3145736 | tf_op jit(solution)/shard_map/ppermute | solution.py:702
  84.4 4.7 %collective-permute-start.11 = (f32[8,8,1024]{2,1,0:T(8,128)S(1)}, f32[8,8,1024]{2,1,0:T(8,128)S(1)}, u32[]{:S(2)}, u32[]{:S(2)}) collective-permute-start(f32[8,8,1024]{2,1,0:T(8,128)S(1)} %get-tuple-element.58), channel_id=1, source_target_pairs={{0,120},{1,121},{2,122},{3,123},{4,124},{5,125},{6,126},{7,127},{8... | collective-permute-start | bytes 786440 | tf_op jit(solution)/shard_map/ppermute | solution.py:697
  89.1 4.2 %shard_map.54 = (f32[34,32,256]{2,1,0:T(8,128)S(1)}, f32[34,32,256]{2,1,0:T(8,128)S(1)}, f32[34,32,256]{2,1,0:T(8,128)S(1)}, f32[34,32,256]{2,1,0:T(8,128)S(1)},...) custom-call(f32[64,2,8,256]{3,2,1,0:T(8,128)S(1)} %all_to_all.5.mine, ...), custom_call_target="tpu_custom_call" | custom-call | flops 1000 | tf_op jit(solution)/shard_map/pallas_call | solution.py:191
  93.3 2.2 %collective-permute-done.10.left = f32[8,8,1024]{2,1,0:T(8,128)S(1)} collective-permute-done((f32[8,8,1024]{2,1,0:T(8,128)S(1)}, f32[8,8,1024]{2,1,0:T(8,128)S(1)}, u32[]{:S(2)}, u32[]{:S(2)}) %collective-permute-start.10) | collective-permute-done | bytes 262176 | tf_op jit(solution)/shard_map/ppermute | solution.py:697
  95.6 1.1 %collective-permute-start.12 = (f32[14,8,1024]{2,1,0:T(8,128)S(1)}, f32[14,8,1024]{2,1,0:T(8,128)S(1)}, u32[]{:S(2)}, u32[]{:S(2)}) collective-permute-start(f32[14,8,1024]{2,1,0:T(8,128)S(1)} %get-tuple-element.62), channel_id=1, source_target_pairs={{0,1},{1,2},{2,3},{3,4},{4,5},{5,6},{6,7},{7,0},{8,9},{9,10},{10,1... | collective-permute-start | bytes 1376264 | tf_op jit(solution)/shard_map/ppermute | solution.py:697
  96.7 3.5 %shard_map.56.e2 = f32[6,8,256]{2,1,0:T(8,128)S(1)} custom-call(f32[16,16,128]{2,1,0:T(8,128)S(1)} %get-tuple-element.66.s3, f32[16,16,128]{2,1,0:T(8,128)S(1)} %get-tuple-element.67.c3, f32[34,32,256]{2,1,0:T(8,128)S(1)} %get-tuple-element.68.s, f32[34,32,256]{2,1,0:T(8,128)S(1)} %get-tuple-element.69.c, f32[34,32,256]{2,1,0:T(8,128)S(1)} %get-tuple-element.70.v, ...), custom_call_target="tpu_custom_call" | custom-call | flops 1000 | tf_op jit(solution)/shard_map/pallas_call | solution.py:191
  100.3 1.9 %collective-permute-done.12.nleft = f32[14,8,1024]{2,1,0:T(8,128)S(1)} collective-permute-done((f32[14,8,1024]{2,1,0:T(8,128)S(1)}, f32[14,8,1024]{2,1,0:T(8,128)S(1)}, u32[]{:S(2)}, u32[]{:S(2)}) %collective-permute-start.12) | collective-permute-done | bytes 458784 | tf_op jit(solution)/shard_map/ppermute | solution.py:697
  102.2 2.8 %collective-permute-done.13.nright = f32[14,8,1024]{2,1,0:T(8,128)S(1)} collective-permute-done((f32[14,8,1024]{2,1,0:T(8,128)S(1)}, f32[14,8,1024]{2,1,0:T(8,128)S(1)}, u32[]{:S(2)}, u32[]{:S(2)}) %collective-permute-start.13) | collective-permute-done | bytes 458784 | tf_op jit(solution)/shard_map/ppermute | solution.py:697
  104.9 6.4 %shard_map.57 = (f32[8,16,1024]{2,1,0:T(8,128)}, f32[8,16,1024]{2,1,0:T(8,128)}) custom-call(f32[14,24,1024]{2,1,0:T(8,128)S(1)} %get-tuple-element.41.me, f32[14,24,1024]{2,1,0:T(8,128)S(1)} %get-tuple-element.42.de, f32[14,24,1024]{2,1,0:T(8,128)S(1)} %get-tuple-element.43.w, f32[14,24,1024]{2,1,0:T(8,128)S(1)} %get-tuple-element.44.fa, ...), custom_call_target="tpu_custom_call" | custom-call | flops 30000000 | bytes 11124736 | tf_op jit(solution)/shard_map/pallas_call | solution.py:191
  (25 shorter events, 3.3 us)
Async XLA Ops:
  2.9 18.6 %copy-start = (f32[8,16,1024]{2,1,0:T(8,128)S(1)}, f32[8,16,1024]{2,1,0:T(8,128)}, u32[]{:S(2)}) copy-start(f32[8,16,1024]{2,1,0:T(8,128)} %p.3) | copy-start | bytes 1572868
  2.9 18.6 %copy-start.1 = (f32[8,16,1024]{2,1,0:T(8,128)S(1)}, f32[8,16,1024]{2,1,0:T(8,128)}, u32[]{:S(2)}) copy-start(f32[8,16,1024]{2,1,0:T(8,128)} %m.3) | copy-start | bytes 1572868
  2.9 18.6 %copy-start.2 = (f32[8,16,1024]{2,1,0:T(8,128)S(1)}, f32[8,16,1024]{2,1,0:T(8,128)}, u32[]{:S(2)}) copy-start(f32[8,16,1024]{2,1,0:T(8,128)} %d.3) | copy-start | bytes 1572868
  3.0 18.5 %collective-permute-start = (f32[8,16,1024]{2,1,0:T(8,128)S(1)}, f32[8,16,1024]{2,1,0:T(8,128)S(1)}, u32[]{:S(2)}, u32[]{:S(2)}) collective-permute-start(f32[8,16,1024]{2,1,0:T(8,128)S(1)} %pad_maximum_fusion), channel_id=1, source_target_pairs={{0,8},{1,9},{2,10},{3,11},{4,12},{5,13},{6,14},{7,15},{8,16},{9,17... | collective-permute-start | bytes 1572872 | tf_op jit(solution)/shard_map/ppermute | solution.py:697
  5.6 15.9 %collective-permute-start.1 = (f32[8,16,1024]{2,1,0:T(8,128)S(1)}, f32[8,16,1024]{2,1,0:T(8,128)S(1)}, u32[]{:S(2)}, u32[]{:S(2)}) collective-permute-start(f32[8,16,1024]{2,1,0:T(8,128)S(1)} %pad_maximum_fusion.1), channel_id=1, source_target_pairs={{0,120},{1,121},{2,122},{3,123},{4,124},{5,125},{6,126},{7,127},{8... | collective-permute-start | bytes 1572872 | tf_op jit(solution)/shard_map/ppermute | solution.py:697
  21.7 7.8 %collective-permute-start.2 = (f32[14,8,1024]{2,1,0:T(8,128)S(1)}, f32[14,8,1024]{2,1,0:T(8,128)S(1)}, u32[]{:S(2)}, u32[]{:S(2)}) collective-permute-start(f32[14,8,1024]{2,1,0:T(8,128)S(1)} %get-tuple-element.39), channel_id=1, source_target_pairs={{0,1},{1,2},{2,3},{3,4},{4,5},{5,6},{6,7},{7,0},{8,9},{9,10},{10,1... | collective-permute-start | bytes 1376264 | tf_op jit(solution)/shard_map/ppermute | solution.py:697
  24.1 7.9 %collective-permute-start.3 = (f32[14,8,1024]{2,1,0:T(8,128)S(1)}, f32[14,8,1024]{2,1,0:T(8,128)S(1)}, u32[]{:S(2)}, u32[]{:S(2)}) collective-permute-start(f32[14,8,1024]{2,1,0:T(8,128)S(1)} %get-tuple-element.40), channel_id=1, source_target_pairs={{0,7},{1,0},{2,1},{3,2},{4,3},{5,4},{6,5},{7,6},{8,15},{9,8},{10,9... | collective-permute-start | bytes 1376264 | tf_op jit(solution)/shard_map/ppermute | solution.py:697
  37.6 8.4 %collective-permute-start.4 = (f32[7,8,512]{2,1,0:T(8,128)S(1)}, f32[7,8,512]{2,1,0:T(8,128)S(1)}, u32[]{:S(2)}, u32[]{:S(2)}) collective-permute-start(f32[7,8,512]{2,1,0:T(8,128)S(1)} %get-tuple-element.50), channel_id=1, source_target_pairs={{0,8},{1,9},{2,10},{3,11},{4,12},{5,13},{6,14},{7,15},{8,16},{9,17... | collective-permute-start | bytes 344072 | tf_op jit(solution)/shard_map/ppermute | solution.py:697
  37.7 8.3 %collective-permute-start.5 = (f32[7,8,512]{2,1,0:T(8,128)S(1)}, f32[7,8,512]{2,1,0:T(8,128)S(1)}, u32[]{:S(2)}, u32[]{:S(2)}) collective-permute-start(f32[7,8,512]{2,1,0:T(8,128)S(1)} %get-tuple-element.51), channel_id=1, source_target_pairs={{0,120},{1,121},{2,122},{3,123},{4,124},{5,125},{6,126},{7,127},{8... | collective-permute-start | bytes 344072 | tf_op jit(solution)/shard_map/ppermute | solution.py:697
  46.0 2.8 %collective-permute-start.6 = (f32[12,8,512]{2,1,0:T(8,128)S(1)}, f32[12,8,512]{2,1,0:T(8,128)S(1)}, u32[]{:S(2)}, u32[]{:S(2)}) collective-permute-start(f32[12,8,512]{2,1,0:T(8,128)S(1)} %get-tuple-element.52), channel_id=1, source_target_pairs={{0,1},{1,2},{2,3},{3,4},{4,5},{5,6},{6,7},{7,0},{8,9},{9,10},{10,1... | collective-permute-start | bytes 589832 | tf_op jit(solution)/shard_map/ppermute | solution.py:697
  46.2 5.4 %collective-permute-start.7 = (f32[12,8,512]{2,1,0:T(8,128)S(1)}, f32[12,8,512]{2,1,0:T(8,128)S(1)}, u32[]{:S(2)}, u32[]{:S(2)}) collective-permute-start(f32[12,8,512]{2,1,0:T(8,128)S(1)} %get-tuple-element.53), channel_id=1, source_target_pairs={{0,7},{1,0},{2,1},{3,2},{4,3},{5,4},{6,5},{7,6},{8,15},{9,8},{10,9... | collective-permute-start | bytes 589832 | tf_op jit(solution)/shard_map/ppermute | solution.py:697
  52.8 2.3 %collective-permute-start.8 = (f32[2,8,256]{2,1,0:T(8,128)S(1)}, f32[2,8,256]{2,1,0:T(8,128)S(1)}, u32[]{:S(2)}, u32[]{:S(2)}) collective-permute-start(f32[2,8,256]{2,1,0:T(8,128)S(1)} %get-tuple-element.55), channel_id=1, source_target_pairs={{0,1},{1,0},{2,3},{3,2},{4,5},{5,4},{6,7},{7,6},{8,9},{9,8},{10,11... | collective-permute-start | bytes 49160 | tf_op jit(solution)/shard_map/ppermute | solution.py:702
  82.0 7.0 %collective-permute-start.9 = (f32[64,2,8,256]{3,2,1,0:T(8,128)S(1)}, f32[64,2,8,256]{3,2,1,0:T(8,128)S(1)}, u32[]{:S(2)}, u32[]{:S(2)}) collective-permute-start(f32[64,2,8,256]{3,2,1,0:T(8,128)S(1)} %all_to_all.5.mine), channel_id=1, source_target_pairs={{0,1},{1,0},{2,3},{3,2},{4,5},{5,4},{6,7},{7,6},{8,9},{9,8},{10,11... | collective-permute-start | bytes 3145736 | tf_op jit(solution)/shard_map/ppermute | solution.py:702
  84.3 11.3 %collective-permute-start.10 = (f32[8,8,1024]{2,1,0:T(8,128)S(1)}, f32[8,8,1024]{2,1,0:T(8,128)S(1)}, u32[]{:S(2)}, u32[]{:S(2)}) collective-permute-start(f32[8,8,1024]{2,1,0:T(8,128)S(1)} %get-tuple-element.57), channel_id=1, source_target_pairs={{0,8},{1,9},{2,10},{3,11},{4,12},{5,13},{6,14},{7,15},{8,16},{9,17... | collective-permute-start | bytes 786440 | tf_op jit(solution)/shard_map/ppermute | solution.py:697
  84.4 11.1 %collective-permute-start.11 = (f32[8,8,1024]{2,1,0:T(8,128)S(1)}, f32[8,8,1024]{2,1,0:T(8,128)S(1)}, u32[]{:S(2)}, u32[]{:S(2)}) collective-permute-start(f32[8,8,1024]{2,1,0:T(8,128)S(1)} %get-tuple-element.58), channel_id=1, source_target_pairs={{0,120},{1,121},{2,122},{3,123},{4,124},{5,125},{6,126},{7,127},{8... | collective-permute-start | bytes 786440 | tf_op jit(solution)/shard_map/ppermute | solution.py:697
  95.6 6.5 %collective-permute-start.12 = (f32[14,8,1024]{2,1,0:T(8,128)S(1)}, f32[14,8,1024]{2,1,0:T(8,128)S(1)}, u32[]{:S(2)}, u32[]{:S(2)}) collective-permute-start(f32[14,8,1024]{2,1,0:T(8,128)S(1)} %get-tuple-element.62), channel_id=1, source_target_pairs={{0,1},{1,2},{2,3},{3,4},{4,5},{5,6},{6,7},{7,0},{8,9},{9,10},{10,1... | collective-permute-start | bytes 1376264 | tf_op jit(solution)/shard_map/ppermute | solution.py:697
  96.7 8.2 %collective-permute-start.13 = (f32[14,8,1024]{2,1,0:T(8,128)S(1)}, f32[14,8,1024]{2,1,0:T(8,128)S(1)}, u32[]{:S(2)}, u32[]{:S(2)}) collective-permute-start(f32[14,8,1024]{2,1,0:T(8,128)S(1)} %get-tuple-element.63), channel_id=1, source_target_pairs={{0,7},{1,0},{2,1},{3,2},{4,3},{5,4},{6,5},{7,6},{8,15},{9,8},{10,9... | collective-permute-start | bytes 1376264 | tf_op jit(solution)/shard_map/ppermute | solution.py:697

commit v2 on v1

--- a/solution.py
+++ b/solution.py
@@ -184,7 +184,7 @@
     return wide, narrow, core, inside
 
 
-def call(kernel, outs, scratch, *args, flops=1_000_000):
+def call(kernel, outs, scratch, *args, flops=1_000_000, copies=0):
     vmem = pl.BlockSpec(memory_space=pltpu.VMEM)
     size = 4 * sum(a.size for a in args)
     held = size + 4 * sum(math.prod(s) for s in outs + scratch)
@@ -192,11 +192,21 @@
         kernel,
         out_shape=[jax.ShapeDtypeStruct(s, F32) for s in outs],
         in_specs=[vmem] * len(args),
-        out_specs=[vmem] * len(outs),
-        scratch_shapes=[pltpu.VMEM(s, F32) for s in scratch],
+        out_specs=[pl.BlockSpec(memory_space=pltpu.HBM) if copies else vmem] * len(outs),
+        scratch_shapes=[pltpu.VMEM(s, F32) for s in scratch] + [pltpu.SemaphoreType.DMA((copies,))] * (copies > 0),
         compiler_params=pltpu.CompilerParams(vmem_limit_bytes=held + SPARE),
         cost_estimate=pl.CostEstimate(flops=flops, bytes_accessed=0 if flops == 1000 else size, transcendentals=0),
     )(*args)
+
+
+def coarse_coefficients(m, c1, c2):
+    for i in range(4):
+        x = coarse_sum(blocks_of(m[2 * i]), blocks_of(m[2 * i + 1]))
+        for k, a in enumerate(x):
+            c1[i, :, 128 * k : 128 * k + 128] = 0.125 * a
+    for i in range(2):
+        even, odd = coarse_sum(blocks_of(c1[2 * i]), blocks_of(c1[2 * i + 1]), True)
+        c2[i] = 0.125 * (even + pltpu.roll(odd, 4, 0))
 
 
 def pack_zero(p, d, m, left, right, to_left, to_right):
@@ -245,7 +255,7 @@
     ]
 
 
-def level_zero(p, d, m, left, right, nleft, nright, field, s1, c1, up, down, me, de, w, fa, fb, fz, v, u):
+def level_zero(p, d, m, left, right, c1, nleft, nright, field, s1, up, down, me, de, w, fa, fb, fz, v, u):
     _, _, _, (low, high, nlow, nhigh) = scalars()
     at = iota((8, 1024), 0)
     for r in range(14):
@@ -274,10 +284,8 @@
         r = 2 * i + 3
         x = residual_row(v, de, me, fa, fb, fz, r, 16)
         y = residual_row(v, de, me, fa, fb, fz, r + 1, 16)
-        mx, my = blocks_of(me[r, 0:16]), blocks_of(me[r + 1, 0:16])
-        for k, (a, b) in enumerate(zip(coarse_sum(x, y), coarse_sum(mx, my))):
+        for k, a in enumerate(coarse_sum(x, y)):
             s1[i, :, 128 * k : 128 * k + 128] = 0.5 * a
-            c1[i, :, 128 * k : 128 * k + 128] = 0.125 * b
         return carry
 
     lax.fori_loop(0, 4, coarse, 0)
@@ -302,8 +310,8 @@
         to_right[r] = jnp.where(at >= 4, vc, pltpu.roll(vs, 4, 0))
 
 
-def level_one(s, c, left, right, nleft, nright, f0, se, ce, field, send, keep, up, down, v, u, fa, fb, fz, w):
-    _, _, core, (low, high, nlow, nhigh) = scalars()
+def level_one(s, c, left, right, nleft, nright, f0, field, s2, up, down, se, ce, fa, fb, fz, w, v, u):
+    _, _, _, (low, high, nlow, nhigh) = scalars()
     at = iota((8, 512), 0)
     for r in range(12):
         a = r - 4
@@ -318,26 +326,18 @@
         x, y = nright[r] * nhigh, nleft[r] * nlow
         ce[r, 8:16] = jnp.where(at < 4, x, y)
         se[r, 8:16] = jnp.where(at < 4, pltpu.roll(x, 4, 0), pltpu.roll(y, 4, 0))
-    faces(ce, (2, 10), fa, fb, fz, w, 4)
+    faces(ce, (1, 11), fa, fb, fz, w, 5)
 
     for r in range(2, 10):
         u[r] = w[r] * se[r]
     sweep(u, v, se, ce, fa, fb, fz, w, (3, 9), 3)
     field[...] = v[4:8, 0:8]
-    rows = iota((8, 256), 0)
-    index = iota((8, 256), 0) % 4
-    mine = rows // 4 == core
     for i in range(2):
         r = 2 * i + 4
         x = residual_row(v, se, ce, fa, fb, fz, r, 8)
         y = residual_row(v, se, ce, fa, fb, fz, r + 1, 8)
-        mx, my = blocks_of(ce[r, 0:8]), blocks_of(ce[r + 1, 0:8])
-        s2 = 0.5 * jnp.concatenate(coarse_sum(x, y, True), axis=1)
-        c2 = 0.125 * jnp.concatenate(coarse_sum(mx, my, True), axis=1)
-        s2 = jnp.where(mine, take_rows(s2, index[:, :128]), 0.0)
-        c2 = jnp.where(mine, take_rows(c2, index[:, :128]), 0.0)
-        send[i] = jnp.where(core == 0, c2, s2)
-        keep[i] = jnp.where(core == 0, s2, c2)
+        even, odd = coarse_sum(x, y, True)
+        s2[i] = 0.5 * (even + pltpu.roll(odd, 4, 0))
     for r in range(3):
         for t in range(2):
             up[2 * r + t] = f0[5 + r, 8 * t : 8 * t + 8]
@@ -351,30 +351,33 @@
 def pack_up(f0, f1, left, right, to_left, to_right):
     _, _, _, (low, high, _, _) = scalars()
     at = iota((8, 1024), 0)
-    for r in range(14):
-        for side, out in ((0, to_left), (1, to_right)):
-            tile = slice(8 * side, 8 * side + 8)
-            if r < 3:
-                x = left[2 * r + side] * low
-            elif r < 11:
-                x = f0[r - 3, tile]
-            else:
-                x = right[2 * (r - 11) + side] * high
-            if r < 2:
-                y = left[6 + r] * low
-            elif r < 4:
-                y = jnp.concatenate([f1[2 * r - 4], f1[2 * r - 3]], axis=1)
-            elif r < 6:
-                y = right[2 + r] * high
-            else:
-                y = None
-            if y is not None:
-                y = pltpu.roll(y, 4, 0)
-                x = jnp.where(at < 4, x, y) if side == 0 else jnp.where(at >= 4, x, y)
-            out[r] = x
-
-
-def level_up(me, de, w, fa, fb, fz, f0, left, right, nleft, nright, se, ce, f1, e2, out, res, v, u, v1, u1, fa1, fb1, fz1, w1):
+
+    def fine(r, side):
+        if r < 3:
+            return left[2 * r + side] * low
+        if r < 11:
+            return f0[r - 3, 8 * side : 8 * side + 8]
+        return right[2 * (r - 11) + side] * high
+
+    def pair(r):
+        if r < 2:
+            return left[6 + r] * low
+        if r < 4:
+            return jnp.concatenate([f1[2 * r - 4], f1[2 * r - 3]], axis=1)
+        return right[2 + r] * high
+
+    for t in range(7):
+        to_left[t] = jnp.where(at < 4, fine(2 * t, 0), pltpu.roll(fine(2 * t + 1, 0), 4, 0))
+        to_right[t] = jnp.where(at >= 4, fine(2 * t, 1), pltpu.roll(fine(2 * t + 1, 1), 4, 0))
+    for t in range(3):
+        to_left[7 + t] = jnp.where(at < 4, pair(2 * t), pltpu.roll(pair(2 * t + 1), 4, 0))
+        to_right[7 + t] = jnp.where(at >= 4, pair(2 * t), pltpu.roll(pair(2 * t + 1), 4, 0))
+
+
+def level_up(
+    me, de, w, fa, fb, fz, se, ce, fa1, fb1, fz1, w1, f0, f1, left, right, nleft, nright, e2,
+    out, res, v, u, v1, u1, kept, sent,
+):
     _, _, _, (low, high, nlow, nhigh) = scalars()
     at = iota((8, 512), 0)
     half = iota((8, 128), 0)
@@ -385,15 +388,16 @@
             f = f1[r - 4]
         else:
             f = right[2 + r // 2][:, 512 * (r % 2) : 512 * (r % 2) + 512] * high
-        x = nright[r // 2][:, 512 * (r % 2) : 512 * (r % 2) + 512] * nhigh
-        y = nleft[r // 2][:, 512 * (r % 2) : 512 * (r % 2) + 512] * nlow
-        g = jnp.where(at < 4, pltpu.roll(x, 4, 0), pltpu.roll(y, 4, 0))
+        x = nright[7 + r // 4][:, 512 * (r % 2) : 512 * (r % 2) + 512] * nhigh
+        y = nleft[7 + r // 4][:, 512 * (r % 2) : 512 * (r % 2) + 512] * nlow
+        if r % 4 > 1:
+            x, y = pltpu.roll(x, 4, 0), pltpu.roll(y, 4, 0)
+        g = jnp.where(at < 4, x, y)
         e = e2[r // 2]
         own = widen_split(take_rows(e, 2 + half // 2))
         beside = widen_split(take_rows(e, jnp.where(half < 4, 6 + half // 2, (half - 4) // 2)))
         v1[r, 0:8] = f + jnp.where(ce[r, 0:8] > 0.0, own, 0.0)
         v1[r, 8:16] = g + jnp.where(ce[r, 8:16] > 0.0, beside, 0.0)
-    faces(ce, (1, 11), fa1, fb1, fz1, w1, 5)
     sweep(v1, u1, se, ce, fa1, fb1, fz1, w1, (1, 11), 5)
     sweep(u1, v1, se, ce, fa1, fb1, fz1, w1, (2, 10), 4)
     zero = iota((8, 1024), 0)
@@ -404,7 +408,9 @@
             f = [f0[r - 3, 0:8], f0[r - 3, 8:16]]
         else:
             f = [right[2 * (r - 11)] * high, right[2 * (r - 11) + 1] * high]
-        x, y = nright[r] * nhigh, nleft[r] * nlow
+        x, y = nright[r // 2] * nhigh, nleft[r // 2] * nlow
+        if r % 2 > 0:
+            x, y = pltpu.roll(x, 4, 0), pltpu.roll(y, 4, 0)
         f.append(jnp.where(zero < 3, x, jnp.where(zero >= 5, y, 0.0)))
         e = v1[(r + 5) // 2]
         pieces = (
@@ -419,13 +425,21 @@
 
     sweep(v, u, de, me, fa, fb, fz, w, (1, 13), 2)
     sweep(u, v, de, me, fa, fb, fz, w, (2, 12), 2)
-    out[...] = v[3:11, 0:16]
+    first = pltpu.make_async_copy(v.at[3:11, 0:16], out, sent.at[0])
+    first.start()
 
     def final(r):
         for k, x in enumerate(residual_row(v, de, me, fa, fb, fz, r, 16)):
-            res[r - 3, :, 128 * k : 128 * k + 128] = x
-
-    over_rows(3, 11, 2, final)
+            kept[r - 3, :, 128 * k : 128 * k + 128] = x
+
+    over_rows(3, 7, 2, final)
+    second = pltpu.make_async_copy(kept.at[0:4], res.at[0:4], sent.at[1])
+    second.start()
+    over_rows(7, 11, 2, final)
+    third = pltpu.make_async_copy(kept.at[4:8], res.at[4:8], sent.at[2])
+    third.start()
+    for copy in (first, second, third):
+        copy.wait()
 
 
 def shifted(x, step):
@@ -615,18 +629,25 @@
 
 def level_two(mine, other, s, c, v, fa, fb, fz, ends, w, s3, c3, u):
     _, _, core, _ = scalars()
-    strips = mine.shape[0] // 16
+    strips = mine.shape[0] // 32
     rows, cols = 32, 8 * strips
+    first = iota((8, 128), 0) < 4
     edge = jnp.zeros((cols, 256), F32)
     for x in (c, v, u):
         x[0], x[rows + 1] = edge, edge
 
+    def place(target, r, y, near, far):
+        target[r, 8 * y : 8 * y + 8, 0:128] = jnp.where(first, near, pltpu.roll(far, 4, 0))
+        target[r, 8 * y : 8 * y + 8, 128:256] = jnp.where(first, pltpu.roll(near, 4, 0), far)
+
     def load(k):
         for y in range(strips):
+            at = 2 * (k * strips + y)
             for i in range(2):
-                x, z = mine[k * strips + y, i], other[k * strips + y, i]
-                s[2 * k + i + 1, 8 * y : 8 * y + 8] = jnp.where(core == 0, x, z)
-                c[2 * k + i + 1, 8 * y : 8 * y + 8] = jnp.where(core == 0, z, x)
+                r = 2 * k + i + 1
+                x, z = (mine[at, i], mine[at + 1, i]), (other[at, i], other[at + 1, i])
+                place(s, r, y, *(jnp.where(core == 0, a, b) for a, b in zip(x, z)))
+                place(c, r, y, *(jnp.where(core == 0, b, a) for a, b in zip(x, z)))
 
     over_rows(0, rows // 2, 2, load)
     fa[0] = 0.5 * c[1]
@@ -702,52 +723,55 @@
     return lax.ppermute(x, AX, [(i, i ^ 1) for i in range(w * y * k)])
 
 
-def gathered(x):
+def gathered(s2, c2):
     chips = lax.axis_size("wide") * lax.axis_size("ny")
-    return lax.all_to_all(jnp.broadcast_to(x[None], (chips,) + x.shape), ("wide", "ny"), 0, 0, tiled=True)
+    both = jnp.stack([s2, c2])
+    sent = jnp.broadcast_to(both[None], (chips,) + both.shape).reshape((-1,) + s2.shape)
+    return lax.all_to_all(sent, AX, 0, 0, tiled=True)
 
 
 def per_device(p, d, m):
     up = jnp.concatenate([p[5:8], m[5:8], d[6:8]], axis=0)
     down = jnp.concatenate([p[0:3], m[0:3], d[0:2]], axis=0)
     left, right = moved(up, 1, 0), moved(down, -1, 0)
+    c1, c2 = call(coarse_coefficients, [(4, 8, 512), (2, 8, 128)], [], m)
     to_left, to_right = call(pack_zero, [(14, 8, 1024)] * 2, [], p, d, m, left, right)
     nleft, nright = moved(to_right, 0, 1), moved(to_left, 0, -1)
     big = (14, 24, 1024)
-    f0, s1, c1, up, down, *zero = call(
+    f0, s1, up, down, *zero = call(
         level_zero,
-        [(8, 16, 1024), (4, 8, 512), (4, 8, 512), (7, 8, 512), (7, 8, 512)] + [big] * 6,
+        [(8, 16, 1024), (4, 8, 512)] + [(7, 8, 512)] * 2 + [big] * 6,
         [big] * 2,
-        p, d, m, left, right, nleft, nright,
+        p, d, m, left, right, c1, nleft, nright,
         flops=30_000_000,
     )
     left1, right1 = moved(up, 1, 0), moved(down, -1, 0)
     to_left, to_right = call(pack_one, [(12, 8, 512)] * 2, [], s1, c1, left1, right1)
     nleft1, nright1 = moved(to_right, 0, 1), moved(to_left, 0, -1)
     mid = (12, 16, 512)
-    se, ce, f1, send, keep, up, down = call(
+    f1, s2, up, down, *one = call(
         level_one,
-        [mid, mid, (4, 8, 512), (2, 8, 256), (2, 8, 256), (8, 8, 1024), (8, 8, 1024)],
-        [mid] * 6,
+        [(4, 8, 512), (2, 8, 128)] + [(8, 8, 1024)] * 2 + [mid] * 6,
+        [mid] * 2,
         s1, c1, left1, right1, nleft1, nright1, f0,
         flops=10_000_000,
     )
     hleft, hright = moved(up, 1, 0), moved(down, -1, 0)
-    pair = keep + other_core(send)
-    mine = gathered(pair)
+    mine = gathered(s2, c2)
     other = other_core(mine)
     whole, small = (34, 32, 256), (16, 16, 128)
     *two, s3, c3 = call(level_two, [whole] * 8 + [small] * 2, [whole], mine, other, flops=1000)
     s3, hleft, hright = lax.optimization_barrier((s3, hleft, hright))
-    to_left, to_right = call(pack_up, [(14, 8, 1024)] * 2, [], f0, f1, hleft, hright)
+    to_left, to_right = call(pack_up, [(10, 8, 1024)] * 2, [], f0, f1, hleft, hright)
     nhleft, nhright = moved(to_right, 0, 1), moved(to_left, 0, -1)
     (e2,) = call(coarse_levels, [(6, 8, 256)], [small] + [whole] * 2, s3, c3, *two, flops=1000)
     return call(
         level_up,
         [(8, 16, 1024)] * 2,
-        [big] * 2 + [mid] * 6,
-        *zero, f0, hleft, hright, nhleft, nhright, se, ce, f1, e2,
+        [big] * 2 + [mid] * 2 + [(8, 16, 1024)],
+        *zero, *one, f0, f1, hleft, hright, nhleft, nhright, e2,
         flops=30_000_000,
+        copies=3,
     )
 
 

time: 112 us -> 107 us (0.955)
  starting transfers between devices: 24.7 us -> 21.9 us
  waiting for transfers between devices: 35.4 us -> 32.7 us
  blocking collectives: 26.8 us -> 28.7 us
    ppermute x2 -> x1, starting transfers between devices: 3.71 us -> 1.17 us  [other_core(): return lax.ppermute(x, AX, [(i, i ^ 1) for i in range(w * y * k)])]
    ppermute x12, waiting for transfers between devices: 34.6 us -> 32.7 us  [moved(): return lax.ppermute(x, AX, pairs)]
    all_to_all x1, blocking collectives: 26.8 us -> 28.7 us  [gathered(): return lax.all_to_all(sent, AX, 0, 0, tiled=True)]
    pallas_call x8 -> x9, Pallas kernels: 21.1 us -> 20.7 us  [call(): pl.pallas_call(kernel, out_shape=[jax.ShapeDtypeStruct(s, F32) for s in o...]
  transfers between devices with their start and end apart: 14 -> 13, of which waited for: 10 -> 9; matrix products, arithmetic and copies ran while one was open for 0% -> 0% of each run, Pallas kernels for 7% -> 8%
where the time goes in v2:
time: 107 us
  waiting for transfers between devices  32.7 us (31%)
  blocking collectives  28.7 us (27%)
  starting transfers between devices  21.9 us (20%)
  Pallas kernels  20.7 us (19%)
  local copies, waits for them, and re-layouts  2.41 us (2%)
    ppermute x12, waiting for transfers between devices, moved(): return lax.ppermute(x, AX, pairs)  32.7 us
    all_to_all x1, blocking collectives, gathered(): return lax.all_to_all(sent, AX, 0, 0, tiled=True)  28.7 us
    pallas_call x9, Pallas kernels, call(): pl.pallas_call(kernel, out_shape=[jax.ShapeDtypeStruct(s, F32) for s in o...  20.7 us
    ppermute x12, starting transfers between devices, moved(): return lax.ppermute(x, AX, pairs)  20.7 us
    slice x2, local copies, waits for them, and re-layouts, per_device(): down = jnp.concatenate([p[0:3], m[0:3], d[0:2]], axis=0)  2.28 us
  transfers between devices with their start and end apart: 13, of which 9 were waited for; matrix products, arithmetic and copies ran while one was open for 0% of the time, Pallas kernels for 8%

profile of v2, /device:TPU:1, one launch (start us, length us, event | category | flops | bytes accessed | tf_op | source)
XLA Modules:
  0.0 107.3 jit_solution(4550404461899244804)
XLA Ops:
  0.6 1.0 fusion.2
  1.6 1.3 %fusion = (f32[3,16,1024]{2,1,0:T(8,128)S(1)}, f32[3,16,1024]{2,1,0:T(8,128)S(1)}, f32[3,16,1024]{2,1,0:T(8,128)S(1)}, f32[3,16,1024]{2,1,0:T(8,128)S(1)}) fusion(f32[8,16,1024]{2,1,0:T(8,128)} %p.3, f32[8,16,1024]{2,1,0:T(8,128)} %m.5), kind=kLoop, calls=%fused_computation.3 | loop fusion | bytes 1572864 | tf_op jit(solution)/shard_map/slice | solution.py:735
  3.0 2.5 %collective-permute-start = (f32[8,16,1024]{2,1,0:T(8,128)S(1)}, f32[8,16,1024]{2,1,0:T(8,128)S(1)}, u32[]{:S(2)}, u32[]{:S(2)}) collective-permute-start(f32[8,16,1024]{2,1,0:T(8,128)S(1)} %pad_maximum_fusion), channel_id=1, source_target_pairs={{0,8},{1,9},{2,10},{3,11},{4,12},{5,13},{6,14},{7,15},{8,16},{9,17... | collective-permute-start | bytes 1572872 | tf_op jit(solution)/shard_map/ppermute | solution.py:718
  5.6 4.4 %collective-permute-start.1 = (f32[8,16,1024]{2,1,0:T(8,128)S(1)}, f32[8,16,1024]{2,1,0:T(8,128)S(1)}, u32[]{:S(2)}, u32[]{:S(2)}) collective-permute-start(f32[8,16,1024]{2,1,0:T(8,128)S(1)} %pad_maximum_fusion.1), channel_id=1, source_target_pairs={{0,120},{1,121},{2,122},{3,123},{4,124},{5,125},{6,126},{7,127},{8... | collective-permute-start | bytes 1572872 | tf_op jit(solution)/shard_map/ppermute | solution.py:718
  10.0 11.5 %collective-permute-done.left = f32[8,16,1024]{2,1,0:T(8,128)S(1)} collective-permute-done((f32[8,16,1024]{2,1,0:T(8,128)S(1)}, f32[8,16,1024]{2,1,0:T(8,128)S(1)}, u32[]{:S(2)}, u32[]{:S(2)}) %collective-permute-start) | collective-permute-done | bytes 524320 | tf_op jit(solution)/shard_map/ppermute | solution.py:718
  21.7 2.4 %collective-permute-start.2 = (f32[14,8,1024]{2,1,0:T(8,128)S(1)}, f32[14,8,1024]{2,1,0:T(8,128)S(1)}, u32[]{:S(2)}, u32[]{:S(2)}) collective-permute-start(f32[14,8,1024]{2,1,0:T(8,128)S(1)} %get-tuple-element.44), channel_id=1, source_target_pairs={{0,1},{1,2},{2,3},{3,4},{4,5},{5,6},{6,7},{7,0},{8,9},{9,10},{10,1... | collective-permute-start | bytes 1376264 | tf_op jit(solution)/shard_map/ppermute | solution.py:718
  24.5 5.1 %collective-permute-done.2.nleft = f32[14,8,1024]{2,1,0:T(8,128)S(1)} collective-permute-done((f32[14,8,1024]{2,1,0:T(8,128)S(1)}, f32[14,8,1024]{2,1,0:T(8,128)S(1)}, u32[]{:S(2)}, u32[]{:S(2)}) %collective-permute-start.2) | collective-permute-done | bytes 458784 | tf_op jit(solution)/shard_map/ppermute | solution.py:718
  29.5 2.5 %collective-permute-done.3.nright = f32[14,8,1024]{2,1,0:T(8,128)S(1)} collective-permute-done((f32[14,8,1024]{2,1,0:T(8,128)S(1)}, f32[14,8,1024]{2,1,0:T(8,128)S(1)}, u32[]{:S(2)}, u32[]{:S(2)}) %collective-permute-start.3) | collective-permute-done | bytes 458784 | tf_op jit(solution)/shard_map/ppermute | solution.py:718
  32.0 5.5 %shard_map.52 = (f32[8,16,1024]{2,1,0:T(8,128)S(1)}, f32[4,8,512]{2,1,0:T(8,128)S(1)}, f32[7,8,512]{2,1,0:T(8,128)S(1)}, f32[7,8,512]{2,1,0:T(8,128)S(1)}, f32[1...) custom-call(f32[8,16,1024]{2,1,0:T(8,128)S(1)} %copy-done.1, ...), custom_call_target="tpu_custom_call" | custom-call | flops 30000000 | bytes 3604480 | tf_op jit(solution)/shard_map/pallas_call | solution.py:191
  37.6 5.0 %collective-permute-start.5 = (f32[7,8,512]{2,1,0:T(8,128)S(1)}, f32[7,8,512]{2,1,0:T(8,128)S(1)}, u32[]{:S(2)}, u32[]{:S(2)}) collective-permute-start(f32[7,8,512]{2,1,0:T(8,128)S(1)} %get-tuple-element.54), channel_id=1, source_target_pairs={{0,120},{1,121},{2,122},{3,123},{4,124},{5,125},{6,126},{7,127},{8... | collective-permute-start | bytes 344072 | tf_op jit(solution)/shard_map/ppermute | solution.py:718
  42.6 3.3 %collective-permute-done.4.left = f32[7,8,512]{2,1,0:T(8,128)S(1)} collective-permute-done((f32[7,8,512]{2,1,0:T(8,128)S(1)}, f32[7,8,512]{2,1,0:T(8,128)S(1)}, u32[]{:S(2)}, u32[]{:S(2)}) %collective-permute-start.4) | collective-permute-done | bytes 114720 | tf_op jit(solution)/shard_map/ppermute | solution.py:718
  46.2 0.5 collective-permute-start.7
  46.7 2.1 %collective-permute-done.6.nleft = f32[12,8,512]{2,1,0:T(8,128)S(1)} collective-permute-done((f32[12,8,512]{2,1,0:T(8,128)S(1)}, f32[12,8,512]{2,1,0:T(8,128)S(1)}, u32[]{:S(2)}, u32[]{:S(2)}) %collective-permute-start.6) | collective-permute-done | bytes 196640 | tf_op jit(solution)/shard_map/ppermute | solution.py:718
  48.8 2.8 %collective-permute-done.7.nright = f32[12,8,512]{2,1,0:T(8,128)S(1)} collective-permute-done((f32[12,8,512]{2,1,0:T(8,128)S(1)}, f32[12,8,512]{2,1,0:T(8,128)S(1)}, u32[]{:S(2)}, u32[]{:S(2)}) %collective-permute-start.7) | collective-permute-done | bytes 196640 | tf_op jit(solution)/shard_map/ppermute | solution.py:718
  51.6 1.2 %shard_map.54 = (f32[4,8,512]{2,1,0:T(8,128)S(1)}, f32[2,8,128]{2,1,0:T(8,128)S(1)}, f32[8,8,1024]{2,1,0:T(8,128)S(1)}, f32[8,8,1024]{2,1,0:T(8,128)S(1)}, f32[1...) custom-call(f32[4,8,512]{2,1,0:T(8,128)S(1)} %get-tuple-element.52.s, ...), custom_call_target="tpu_custom_call" | custom-call | flops 10000000 | bytes 1277952 | tf_op jit(solution)/shard_map/pallas_call | solution.py:191
  52.9 28.7 %all_to_all.5.mine = f32[128,2,8,128]{3,2,1,0:T(8,128)S(1)} all-to-all(f32[128,2,8,128]{3,2,1,0:T(8,128)S(1)} %bitcast.5), channel_id=1, replica_groups=mesh['wide'=16,'ny'=4,'core'=2] {'wide','ny','core'}, dimensions={0} | all-to-all | bytes 2097152 | tf_op jit(solution)/shard_map/all_to_all | solution.py:730
  81.5 1.2 %collective-permute-start.8 = (f32[128,2,8,128]{3,2,1,0:T(8,128)S(1)}, f32[128,2,8,128]{3,2,1,0:T(8,128)S(1)}, u32[]{:S(2)}, u32[]{:S(2)}) collective-permute-start(f32[128,2,8,128]{3,2,1,0:T(8,128)S(1)} %all_to_all.5.mine), channel_id=1, source_target_pairs={{0,1},{1,0},{2,3},{3,2},{4,5},{5,4},{6,7},{7,6},{8,9},{9,8},{10,11... | collective-permute-start | bytes 3145736 | tf_op jit(solution)/shard_map/ppermute | solution.py:723
  83.2 4.3 %collective-permute-start.10 = (f32[8,8,1024]{2,1,0:T(8,128)S(1)}, f32[8,8,1024]{2,1,0:T(8,128)S(1)}, u32[]{:S(2)}, u32[]{:S(2)}) collective-permute-start(f32[8,8,1024]{2,1,0:T(8,128)S(1)} %get-tuple-element.69), channel_id=1, source_target_pairs={{0,120},{1,121},{2,122},{3,123},{4,124},{5,125},{6,126},{7,127},{8... | collective-permute-start | bytes 786440 | tf_op jit(solution)/shard_map/ppermute | solution.py:718
  87.5 4.3 %shard_map.55 = (f32[34,32,256]{2,1,0:T(8,128)S(1)}, f32[34,32,256]{2,1,0:T(8,128)S(1)}, f32[34,32,256]{2,1,0:T(8,128)S(1)}, f32[34,32,256]{2,1,0:T(8,128)S(1)},...) custom-call(f32[128,2,8,128]{3,2,1,0:T(8,128)S(1)} %all_to_all.5.min, ...), custom_call_target="tpu_custom_call" | custom-call | flops 1000 | tf_op jit(solution)/shard_map/pallas_call | solution.py:191
  91.8 2.2 %collective-permute-done.9.left = f32[8,8,1024]{2,1,0:T(8,128)S(1)} collective-permute-done((f32[8,8,1024]{2,1,0:T(8,128)S(1)}, f32[8,8,1024]{2,1,0:T(8,128)S(1)}, u32[]{:S(2)}, u32[]{:S(2)}) %collective-permute-start.9) | collective-permute-done | bytes 262176 | tf_op jit(solution)/shard_map/ppermute | solution.py:718
  94.1 0.8 collective-permute-start.11
  94.9 3.5 %shard_map.57.e2 = f32[6,8,256]{2,1,0:T(8,128)S(1)} custom-call(f32[16,16,128]{2,1,0:T(8,128)S(1)} %get-tuple-element.74.s3, f32[16,16,128]{2,1,0:T(8,128)S(1)} %get-tuple-element.75.c3, f32[34,32,256]{2,1,0:T(8,128)S(1)} %get-tuple-element.76.s, f32[34,32,256]{2,1,0:T(8,128)S(1)} %get-tuple-element.77.c, f32[34,32,256]{2,1,0:T(8,128)S(1)} %get-tuple-element.78.v, ...), custom_call_target="tpu_custom_call" | custom-call | flops 1000 | tf_op jit(solution)/shard_map/pallas_call | solution.py:191
  98.9 2.8 %collective-permute-done.12.nright = f32[10,8,1024]{2,1,0:T(8,128)S(1)} collective-permute-done((f32[10,8,1024]{2,1,0:T(8,128)S(1)}, f32[10,8,1024]{2,1,0:T(8,128)S(1)}, u32[]{:S(2)}, u32[]{:S(2)}) %collective-permute-start.12) | collective-permute-done | bytes 327712 | tf_op jit(solution)/shard_map/ppermute | solution.py:718
  101.6 5.7 %shard_map.58 = (f32[8,16,1024]{2,1,0:T(8,128)}, f32[8,16,1024]{2,1,0:T(8,128)}) custom-call(f32[14,24,1024]{2,1,0:T(8,128)S(1)} %get-tuple-element.46.me, f32[14,24,1024]{2,1,0:T(8,128)S(1)} %get-tuple-element.47.de, f32[14,24,1024]{2,1,0:T(8,128)S(1)} %get-tuple-element.48.w, f32[14,24,1024]{2,1,0:T(8,128)S(1)} %get-tuple-element.49.fa, ...), custom_call_target="tpu_custom_call" | custom-call | flops 30000000 | bytes 12435456 | tf_op jit(solution)/shard_map/pallas_call | solution.py:191
  (24 shorter events, 2.1 us)
Async XLA Ops:
  2.9 18.6 %copy-start = (f32[8,16,1024]{2,1,0:T(8,128)S(1)}, f32[8,16,1024]{2,1,0:T(8,128)}, u32[]{:S(2)}) copy-start(f32[8,16,1024]{2,1,0:T(8,128)} %m.5) | copy-start | bytes 1572868
  2.9 18.6 %copy-start.1 = (f32[8,16,1024]{2,1,0:T(8,128)S(1)}, f32[8,16,1024]{2,1,0:T(8,128)}, u32[]{:S(2)}) copy-start(f32[8,16,1024]{2,1,0:T(8,128)} %p.3) | copy-start | bytes 1572868
  2.9 18.6 %copy-start.2 = (f32[8,16,1024]{2,1,0:T(8,128)S(1)}, f32[8,16,1024]{2,1,0:T(8,128)}, u32[]{:S(2)}) copy-start(f32[8,16,1024]{2,1,0:T(8,128)} %d.3) | copy-start | bytes 1572868
  3.0 18.5 %collective-permute-start = (f32[8,16,1024]{2,1,0:T(8,128)S(1)}, f32[8,16,1024]{2,1,0:T(8,128)S(1)}, u32[]{:S(2)}, u32[]{:S(2)}) collective-permute-start(f32[8,16,1024]{2,1,0:T(8,128)S(1)} %pad_maximum_fusion), channel_id=1, source_target_pairs={{0,8},{1,9},{2,10},{3,11},{4,12},{5,13},{6,14},{7,15},{8,16},{9,17... | collective-permute-start | bytes 1572872 | tf_op jit(solution)/shard_map/ppermute | solution.py:718
  5.6 15.9 %collective-permute-start.1 = (f32[8,16,1024]{2,1,0:T(8,128)S(1)}, f32[8,16,1024]{2,1,0:T(8,128)S(1)}, u32[]{:S(2)}, u32[]{:S(2)}) collective-permute-start(f32[8,16,1024]{2,1,0:T(8,128)S(1)} %pad_maximum_fusion.1), channel_id=1, source_target_pairs={{0,120},{1,121},{2,122},{3,123},{4,124},{5,125},{6,126},{7,127},{8... | collective-permute-start | bytes 1572872 | tf_op jit(solution)/shard_map/ppermute | solution.py:718
  21.7 7.8 %collective-permute-start.2 = (f32[14,8,1024]{2,1,0:T(8,128)S(1)}, f32[14,8,1024]{2,1,0:T(8,128)S(1)}, u32[]{:S(2)}, u32[]{:S(2)}) collective-permute-start(f32[14,8,1024]{2,1,0:T(8,128)S(1)} %get-tuple-element.44), channel_id=1, source_target_pairs={{0,1},{1,2},{2,3},{3,4},{4,5},{5,6},{6,7},{7,0},{8,9},{9,10},{10,1... | collective-permute-start | bytes 1376264 | tf_op jit(solution)/shard_map/ppermute | solution.py:718
  24.1 7.9 %collective-permute-start.3 = (f32[14,8,1024]{2,1,0:T(8,128)S(1)}, f32[14,8,1024]{2,1,0:T(8,128)S(1)}, u32[]{:S(2)}, u32[]{:S(2)}) collective-permute-start(f32[14,8,1024]{2,1,0:T(8,128)S(1)} %get-tuple-element.45), channel_id=1, source_target_pairs={{0,7},{1,0},{2,1},{3,2},{4,3},{5,4},{6,5},{7,6},{8,15},{9,8},{10,9... | collective-permute-start | bytes 1376264 | tf_op jit(solution)/shard_map/ppermute | solution.py:718
  37.5 8.4 %collective-permute-start.4 = (f32[7,8,512]{2,1,0:T(8,128)S(1)}, f32[7,8,512]{2,1,0:T(8,128)S(1)}, u32[]{:S(2)}, u32[]{:S(2)}) collective-permute-start(f32[7,8,512]{2,1,0:T(8,128)S(1)} %get-tuple-element.53), channel_id=1, source_target_pairs={{0,8},{1,9},{2,10},{3,11},{4,12},{5,13},{6,14},{7,15},{8,16},{9,17... | collective-permute-start | bytes 344072 | tf_op jit(solution)/shard_map/ppermute | solution.py:718
  37.6 8.3 %collective-permute-start.5 = (f32[7,8,512]{2,1,0:T(8,128)S(1)}, f32[7,8,512]{2,1,0:T(8,128)S(1)}, u32[]{:S(2)}, u32[]{:S(2)}) collective-permute-start(f32[7,8,512]{2,1,0:T(8,128)S(1)} %get-tuple-element.54), channel_id=1, source_target_pairs={{0,120},{1,121},{2,122},{3,123},{4,124},{5,125},{6,126},{7,127},{8... | collective-permute-start | bytes 344072 | tf_op jit(solution)/shard_map/ppermute | solution.py:718
  46.0 2.8 %collective-permute-start.6 = (f32[12,8,512]{2,1,0:T(8,128)S(1)}, f32[12,8,512]{2,1,0:T(8,128)S(1)}, u32[]{:S(2)}, u32[]{:S(2)}) collective-permute-start(f32[12,8,512]{2,1,0:T(8,128)S(1)} %get-tuple-element.55), channel_id=1, source_target_pairs={{0,1},{1,2},{2,3},{3,4},{4,5},{5,6},{6,7},{7,0},{8,9},{9,10},{10,1... | collective-permute-start | bytes 589832 | tf_op jit(solution)/shard_map/ppermute | solution.py:718
  46.2 5.4 %collective-permute-start.7 = (f32[12,8,512]{2,1,0:T(8,128)S(1)}, f32[12,8,512]{2,1,0:T(8,128)S(1)}, u32[]{:S(2)}, u32[]{:S(2)}) collective-permute-start(f32[12,8,512]{2,1,0:T(8,128)S(1)} %get-tuple-element.56), channel_id=1, source_target_pairs={{0,7},{1,0},{2,1},{3,2},{4,3},{5,4},{6,5},{7,6},{8,15},{9,8},{10,9... | collective-permute-start | bytes 589832 | tf_op jit(solution)/shard_map/ppermute | solution.py:718
  81.5 6.0 %collective-permute-start.8 = (f32[128,2,8,128]{3,2,1,0:T(8,128)S(1)}, f32[128,2,8,128]{3,2,1,0:T(8,128)S(1)}, u32[]{:S(2)}, u32[]{:S(2)}) collective-permute-start(f32[128,2,8,128]{3,2,1,0:T(8,128)S(1)} %all_to_all.5.mine), channel_id=1, source_target_pairs={{0,1},{1,0},{2,3},{3,2},{4,5},{5,4},{6,7},{7,6},{8,9},{9,8},{10,11... | collective-permute-start | bytes 3145736 | tf_op jit(solution)/shard_map/ppermute | solution.py:723
  82.7 11.3 %collective-permute-start.9 = (f32[8,8,1024]{2,1,0:T(8,128)S(1)}, f32[8,8,1024]{2,1,0:T(8,128)S(1)}, u32[]{:S(2)}, u32[]{:S(2)}) collective-permute-start(f32[8,8,1024]{2,1,0:T(8,128)S(1)} %get-tuple-element.68), channel_id=1, source_target_pairs={{0,8},{1,9},{2,10},{3,11},{4,12},{5,13},{6,14},{7,15},{8,16},{9,17... | collective-permute-start | bytes 786440 | tf_op jit(solution)/shard_map/ppermute | solution.py:718
  83.2 10.8 %collective-permute-start.10 = (f32[8,8,1024]{2,1,0:T(8,128)S(1)}, f32[8,8,1024]{2,1,0:T(8,128)S(1)}, u32[]{:S(2)}, u32[]{:S(2)}) collective-permute-start(f32[8,8,1024]{2,1,0:T(8,128)S(1)} %get-tuple-element.69), channel_id=1, source_target_pairs={{0,120},{1,121},{2,122},{3,123},{4,124},{5,125},{6,126},{7,127},{8... | collective-permute-start | bytes 786440 | tf_op jit(solution)/shard_map/ppermute | solution.py:718
  94.1 4.8 %collective-permute-start.11 = (f32[10,8,1024]{2,1,0:T(8,128)S(1)}, f32[10,8,1024]{2,1,0:T(8,128)S(1)}, u32[]{:S(2)}, u32[]{:S(2)}) collective-permute-start(f32[10,8,1024]{2,1,0:T(8,128)S(1)} %get-tuple-element.72), channel_id=1, source_target_pairs={{0,1},{1,2},{2,3},{3,4},{4,5},{5,6},{6,7},{7,0},{8,9},{9,10},{10,1... | collective-permute-start | bytes 983048 | tf_op jit(solution)/shard_map/ppermute | solution.py:718
  94.8 6.8 %collective-permute-start.12 = (f32[10,8,1024]{2,1,0:T(8,128)S(1)}, f32[10,8,1024]{2,1,0:T(8,128)S(1)}, u32[]{:S(2)}, u32[]{:S(2)}) collective-permute-start(f32[10,8,1024]{2,1,0:T(8,128)S(1)} %get-tuple-element.73), channel_id=1, source_target_pairs={{0,7},{1,0},{2,1},{3,2},{4,3},{5,4},{6,5},{7,6},{8,15},{9,8},{10,9... | collective-permute-start | bytes 983048 | tf_op jit(solution)/shard_map/ppermute | solution.py:718

commit v3 on v2

--- a/solution.py
+++ b/solution.py
@@ -26,6 +26,8 @@
 
 
 def lanes(x, r, k):
+    if isinstance(x, tuple):
+        return jnp.concatenate([lanes(part, r, k) for part in x], axis=0)
     return x[r, :, 128 * k : 128 * k + 128]
 
 
@@ -212,7 +214,7 @@
 def pack_zero(p, d, m, left, right, to_left, to_right):
     _, _, _, (low, high, _, _) = scalars()
     at = iota((8, 1024), 0)
-    for r in range(14):
+    for r in range(1, 13):
         a = r - 3
         for side, out in ((0, to_left), (1, to_right)):
             tile = slice(8 * side, 8 * side + 8)
@@ -226,10 +228,10 @@
                 vd = right[a - 2, tile] * high if a < 10 else jnp.zeros_like(vp)
             if side == 0:
                 vm, vd = pltpu.roll(vm, 3, 0), pltpu.roll(vd, 6, 0)
-                out[r] = jnp.where(at < 3, vp, jnp.where(at < 6, vm, vd))
+                out[r - 1] = jnp.where(at < 3, vp, jnp.where(at < 6, vm, vd))
             else:
                 vm, vd = pltpu.roll(vm, 5, 0), pltpu.roll(vd, 2, 0)
-                out[r] = jnp.where(at >= 5, vp, jnp.where(at >= 2, vm, vd))
+                out[r - 1] = jnp.where(at >= 5, vp, jnp.where(at >= 2, vm, vd))
 
 
 def faces(c, rows, fa, fb, fz, w, step):
@@ -243,7 +245,7 @@
     def one(r):
         for k, a in enumerate(row_operator(source, r, c, fa, fb, fz)):
             at = slice(128 * k, 128 * k + 128)
-            target[r, :, at] = source[r, :, at] + w[r, :, at] * (s[r, :, at] - a)
+            target[r, :, at] = source[r, :, at] + w[r, :, at] * (lanes(s, r, k) - a)
 
     over_rows(rows[0], rows[1], step, one)
 
@@ -255,29 +257,83 @@
     ]
 
 
-def level_zero(p, d, m, left, right, c1, nleft, nright, field, s1, up, down, me, de, w, fa, fb, fz, v, u):
-    _, _, _, (low, high, nlow, nhigh) = scalars()
-    at = iota((8, 1024), 0)
+def across(r, v, c, s, fa, fz, diagonal, left_over):
+    lane = iota((c.shape[1], 128), 1)
+    count = c.shape[2] // 128
+    turn = lambda x, k: pltpu.roll(lanes(x, r, k), 127, 1) if k < count else 0.0
+    here, there, c_next, v_next = lanes(c, r, 0), lanes(v, r, 0), turn(c, 0), turn(v, 0)
+    for k in range(count):
+        at = slice(128 * k, 128 * k + 128)
+        c_later, v_later = turn(c, k + 1), turn(v, k + 1)
+        z = 0.5 * (here + jnp.where(lane == 127, c_later, c_next))
+        flux = z * (jnp.where(lane == 127, v_later, v_next) - there)
+        z_turned, flux_turned = pltpu.roll(z, 1, 1), pltpu.roll(flux, 1, 1)
+        if k == 0:
+            z_before, flux_before = 0.5 * here, 0.5 * here * there
+        above, below = 0.5 * (here + lanes(c, r + 1, k)), 0.5 * (here + lanes(c, r - 1, k))
+        fa[r, :, at], fz[r, :, at] = above, z
+        diagonal[r, :, at] = above + below + (z + jnp.where(lane == 0, z_before, z_turned))
+        a = above * (there - lanes(v, r + 1, k)) + below * (there - lanes(v, r - 1, k))
+        a = a + (jnp.where(lane == 0, flux_before, flux_turned) - flux)
+        left_over[r, :, at] = s[r, :, at] - a
+        if k + 1 < count:
+            here, there = lanes(c, r, k + 1), lanes(v, r, k + 1)
+        c_next, v_next, z_before, flux_before = c_later, v_later, z_turned, flux_turned
+
+
+def first_face(c, fa):
+    fa[0] = 0.5 * (c[0] + c[1])
+
+
+def level_zero_own(p, d, m, left, right, v, me, de, fa, fz, diagonal, left_over):
+    _, _, _, (low, high, _, _) = scalars()
     for r in range(14):
         a = r - 3
         if a < 0:
-            v[r, 0:16], me[r, 0:16] = left[r] * low, left[3 + r] * low
-            de[r, 0:16] = left[5 + r] * low if r > 0 else jnp.zeros((16, 1024), F32)
+            v[r], me[r] = left[r] * low, left[3 + r] * low
+            de[r] = left[5 + r] * low if r > 0 else jnp.zeros((16, 1024), F32)
         elif a < 8:
-            v[r, 0:16], me[r, 0:16], de[r, 0:16] = p[a], m[a], d[a]
+            v[r], me[r], de[r] = p[a], m[a], d[a]
         else:
-            v[r, 0:16], me[r, 0:16] = right[a - 8] * high, right[a - 5] * high
-            de[r, 0:16] = right[a - 2] * high if a < 10 else jnp.zeros((16, 1024), F32)
-        x, y = nright[r] * nhigh, nleft[r] * nlow
-        v[r, 16:24] = jnp.where(at < 3, x, jnp.where(at >= 5, y, 0.0))
+            v[r], me[r] = right[a - 8] * high, right[a - 5] * high
+            de[r] = right[a - 2] * high if a < 10 else jnp.zeros((16, 1024), F32)
+    first_face(me, fa)
+    over_rows(1, 13, 2, lambda r: across(r, v, me, de, fa, fz, diagonal, left_over))
+
+
+def level_zero(
+    own_v, own_me, own_de, own_fa, own_fz, own_diagonal, own_left_over, c1, nleft, nright,
+    field, s1, up, down, me, de, fa, fz, fb, w, v, u, beside, diagonal, left_over,
+):
+    _, _, _, (_, _, nlow, nhigh) = scalars()
+    at = iota((8, 1024), 0)
+    for r in (0, 13):
+        beside[r] = me[r] = de[r] = jnp.zeros((8, 1024), F32)
+    for r in range(1, 13):
+        x, y = nright[r - 1] * nhigh, nleft[r - 1] * nlow
+        beside[r] = jnp.where(at < 3, x, jnp.where(at >= 5, y, 0.0))
         x3, y3 = pltpu.roll(x, 5, 0), pltpu.roll(y, 3, 0)
-        me[r, 16:24] = jnp.where(at < 3, x3, jnp.where(at >= 5, y3, 0.0))
+        me[r] = jnp.where(at < 3, x3, jnp.where(at >= 5, y3, 0.0))
         x6, y6 = pltpu.roll(x, 2, 0), pltpu.roll(y, 6, 0)
-        de[r, 16:24] = jnp.where(at < 2, x6, jnp.where(at >= 6, y6, 0.0))
-    faces(me, (1, 13), fa, fb, fz, w, 2)
-    u[0], u[13] = v[0], v[13]
-    sweep(v, u, de, me, fa, fb, fz, w, (1, 13), 2)
-    sweep(u, v, de, me, fa, fb, fz, w, (2, 12), 2)
+        de[r] = jnp.where(at < 2, x6, jnp.where(at >= 6, y6, 0.0))
+    first_face(me, fa)
+    pairs = [(own_v, beside), (own_me, me), (own_diagonal, diagonal), (own_left_over, left_over)]
+
+    def one(r):
+        across(r, beside, me, de, fa, fz, diagonal, left_over)
+        for k in range(8):
+            lane = slice(128 * k, 128 * k + 128)
+            there, here, total, rest = [lanes(x, r, k) for x in pairs]
+            y = 0.5 * (here + following(here, 0))
+            flux = y * (following(there, 0) - there)
+            total = total + (y + preceding(y, 0))
+            factor = jnp.where(here > 0.0, OMEGA / total, 0.0)
+            fb[r, :, lane], w[r, :, lane] = y, factor
+            u[r, :, lane] = there + factor * (rest - (preceding(flux, 0) - flux))
+
+    over_rows(1, 13, 2, one)
+    me, de, fa, fz = (own_me, me), (own_de, de), (own_fa, fa), (own_fz, fz)
+    sweep(u, v, de, me, fa, fb, fz, w, (2, 12), 3)
     field[...] = v[3:11, 0:16]
 
     def coarse(i, carry):
@@ -296,7 +352,7 @@
 def pack_one(s, c, left, right, to_left, to_right):
     _, _, _, (low, high, _, _) = scalars()
     at = iota((8, 512), 0)
-    for r in range(12):
+    for r in range(1, 11):
         a = r - 4
         if a < 0:
             vc = left[3 + r] * low
@@ -306,8 +362,8 @@
         else:
             vc = right[a - 1] * high
             vs = right[a - 4] * high if a < 7 else jnp.zeros_like(vc)
-        to_left[r] = jnp.where(at < 4, vc, pltpu.roll(vs, 4, 0))
-        to_right[r] = jnp.where(at >= 4, vc, pltpu.roll(vs, 4, 0))
+        to_left[r - 1] = jnp.where(at < 4, vc, pltpu.roll(vs, 4, 0))
+        to_right[r - 1] = jnp.where(at >= 4, vc, pltpu.roll(vs, 4, 0))
 
 
 def level_one(s, c, left, right, nleft, nright, f0, field, s2, up, down, se, ce, fa, fb, fz, w, v, u):
@@ -323,7 +379,10 @@
         else:
             ce[r, 0:8] = right[a - 1] * high
             se[r, 0:8] = right[a - 4] * high if a < 7 else jnp.zeros((8, 512), F32)
-        x, y = nright[r] * nhigh, nleft[r] * nlow
+        if r in (0, 11):
+            ce[r, 8:16] = se[r, 8:16] = jnp.zeros((8, 512), F32)
+            continue
+        x, y = nright[r - 1] * nhigh, nleft[r - 1] * nlow
         ce[r, 8:16] = jnp.where(at < 4, x, y)
         se[r, 8:16] = jnp.where(at < 4, pltpu.roll(x, 4, 0), pltpu.roll(y, 4, 0))
     faces(ce, (1, 11), fa, fb, fz, w, 5)
@@ -366,16 +425,17 @@
             return jnp.concatenate([f1[2 * r - 4], f1[2 * r - 3]], axis=1)
         return right[2 + r] * high
 
-    for t in range(7):
-        to_left[t] = jnp.where(at < 4, fine(2 * t, 0), pltpu.roll(fine(2 * t + 1, 0), 4, 0))
-        to_right[t] = jnp.where(at >= 4, fine(2 * t, 1), pltpu.roll(fine(2 * t + 1, 1), 4, 0))
+    for t in range(6):
+        to_left[t] = jnp.where(at < 4, fine(2 * t + 1, 0), pltpu.roll(fine(2 * t + 2, 0), 4, 0))
+        to_right[t] = jnp.where(at >= 4, fine(2 * t + 1, 1), pltpu.roll(fine(2 * t + 2, 1), 4, 0))
     for t in range(3):
-        to_left[7 + t] = jnp.where(at < 4, pair(2 * t), pltpu.roll(pair(2 * t + 1), 4, 0))
-        to_right[7 + t] = jnp.where(at >= 4, pair(2 * t), pltpu.roll(pair(2 * t + 1), 4, 0))
+        to_left[6 + t] = jnp.where(at < 4, pair(2 * t), pltpu.roll(pair(2 * t + 1), 4, 0))
+        to_right[6 + t] = jnp.where(at >= 4, pair(2 * t), pltpu.roll(pair(2 * t + 1), 4, 0))
 
 
 def level_up(
-    me, de, w, fa, fb, fz, se, ce, fa1, fb1, fz1, w1, f0, f1, left, right, nleft, nright, e2,
+    own_me, own_de, own_fa, own_fz, me, de, fa, fz, fb, w, se, ce, fa1, fb1, fz1, w1,
+    f0, f1, left, right, nleft, nright, e2,
     out, res, v, u, v1, u1, kept, sent,
 ):
     _, _, _, (low, high, nlow, nhigh) = scalars()
@@ -388,8 +448,8 @@
             f = f1[r - 4]
         else:
             f = right[2 + r // 2][:, 512 * (r % 2) : 512 * (r % 2) + 512] * high
-        x = nright[7 + r // 4][:, 512 * (r % 2) : 512 * (r % 2) + 512] * nhigh
-        y = nleft[7 + r // 4][:, 512 * (r % 2) : 512 * (r % 2) + 512] * nlow
+        x = nright[6 + r // 4][:, 512 * (r % 2) : 512 * (r % 2) + 512] * nhigh
+        y = nleft[6 + r // 4][:, 512 * (r % 2) : 512 * (r % 2) + 512] * nlow
         if r % 4 > 1:
             x, y = pltpu.roll(x, 4, 0), pltpu.roll(y, 4, 0)
         g = jnp.where(at < 4, x, y)
@@ -408,10 +468,13 @@
             f = [f0[r - 3, 0:8], f0[r - 3, 8:16]]
         else:
             f = [right[2 * (r - 11)] * high, right[2 * (r - 11) + 1] * high]
-        x, y = nright[r // 2] * nhigh, nleft[r // 2] * nlow
-        if r % 2 > 0:
-            x, y = pltpu.roll(x, 4, 0), pltpu.roll(y, 4, 0)
-        f.append(jnp.where(zero < 3, x, jnp.where(zero >= 5, y, 0.0)))
+        if r in (0, 13):
+            f.append(jnp.zeros((8, 1024), F32))
+        else:
+            x, y = nright[(r - 1) // 2] * nhigh, nleft[(r - 1) // 2] * nlow
+            if r % 2 == 0:
+                x, y = pltpu.roll(x, 4, 0), pltpu.roll(y, 4, 0)
+            f.append(jnp.where(zero < 3, x, jnp.where(zero >= 5, y, 0.0)))
         e = v1[(r + 5) // 2]
         pieces = (
             (e[0:8], half // 2),
@@ -421,10 +484,12 @@
         for t, (part, index) in enumerate(pieces):
             fine = widen(take_rows(part, index), 8)
             tile = slice(8 * t, 8 * t + 8)
-            v[r, tile] = f[t] + jnp.where(me[r, tile] > 0.0, fine, 0.0)
-
-    sweep(v, u, de, me, fa, fb, fz, w, (1, 13), 2)
-    sweep(u, v, de, me, fa, fb, fz, w, (2, 12), 2)
+            inside = own_me[r, tile] if t < 2 else me[r]
+            v[r, tile] = f[t] + jnp.where(inside > 0.0, fine, 0.0)
+
+    me, de, fa, fz = (own_me, me), (own_de, de), (own_fa, fa), (own_fz, fz)
+    sweep(v, u, de, me, fa, fb, fz, w, (1, 13), 3)
+    sweep(u, v, de, me, fa, fb, fz, w, (2, 12), 3)
     first = pltpu.make_async_copy(v.at[3:11, 0:16], out, sent.at[0])
     first.start()
 
@@ -629,7 +694,7 @@
 
 def level_two(mine, other, s, c, v, fa, fb, fz, ends, w, s3, c3, u):
     _, _, core, _ = scalars()
-    strips = mine.shape[0] // 32
+    strips = mine.shape[0] // 16
     rows, cols = 32, 8 * strips
     first = iota((8, 128), 0) < 4
     edge = jnp.zeros((cols, 256), F32)
@@ -642,12 +707,12 @@
 
     def load(k):
         for y in range(strips):
-            at = 2 * (k * strips + y)
+            at = k * strips + y
             for i in range(2):
                 r = 2 * k + i + 1
-                x, z = (mine[at, i], mine[at + 1, i]), (other[at, i], other[at + 1, i])
-                place(s, r, y, *(jnp.where(core == 0, a, b) for a, b in zip(x, z)))
-                place(c, r, y, *(jnp.where(core == 0, b, a) for a, b in zip(x, z)))
+                for n, target in enumerate((s, c)):
+                    x, z = mine[at, n, i], other[at, n, i]
+                    place(target, r, y, jnp.where(core == 0, x, z), jnp.where(core == 0, z, x))
 
     over_rows(0, rows // 2, 2, load)
     fa[0] = 0.5 * c[1]
@@ -669,8 +734,8 @@
             ends[r, :, at], w[r, :, at] = e, factor
             u[r, :, at] = factor * s[r, :, at]
 
-    over_rows(1, rows + 1, 4, one)
-    over_rows(1, rows + 1, 4, lambda r: split_sweep(u, v, s, c, fa, fb, fz, ends, w, r))
+    over_rows(1, rows + 1, 8, one)
+    over_rows(1, rows + 1, 16, lambda r: split_sweep(u, v, s, c, fa, fb, fz, ends, w, r))
 
     def coarse(i):
         total = None
@@ -682,7 +747,7 @@
         total = (lanes(c, 2 * i + 1, 0) + lanes(c, 2 * i + 1, 1)) + (lanes(c, 2 * i + 2, 0) + lanes(c, 2 * i + 2, 1))
         c3[i] = 0.125 * half_columns(total)
 
-    over_rows(0, rows // 2, 2, coarse)
+    over_rows(0, rows // 2, 4, coarse)
 
 
 def coarse_levels(s3, c3, s, c, v, fa, fb, fz, ends, w, e2, e3, u, t):
@@ -724,10 +789,9 @@
 
 
 def gathered(s2, c2):
+    both = jnp.stack([s2, c2])
     chips = lax.axis_size("wide") * lax.axis_size("ny")
-    both = jnp.stack([s2, c2])
-    sent = jnp.broadcast_to(both[None], (chips,) + both.shape).reshape((-1,) + s2.shape)
-    return lax.all_to_all(sent, AX, 0, 0, tiled=True)
+    return lax.all_to_all(jnp.broadcast_to(both[None], (chips,) + both.shape), ("wide", "ny"), 0, 0, tiled=True)
 
 
 def per_device(p, d, m):
@@ -735,18 +799,20 @@
     down = jnp.concatenate([p[0:3], m[0:3], d[0:2]], axis=0)
     left, right = moved(up, 1, 0), moved(down, -1, 0)
     c1, c2 = call(coarse_coefficients, [(4, 8, 512), (2, 8, 128)], [], m)
-    to_left, to_right = call(pack_zero, [(14, 8, 1024)] * 2, [], p, d, m, left, right)
+    to_left, to_right = call(pack_zero, [(12, 8, 1024)] * 2, [], p, d, m, left, right)
     nleft, nright = moved(to_right, 0, 1), moved(to_left, 0, -1)
-    big = (14, 24, 1024)
+    big, own, halo = (14, 24, 1024), (14, 16, 1024), (14, 8, 1024)
+    alone = call(level_zero_own, [own] * 7, [], p, d, m, left, right, flops=20_000_000)
     f0, s1, up, down, *zero = call(
         level_zero,
-        [(8, 16, 1024), (4, 8, 512)] + [(7, 8, 512)] * 2 + [big] * 6,
-        [big] * 2,
-        p, d, m, left, right, c1, nleft, nright,
+        [(8, 16, 1024), (4, 8, 512)] + [(7, 8, 512)] * 2 + [halo] * 4 + [big] * 2,
+        [big] * 2 + [halo] * 3,
+        *alone, c1, nleft, nright,
         flops=30_000_000,
     )
+    zero = [*alone[1:5], *zero]
     left1, right1 = moved(up, 1, 0), moved(down, -1, 0)
-    to_left, to_right = call(pack_one, [(12, 8, 512)] * 2, [], s1, c1, left1, right1)
+    to_left, to_right = call(pack_one, [(10, 8, 512)] * 2, [], s1, c1, left1, right1)
     nleft1, nright1 = moved(to_right, 0, 1), moved(to_left, 0, -1)
     mid = (12, 16, 512)
     f1, s2, up, down, *one = call(
@@ -762,7 +828,7 @@
     whole, small = (34, 32, 256), (16, 16, 128)
     *two, s3, c3 = call(level_two, [whole] * 8 + [small] * 2, [whole], mine, other, flops=1000)
     s3, hleft, hright = lax.optimization_barrier((s3, hleft, hright))
-    to_left, to_right = call(pack_up, [(10, 8, 1024)] * 2, [], f0, f1, hleft, hright)
+    to_left, to_right = call(pack_up, [(9, 8, 1024)] * 2, [], f0, f1, hleft, hright)
     nhleft, nhright = moved(to_right, 0, 1), moved(to_left, 0, -1)
     (e2,) = call(coarse_levels, [(6, 8, 256)], [small] + [whole] * 2, s3, c3, *two, flops=1000)
     return call(

time: 107 us -> 103 us (0.963)
  waiting for transfers between devices: 32.7 us -> 30.1 us
    ppermute x12, waiting for transfers between devices: 32.7 us -> 30.1 us  [moved(): return lax.ppermute(x, AX, pairs)]
    ppermute x1, starting transfers between devices: 1.17 us -> 0.01 us  [other_core(): return lax.ppermute(x, AX, [(i, i ^ 1) for i in range(w * y * k)])]
    pallas_call x9 -> x10, Pallas kernels: 20.7 us -> 19.9 us  [call(): pl.pallas_call(kernel, out_shape=[jax.ShapeDtypeStruct(s, F32) for s in o...]
  transfers between devices with their start and end apart: 13 -> 13, of which waited for: 9 -> 9; matrix products, arithmetic and copies ran while one was open for 0% -> 0% of each run, Pallas kernels for 8% -> 9%
where the time goes in v3:
time: 103 us
  waiting for transfers between devices  30.1 us (29%)
  blocking collectives  28.3 us (27%)
  starting transfers between devices  21.7 us (21%)
  Pallas kernels  19.9 us (19%)
  local copies, waits for them, and re-layouts  2.41 us (2%)
    ppermute x12, waiting for transfers between devices, moved(): return lax.ppermute(x, AX, pairs)  30.1 us
    all_to_all x1, blocking collectives, gathered(): lax.all_to_all(jnp.broadcast_to(both[None], (chips,) + both.shape), ('wid...  28.3 us
    ppermute x12, starting transfers between devices, moved(): return lax.ppermute(x, AX, pairs)  21.7 us
    pallas_call x10, Pallas kernels, call(): pl.pallas_call(kernel, out_shape=[jax.ShapeDtypeStruct(s, F32) for s in o...  19.9 us
    slice x2, local copies, waits for them, and re-layouts, per_device(): down = jnp.concatenate([p[0:3], m[0:3], d[0:2]], axis=0)  2.28 us
  transfers between devices with their start and end apart: 13, of which 9 were waited for; matrix products, arithmetic and copies ran while one was open for 0% of the time, Pallas kernels for 9%

profile of v3, /device:TPU:1, one launch (start us, length us, event | category | flops | bytes accessed | tf_op | source)
XLA Modules:
  0.0 103.3 jit_solution(7961009974715394964)
XLA Ops:
  0.6 1.0 fusion.2
  1.6 1.3 %fusion = (f32[3,16,1024]{2,1,0:T(8,128)S(1)}, f32[3,16,1024]{2,1,0:T(8,128)S(1)}, f32[3,16,1024]{2,1,0:T(8,128)S(1)}, f32[3,16,1024]{2,1,0:T(8,128)S(1)}) fusion(f32[8,16,1024]{2,1,0:T(8,128)} %p.3, f32[8,16,1024]{2,1,0:T(8,128)} %m.5), kind=kLoop, calls=%fused_computation.3 | loop fusion | bytes 1572864 | tf_op jit(solution)/shard_map/slice | solution.py:799
  3.0 2.5 %collective-permute-start = (f32[8,16,1024]{2,1,0:T(8,128)S(1)}, f32[8,16,1024]{2,1,0:T(8,128)S(1)}, u32[]{:S(2)}, u32[]{:S(2)}) collective-permute-start(f32[8,16,1024]{2,1,0:T(8,128)S(1)} %pad_maximum_fusion), channel_id=1, source_target_pairs={{0,8},{1,9},{2,10},{3,11},{4,12},{5,13},{6,14},{7,15},{8,16},{9,17... | collective-permute-start | bytes 1572872 | tf_op jit(solution)/shard_map/ppermute | solution.py:783
  5.6 4.4 %collective-permute-start.1 = (f32[8,16,1024]{2,1,0:T(8,128)S(1)}, f32[8,16,1024]{2,1,0:T(8,128)S(1)}, u32[]{:S(2)}, u32[]{:S(2)}) collective-permute-start(f32[8,16,1024]{2,1,0:T(8,128)S(1)} %pad_maximum_fusion.1), channel_id=1, source_target_pairs={{0,120},{1,121},{2,122},{3,123},{4,124},{5,125},{6,126},{7,127},{8... | collective-permute-start | bytes 1572872 | tf_op jit(solution)/shard_map/ppermute | solution.py:783
  10.0 11.5 %collective-permute-done.left = f32[8,16,1024]{2,1,0:T(8,128)S(1)} collective-permute-done((f32[8,16,1024]{2,1,0:T(8,128)S(1)}, f32[8,16,1024]{2,1,0:T(8,128)S(1)}, u32[]{:S(2)}, u32[]{:S(2)}) %collective-permute-start) | collective-permute-done | bytes 524320 | tf_op jit(solution)/shard_map/ppermute | solution.py:783
  21.7 2.4 %collective-permute-start.2 = (f32[12,8,1024]{2,1,0:T(8,128)S(1)}, f32[12,8,1024]{2,1,0:T(8,128)S(1)}, u32[]{:S(2)}, u32[]{:S(2)}) collective-permute-start(f32[12,8,1024]{2,1,0:T(8,128)S(1)} %get-tuple-element.58), channel_id=1, source_target_pairs={{0,1},{1,2},{2,3},{3,4},{4,5},{5,6},{6,7},{7,0},{8,9},{9,10},{10,1... | collective-permute-start | bytes 1179656 | tf_op jit(solution)/shard_map/ppermute | solution.py:783
  24.4 1.9 %shard_map.50 = (f32[14,16,1024]{2,1,0:T(8,128)S(1)}, f32[14,16,1024]{2,1,0:T(8,128)S(1)}, f32[14,16,1024]{2,1,0:T(8,128)S(1)}, f32[14,16,1024]{2,1,0:T(8,128)S(...) custom-call(f32[8,16,1024]{2,1,0:T(8,128)S(1)} %copy-done.1, ...), custom_call_target="tpu_custom_call" | custom-call | flops 20000000 | bytes 2621440 | tf_op jit(solution)/shard_map/pallas_call | solution.py:193
  26.4 2.4 %collective-permute-done.2.nleft = f32[12,8,1024]{2,1,0:T(8,128)S(1)} collective-permute-done((f32[12,8,1024]{2,1,0:T(8,128)S(1)}, f32[12,8,1024]{2,1,0:T(8,128)S(1)}, u32[]{:S(2)}, u32[]{:S(2)}) %collective-permute-start.2) | collective-permute-done | bytes 393248 | tf_op jit(solution)/shard_map/ppermute | solution.py:783
  28.8 2.5 %collective-permute-done.3.nright = f32[12,8,1024]{2,1,0:T(8,128)S(1)} collective-permute-done((f32[12,8,1024]{2,1,0:T(8,128)S(1)}, f32[12,8,1024]{2,1,0:T(8,128)S(1)}, u32[]{:S(2)}, u32[]{:S(2)}) %collective-permute-start.3) | collective-permute-done | bytes 393248 | tf_op jit(solution)/shard_map/ppermute | solution.py:783
  31.3 4.2 %shard_map.53 = (f32[8,16,1024]{2,1,0:T(8,128)S(1)}, f32[4,8,512]{2,1,0:T(8,128)S(1)}, f32[7,8,512]{2,1,0:T(8,128)S(1)}, f32[7,8,512]{2,1,0:T(8,128)S(1)}, f32[1...) custom-call(f32[14,16,1024]{2,1,0:T(8,128)S(1)} %get-tuple-element.5, ...), custom_call_target="tpu_custom_call" | custom-call | flops 30000000 | bytes 7274496 | tf_op jit(solution)/shard_map/pallas_call | solution.py:193
  35.6 5.0 %collective-permute-start.5 = (f32[7,8,512]{2,1,0:T(8,128)S(1)}, f32[7,8,512]{2,1,0:T(8,128)S(1)}, u32[]{:S(2)}, u32[]{:S(2)}) collective-permute-start(f32[7,8,512]{2,1,0:T(8,128)S(1)} %get-tuple-element.68), channel_id=1, source_target_pairs={{0,120},{1,121},{2,122},{3,123},{4,124},{5,125},{6,126},{7,127},{8... | collective-permute-start | bytes 344072 | tf_op jit(solution)/shard_map/ppermute | solution.py:783
  40.5 3.3 %collective-permute-done.4.left = f32[7,8,512]{2,1,0:T(8,128)S(1)} collective-permute-done((f32[7,8,512]{2,1,0:T(8,128)S(1)}, f32[7,8,512]{2,1,0:T(8,128)S(1)}, u32[]{:S(2)}, u32[]{:S(2)}) %collective-permute-start.4) | collective-permute-done | bytes 114720 | tf_op jit(solution)/shard_map/ppermute | solution.py:783
  44.1 0.5 collective-permute-start.7
  44.6 1.8 %collective-permute-done.6.nleft = f32[10,8,512]{2,1,0:T(8,128)S(1)} collective-permute-done((f32[10,8,512]{2,1,0:T(8,128)S(1)}, f32[10,8,512]{2,1,0:T(8,128)S(1)}, u32[]{:S(2)}, u32[]{:S(2)}) %collective-permute-start.6) | collective-permute-done | bytes 163872 | tf_op jit(solution)/shard_map/ppermute | solution.py:783
  46.4 2.8 %collective-permute-done.7.nright = f32[10,8,512]{2,1,0:T(8,128)S(1)} collective-permute-done((f32[10,8,512]{2,1,0:T(8,128)S(1)}, f32[10,8,512]{2,1,0:T(8,128)S(1)}, u32[]{:S(2)}, u32[]{:S(2)}) %collective-permute-start.7) | collective-permute-done | bytes 163872 | tf_op jit(solution)/shard_map/ppermute | solution.py:783
  49.2 1.2 %shard_map.55 = (f32[4,8,512]{2,1,0:T(8,128)S(1)}, f32[2,8,128]{2,1,0:T(8,128)S(1)}, f32[8,8,1024]{2,1,0:T(8,128)S(1)}, f32[8,8,1024]{2,1,0:T(8,128)S(1)}, f32[1...) custom-call(f32[4,8,512]{2,1,0:T(8,128)S(1)} %get-tuple-element.66.s, ...), custom_call_target="tpu_custom_call" | custom-call | flops 10000000 | bytes 1212416 | tf_op jit(solution)/shard_map/pallas_call | solution.py:193
  50.5 28.3 %all_to_all.5.mine = f32[64,2,2,8,128]{4,3,2,1,0:T(8,128)S(1)} all-to-all(f32[64,2,2,8,128]{4,3,2,1,0:T(8,128)S(1)} %broadcast_in_dim.2), channel_id=1, replica_groups=mesh['wide'=16,'ny'=4,'core'=2] {'wide','ny'}, dimensions={0} | all-to-all | bytes 2097152 | tf_op jit(solution)/shard_map/all_to_all | solution.py:794
  78.9 4.7 %collective-permute-start.10 = (f32[8,8,1024]{2,1,0:T(8,128)S(1)}, f32[8,8,1024]{2,1,0:T(8,128)S(1)}, u32[]{:S(2)}, u32[]{:S(2)}) collective-permute-start(f32[8,8,1024]{2,1,0:T(8,128)S(1)} %get-tuple-element.83), channel_id=1, source_target_pairs={{0,120},{1,121},{2,122},{3,123},{4,124},{5,125},{6,126},{7,127},{8... | collective-permute-start | bytes 786440 | tf_op jit(solution)/shard_map/ppermute | solution.py:783
  83.6 3.0 %shard_map.56 = (f32[34,32,256]{2,1,0:T(8,128)S(1)}, f32[34,32,256]{2,1,0:T(8,128)S(1)}, f32[34,32,256]{2,1,0:T(8,128)S(1)}, f32[34,32,256]{2,1,0:T(8,128)S(1)},...) custom-call(f32[64,2,2,8,128]{4,3,2,1,0:T(8,128)S(1)} %all_to_all.5., ...), custom_call_target="tpu_custom_call" | custom-call | flops 1000 | tf_op jit(solution)/shard_map/pallas_call | solution.py:193
  86.6 2.8 %collective-permute-done.9.left = f32[8,8,1024]{2,1,0:T(8,128)S(1)} collective-permute-done((f32[8,8,1024]{2,1,0:T(8,128)S(1)}, f32[8,8,1024]{2,1,0:T(8,128)S(1)}, u32[]{:S(2)}, u32[]{:S(2)}) %collective-permute-start.9) | collective-permute-done | bytes 262176 | tf_op jit(solution)/shard_map/ppermute | solution.py:783
  89.5 1.8 %collective-permute-start.11 = (f32[9,8,1024]{2,1,0:T(8,128)S(1)}, f32[9,8,1024]{2,1,0:T(8,128)S(1)}, u32[]{:S(2)}, u32[]{:S(2)}) collective-permute-start(f32[9,8,1024]{2,1,0:T(8,128)S(1)} %get-tuple-element.86), channel_id=1, source_target_pairs={{0,1},{1,2},{2,3},{3,4},{4,5},{5,6},{6,7},{7,0},{8,9},{9,10},{10,1... | collective-permute-start | bytes 884744 | tf_op jit(solution)/shard_map/ppermute | solution.py:783
  91.3 3.5 %shard_map.58.e2 = f32[6,8,256]{2,1,0:T(8,128)S(1)} custom-call(f32[16,16,128]{2,1,0:T(8,128)S(1)} %get-tuple-element.88.s3, f32[16,16,128]{2,1,0:T(8,128)S(1)} %get-tuple-element.89.c3, f32[34,32,256]{2,1,0:T(8,128)S(1)} %get-tuple-element.90.s, f32[34,32,256]{2,1,0:T(8,128)S(1)} %get-tuple-element.91.c, f32[34,32,256]{2,1,0:T(8,128)S(1)} %get-tuple-element.92.v, ...), custom_call_target="tpu_custom_call" | custom-call | flops 1000 | tf_op jit(solution)/shard_map/pallas_call | solution.py:193
  95.0 2.8 %collective-permute-done.12.nright = f32[9,8,1024]{2,1,0:T(8,128)S(1)} collective-permute-done((f32[9,8,1024]{2,1,0:T(8,128)S(1)}, f32[9,8,1024]{2,1,0:T(8,128)S(1)}, u32[]{:S(2)}, u32[]{:S(2)}) %collective-permute-start.12) | collective-permute-done | bytes 294944 | tf_op jit(solution)/shard_map/ppermute | solution.py:783
  97.8 5.5 %shard_map.59 = (f32[8,16,1024]{2,1,0:T(8,128)}, f32[8,16,1024]{2,1,0:T(8,128)}) custom-call(f32[14,16,1024]{2,1,0:T(8,128)S(1)} %get-tuple-element.50.own_me, f32[14,16,1024]{2,1,0:T(8,128)S(1)} %get-tuple-element.51.own_de, f32[14,16,1024]{2,1,0:T(8,128)S(1)} %get-tuple-element.52.own_fa, f32[14,16,1024]{2,1,0:T(8,128)S(1)} %get-tuple-element.53.own_fz, ...), custom_call_target="tpu_custom_call" | custom-call | flops 30000000 | bytes 12369920 | tf_op jit(solution)/shard_map/pallas_call | solution.py:193
  (25 shorter events, 1.4 us)
Async XLA Ops:
  2.9 18.6 %copy-start = (f32[8,16,1024]{2,1,0:T(8,128)S(1)}, f32[8,16,1024]{2,1,0:T(8,128)}, u32[]{:S(2)}) copy-start(f32[8,16,1024]{2,1,0:T(8,128)} %m.5) | copy-start | bytes 1572868
  2.9 18.6 %copy-start.1 = (f32[8,16,1024]{2,1,0:T(8,128)S(1)}, f32[8,16,1024]{2,1,0:T(8,128)}, u32[]{:S(2)}) copy-start(f32[8,16,1024]{2,1,0:T(8,128)} %p.3) | copy-start | bytes 1572868
  2.9 18.6 %copy-start.2 = (f32[8,16,1024]{2,1,0:T(8,128)S(1)}, f32[8,16,1024]{2,1,0:T(8,128)}, u32[]{:S(2)}) copy-start(f32[8,16,1024]{2,1,0:T(8,128)} %d.3) | copy-start | bytes 1572868
  3.0 18.5 %collective-permute-start = (f32[8,16,1024]{2,1,0:T(8,128)S(1)}, f32[8,16,1024]{2,1,0:T(8,128)S(1)}, u32[]{:S(2)}, u32[]{:S(2)}) collective-permute-start(f32[8,16,1024]{2,1,0:T(8,128)S(1)} %pad_maximum_fusion), channel_id=1, source_target_pairs={{0,8},{1,9},{2,10},{3,11},{4,12},{5,13},{6,14},{7,15},{8,16},{9,17... | collective-permute-start | bytes 1572872 | tf_op jit(solution)/shard_map/ppermute | solution.py:783
  5.6 15.9 %collective-permute-start.1 = (f32[8,16,1024]{2,1,0:T(8,128)S(1)}, f32[8,16,1024]{2,1,0:T(8,128)S(1)}, u32[]{:S(2)}, u32[]{:S(2)}) collective-permute-start(f32[8,16,1024]{2,1,0:T(8,128)S(1)} %pad_maximum_fusion.1), channel_id=1, source_target_pairs={{0,120},{1,121},{2,122},{3,123},{4,124},{5,125},{6,126},{7,127},{8... | collective-permute-start | bytes 1572872 | tf_op jit(solution)/shard_map/ppermute | solution.py:783
  21.7 7.1 %collective-permute-start.2 = (f32[12,8,1024]{2,1,0:T(8,128)S(1)}, f32[12,8,1024]{2,1,0:T(8,128)S(1)}, u32[]{:S(2)}, u32[]{:S(2)}) collective-permute-start(f32[12,8,1024]{2,1,0:T(8,128)S(1)} %get-tuple-element.58), channel_id=1, source_target_pairs={{0,1},{1,2},{2,3},{3,4},{4,5},{5,6},{6,7},{7,0},{8,9},{9,10},{10,1... | collective-permute-start | bytes 1179656 | tf_op jit(solution)/shard_map/ppermute | solution.py:783
  24.1 7.2 %collective-permute-start.3 = (f32[12,8,1024]{2,1,0:T(8,128)S(1)}, f32[12,8,1024]{2,1,0:T(8,128)S(1)}, u32[]{:S(2)}, u32[]{:S(2)}) collective-permute-start(f32[12,8,1024]{2,1,0:T(8,128)S(1)} %get-tuple-element.59), channel_id=1, source_target_pairs={{0,7},{1,0},{2,1},{3,2},{4,3},{5,4},{6,5},{7,6},{8,15},{9,8},{10,9... | collective-permute-start | bytes 1179656 | tf_op jit(solution)/shard_map/ppermute | solution.py:783
  35.5 8.4 %collective-permute-start.4 = (f32[7,8,512]{2,1,0:T(8,128)S(1)}, f32[7,8,512]{2,1,0:T(8,128)S(1)}, u32[]{:S(2)}, u32[]{:S(2)}) collective-permute-start(f32[7,8,512]{2,1,0:T(8,128)S(1)} %get-tuple-element.67), channel_id=1, source_target_pairs={{0,8},{1,9},{2,10},{3,11},{4,12},{5,13},{6,14},{7,15},{8,16},{9,17... | collective-permute-start | bytes 344072 | tf_op jit(solution)/shard_map/ppermute | solution.py:783
  35.6 8.3 %collective-permute-start.5 = (f32[7,8,512]{2,1,0:T(8,128)S(1)}, f32[7,8,512]{2,1,0:T(8,128)S(1)}, u32[]{:S(2)}, u32[]{:S(2)}) collective-permute-start(f32[7,8,512]{2,1,0:T(8,128)S(1)} %get-tuple-element.68), channel_id=1, source_target_pairs={{0,120},{1,121},{2,122},{3,123},{4,124},{5,125},{6,126},{7,127},{8... | collective-permute-start | bytes 344072 | tf_op jit(solution)/shard_map/ppermute | solution.py:783
  43.9 2.5 %collective-permute-start.6 = (f32[10,8,512]{2,1,0:T(8,128)S(1)}, f32[10,8,512]{2,1,0:T(8,128)S(1)}, u32[]{:S(2)}, u32[]{:S(2)}) collective-permute-start(f32[10,8,512]{2,1,0:T(8,128)S(1)} %get-tuple-element.69), channel_id=1, source_target_pairs={{0,1},{1,2},{2,3},{3,4},{4,5},{5,6},{6,7},{7,0},{8,9},{9,10},{10,1... | collective-permute-start | bytes 491528 | tf_op jit(solution)/shard_map/ppermute | solution.py:783
  44.1 5.0 %collective-permute-start.7 = (f32[10,8,512]{2,1,0:T(8,128)S(1)}, f32[10,8,512]{2,1,0:T(8,128)S(1)}, u32[]{:S(2)}, u32[]{:S(2)}) collective-permute-start(f32[10,8,512]{2,1,0:T(8,128)S(1)} %get-tuple-element.70), channel_id=1, source_target_pairs={{0,7},{1,0},{2,1},{3,2},{4,3},{5,4},{6,5},{7,6},{8,15},{9,8},{10,9... | collective-permute-start | bytes 491528 | tf_op jit(solution)/shard_map/ppermute | solution.py:783
  78.8 4.8 %collective-permute-start.8 = (f32[64,2,2,8,128]{4,3,2,1,0:T(8,128)S(1)}, f32[64,2,2,8,128]{4,3,2,1,0:T(8,128)S(1)}, u32[]{:S(2)}, u32[]{:S(2)}) collective-permute-start(f32[64,2,2,8,128]{4,3,2,1,0:T(8,128)S(1)} %all_to_all.5.mine), channel_id=1, source_target_pairs={{0,1},{1,0},{2,3},{3,2},{4,5},{5,4},{6,7},{7,6},{8,9},{9,8},{10,11... | collective-permute-start | bytes 3145736 | tf_op jit(solution)/shard_map/ppermute | solution.py:788
  78.8 10.7 %collective-permute-start.9 = (f32[8,8,1024]{2,1,0:T(8,128)S(1)}, f32[8,8,1024]{2,1,0:T(8,128)S(1)}, u32[]{:S(2)}, u32[]{:S(2)}) collective-permute-start(f32[8,8,1024]{2,1,0:T(8,128)S(1)} %get-tuple-element.82), channel_id=1, source_target_pairs={{0,8},{1,9},{2,10},{3,11},{4,12},{5,13},{6,14},{7,15},{8,16},{9,17... | collective-permute-start | bytes 786440 | tf_op jit(solution)/shard_map/ppermute | solution.py:783
  78.9 10.5 %collective-permute-start.10 = (f32[8,8,1024]{2,1,0:T(8,128)S(1)}, f32[8,8,1024]{2,1,0:T(8,128)S(1)}, u32[]{:S(2)}, u32[]{:S(2)}) collective-permute-start(f32[8,8,1024]{2,1,0:T(8,128)S(1)} %get-tuple-element.83), channel_id=1, source_target_pairs={{0,120},{1,121},{2,122},{3,123},{4,124},{5,125},{6,126},{7,127},{8... | collective-permute-start | bytes 786440 | tf_op jit(solution)/shard_map/ppermute | solution.py:783
  89.5 5.5 %collective-permute-start.11 = (f32[9,8,1024]{2,1,0:T(8,128)S(1)}, f32[9,8,1024]{2,1,0:T(8,128)S(1)}, u32[]{:S(2)}, u32[]{:S(2)}) collective-permute-start(f32[9,8,1024]{2,1,0:T(8,128)S(1)} %get-tuple-element.86), channel_id=1, source_target_pairs={{0,1},{1,2},{2,3},{3,4},{4,5},{5,6},{6,7},{7,0},{8,9},{9,10},{10,1... | collective-permute-start | bytes 884744 | tf_op jit(solution)/shard_map/ppermute | solution.py:783
  91.3 6.4 %collective-permute-start.12 = (f32[9,8,1024]{2,1,0:T(8,128)S(1)}, f32[9,8,1024]{2,1,0:T(8,128)S(1)}, u32[]{:S(2)}, u32[]{:S(2)}) collective-permute-start(f32[9,8,1024]{2,1,0:T(8,128)S(1)} %get-tuple-element.87), channel_id=1, source_target_pairs={{0,7},{1,0},{2,1},{3,2},{4,3},{5,4},{6,5},{7,6},{8,15},{9,8},{10,9... | collective-permute-start | bytes 884744 | tf_op jit(solution)/shard_map/ppermute | solution.py:783

commit v4 on v3

--- a/solution.py
+++ b/solution.py
@@ -211,27 +211,29 @@
         c2[i] = 0.125 * (even + pltpu.roll(odd, 4, 0))
 
 
-def pack_zero(p, d, m, left, right, to_left, to_right):
-    _, _, _, (low, high, _, _) = scalars()
+def columns_zero(vp, vm, vd, side):
     at = iota((8, 1024), 0)
-    for r in range(1, 13):
-        a = r - 3
+    if side == 0:
+        vm, vd = pltpu.roll(vm, 3, 0), pltpu.roll(vd, 6, 0)
+        return jnp.where(at < 3, vp, jnp.where(at < 6, vm, vd))
+    vm, vd = pltpu.roll(vm, 5, 0), pltpu.roll(vd, 2, 0)
+    return jnp.where(at >= 5, vp, jnp.where(at >= 2, vm, vd))
+
+
+def pack_zero_own(p, d, m, to_left, to_right):
+    for a in range(8):
         for side, out in ((0, to_left), (1, to_right)):
             tile = slice(8 * side, 8 * side + 8)
-            if a < 0:
-                vp, vm = left[r, tile] * low, left[3 + r, tile] * low
-                vd = left[5 + r, tile] * low if r > 0 else jnp.zeros_like(vp)
-            elif a < 8:
-                vp, vm, vd = p[a, tile], m[a, tile], d[a, tile]
-            else:
-                vp, vm = right[a - 8, tile] * high, right[a - 5, tile] * high
-                vd = right[a - 2, tile] * high if a < 10 else jnp.zeros_like(vp)
-            if side == 0:
-                vm, vd = pltpu.roll(vm, 3, 0), pltpu.roll(vd, 6, 0)
-                out[r - 1] = jnp.where(at < 3, vp, jnp.where(at < 6, vm, vd))
-            else:
-                vm, vd = pltpu.roll(vm, 5, 0), pltpu.roll(vd, 2, 0)
-                out[r - 1] = jnp.where(at >= 5, vp, jnp.where(at >= 2, vm, vd))
+            out[a] = columns_zero(p[a, tile], m[a, tile], d[a, tile], side)
+
+
+def pack_zero_edge(left, right, to_left, to_right):
+    _, _, _, (low, high, _, _) = scalars()
+    for side, out in ((0, to_left), (1, to_right)):
+        tile = slice(8 * side, 8 * side + 8)
+        for i in range(2):
+            out[i] = columns_zero(left[1 + i, tile], left[4 + i, tile], left[6 + i, tile], side) * low
+            out[2 + i] = columns_zero(right[i, tile], right[3 + i, tile], right[6 + i, tile], side) * high
 
 
 def faces(c, rows, fa, fb, fz, w, step):
@@ -302,7 +304,7 @@
 
 
 def level_zero(
-    own_v, own_me, own_de, own_fa, own_fz, own_diagonal, own_left_over, c1, nleft, nright,
+    own_v, own_me, own_de, own_fa, own_fz, own_diagonal, own_left_over, c1, nleft, nright, nleft_edge, nright_edge,
     field, s1, up, down, me, de, fa, fz, fb, w, v, u, beside, diagonal, left_over,
 ):
     _, _, _, (_, _, nlow, nhigh) = scalars()
@@ -310,7 +312,11 @@
     for r in (0, 13):
         beside[r] = me[r] = de[r] = jnp.zeros((8, 1024), F32)
     for r in range(1, 13):
-        x, y = nright[r - 1] * nhigh, nleft[r - 1] * nlow
+        if 3 <= r < 11:
+            x, y = nright[r - 3] * nhigh, nleft[r - 3] * nlow
+        else:
+            e = r - 1 if r < 3 else r - 9
+            x, y = nright_edge[e] * nhigh, nleft_edge[e] * nlow
         beside[r] = jnp.where(at < 3, x, jnp.where(at >= 5, y, 0.0))
         x3, y3 = pltpu.roll(x, 5, 0), pltpu.roll(y, 3, 0)
         me[r] = jnp.where(at < 3, x3, jnp.where(at >= 5, y3, 0.0))
@@ -407,35 +413,38 @@
         down[6 + r] = both
 
 
-def pack_up(f0, f1, left, right, to_left, to_right):
+def two_rows(x, y, side):
+    at = iota((8, 1024), 0)
+    return jnp.where(at < 4 if side == 0 else at >= 4, x, pltpu.roll(y, 4, 0))
+
+
+def pack_up_own(f0, f1, to_left, to_right):
+    for side, out in ((0, to_left), (1, to_right)):
+        tile = slice(8 * side, 8 * side + 8)
+        for t in range(4):
+            out[t] = two_rows(f0[2 * t, tile], f0[2 * t + 1, tile], side)
+        pair = [jnp.concatenate([f1[2 * k], f1[2 * k + 1]], axis=1) for k in range(2)]
+        out[4] = two_rows(pair[0], pair[1], side)
+
+
+def pack_up_edge(left, right, to_left, to_right):
     _, _, _, (low, high, _, _) = scalars()
-    at = iota((8, 1024), 0)
-
-    def fine(r, side):
-        if r < 3:
-            return left[2 * r + side] * low
-        if r < 11:
-            return f0[r - 3, 8 * side : 8 * side + 8]
-        return right[2 * (r - 11) + side] * high
-
-    def pair(r):
-        if r < 2:
-            return left[6 + r] * low
-        if r < 4:
-            return jnp.concatenate([f1[2 * r - 4], f1[2 * r - 3]], axis=1)
-        return right[2 + r] * high
-
-    for t in range(6):
-        to_left[t] = jnp.where(at < 4, fine(2 * t + 1, 0), pltpu.roll(fine(2 * t + 2, 0), 4, 0))
-        to_right[t] = jnp.where(at >= 4, fine(2 * t + 1, 1), pltpu.roll(fine(2 * t + 2, 1), 4, 0))
-    for t in range(3):
-        to_left[6 + t] = jnp.where(at < 4, pair(2 * t), pltpu.roll(pair(2 * t + 1), 4, 0))
-        to_right[6 + t] = jnp.where(at >= 4, pair(2 * t), pltpu.roll(pair(2 * t + 1), 4, 0))
+    for side, out in ((0, to_left), (1, to_right)):
+        out[0] = two_rows(left[2 + side], left[4 + side], side) * low
+        out[1] = two_rows(right[side], right[2 + side], side) * high
+        out[2] = two_rows(left[6], left[7], side) * low
+        out[3] = two_rows(right[6], right[7], side) * high
+
+
+def tile_up(own, edge, t):
+    if t in (0, 5, 6, 8):
+        return edge[(0, 5, 6, 8).index(t)]
+    return own[4 if t == 7 else t - 1]
 
 
 def level_up(
     own_me, own_de, own_fa, own_fz, me, de, fa, fz, fb, w, se, ce, fa1, fb1, fz1, w1,
-    f0, f1, left, right, nleft, nright, e2,
+    f0, f1, left, right, nleft, nright, nleft_edge, nright_edge, e2,
     out, res, v, u, v1, u1, kept, sent,
 ):
     _, _, _, (low, high, nlow, nhigh) = scalars()
@@ -448,8 +457,9 @@
             f = f1[r - 4]
         else:
             f = right[2 + r // 2][:, 512 * (r % 2) : 512 * (r % 2) + 512] * high
-        x = nright[6 + r // 4][:, 512 * (r % 2) : 512 * (r % 2) + 512] * nhigh
-        y = nleft[6 + r // 4][:, 512 * (r % 2) : 512 * (r % 2) + 512] * nlow
+        half_tile = slice(512 * (r % 2), 512 * (r % 2) + 512)
+        x = tile_up(nright, nright_edge, 6 + r // 4)[:, half_tile] * nhigh
+        y = tile_up(nleft, nleft_edge, 6 + r // 4)[:, half_tile] * nlow
         if r % 4 > 1:
             x, y = pltpu.roll(x, 4, 0), pltpu.roll(y, 4, 0)
         g = jnp.where(at < 4, x, y)
@@ -471,7 +481,8 @@
         if r in (0, 13):
             f.append(jnp.zeros((8, 1024), F32))
         else:
-            x, y = nright[(r - 1) // 2] * nhigh, nleft[(r - 1) // 2] * nlow
+            t = (r - 1) // 2
+            x, y = tile_up(nright, nright_edge, t) * nhigh, tile_up(nleft, nleft_edge, t) * nlow
             if r % 2 == 0:
                 x, y = pltpu.roll(x, 4, 0), pltpu.roll(y, 4, 0)
             f.append(jnp.where(zero < 3, x, jnp.where(zero >= 5, y, 0.0)))
@@ -799,15 +810,18 @@
     down = jnp.concatenate([p[0:3], m[0:3], d[0:2]], axis=0)
     left, right = moved(up, 1, 0), moved(down, -1, 0)
     c1, c2 = call(coarse_coefficients, [(4, 8, 512), (2, 8, 128)], [], m)
-    to_left, to_right = call(pack_zero, [(12, 8, 1024)] * 2, [], p, d, m, left, right)
+    to_left, to_right = call(pack_zero_own, [(8, 8, 1024)] * 2, [], p, d, m)
     nleft, nright = moved(to_right, 0, 1), moved(to_left, 0, -1)
+    left, right, nleft, nright = lax.optimization_barrier((left, right, nleft, nright))
+    to_left, to_right = call(pack_zero_edge, [(4, 8, 1024)] * 2, [], left, right)
+    nleft_edge, nright_edge = moved(to_right, 0, 1), moved(to_left, 0, -1)
     big, own, halo = (14, 24, 1024), (14, 16, 1024), (14, 8, 1024)
     alone = call(level_zero_own, [own] * 7, [], p, d, m, left, right, flops=20_000_000)
     f0, s1, up, down, *zero = call(
         level_zero,
         [(8, 16, 1024), (4, 8, 512)] + [(7, 8, 512)] * 2 + [halo] * 4 + [big] * 2,
         [big] * 2 + [halo] * 3,
-        *alone, c1, nleft, nright,
+        *alone, c1, nleft, nright, nleft_edge, nright_edge,
         flops=30_000_000,
     )
     zero = [*alone[1:5], *zero]
@@ -827,15 +841,17 @@
     other = other_core(mine)
     whole, small = (34, 32, 256), (16, 16, 128)
     *two, s3, c3 = call(level_two, [whole] * 8 + [small] * 2, [whole], mine, other, flops=1000)
-    s3, hleft, hright = lax.optimization_barrier((s3, hleft, hright))
-    to_left, to_right = call(pack_up, [(9, 8, 1024)] * 2, [], f0, f1, hleft, hright)
+    to_left, to_right = call(pack_up_own, [(5, 8, 1024)] * 2, [], f0, f1)
     nhleft, nhright = moved(to_right, 0, 1), moved(to_left, 0, -1)
+    s3, hleft, hright, nhleft, nhright = lax.optimization_barrier((s3, hleft, hright, nhleft, nhright))
+    to_left, to_right = call(pack_up_edge, [(4, 8, 1024)] * 2, [], hleft, hright)
+    edges = [moved(to_right, 0, 1), moved(to_left, 0, -1)]
     (e2,) = call(coarse_levels, [(6, 8, 256)], [small] + [whole] * 2, s3, c3, *two, flops=1000)
     return call(
         level_up,
         [(8, 16, 1024)] * 2,
         [big] * 2 + [mid] * 2 + [(8, 16, 1024)],
-        *zero, *one, f0, f1, hleft, hright, nhleft, nhright, e2,
+        *zero, *one, f0, f1, hleft, hright, nhleft, nhright, *edges, e2,
         flops=30_000_000,
         copies=3,
     )

time: 103 us -> 98.8 us (0.959)
  waiting for transfers between devices: 30.1 us -> 22.4 us
  starting transfers between devices: 21.7 us -> 24.7 us
    ppermute x12 -> x16, waiting for transfers between devices: 30.1 us -> 22.4 us  [moved(): return lax.ppermute(x, AX, pairs)]
    ppermute x12 -> x16, starting transfers between devices: 21.7 us -> 24.7 us  [moved(): return lax.ppermute(x, AX, pairs)]
    pallas_call x10 -> x12, Pallas kernels: 19.9 us -> 19.9 us  [call(): pl.pallas_call(kernel, out_shape=[jax.ShapeDtypeStruct(s, F32) for s in o...]
  transfers between devices with their start and end apart: 13 -> 17, of which waited for: 9 -> 9; matrix products, arithmetic and copies ran while one was open for 0% -> 0% of each run, Pallas kernels for 9% -> 9%
where the time goes in v4:
time: 98.8 us; the launch traced here: 98.6 us
  blocking collectives  28.4 us (29%)
  starting transfers between devices  24.7 us (25%)
  waiting for transfers between devices  22.4 us (23%)
  Pallas kernels  19.9 us (20%)
  local copies, waits for them, and re-layouts  2.41 us (2%)
    all_to_all x1, blocking collectives, gathered(): lax.all_to_all(jnp.broadcast_to(both[None], (chips,) + both.shape), ('wid...  28.4 us
    ppermute x16, starting transfers between devices, moved(): return lax.ppermute(x, AX, pairs)  24.7 us
    ppermute x16, waiting for transfers between devices, moved(): return lax.ppermute(x, AX, pairs)  22.4 us
    pallas_call x12, Pallas kernels, call(): pl.pallas_call(kernel, out_shape=[jax.ShapeDtypeStruct(s, F32) for s in o...  19.9 us
    slice x2, local copies, waits for them, and re-layouts, per_device(): down = jnp.concatenate([p[0:3], m[0:3], d[0:2]], axis=0)  2.28 us
  transfers between devices with their start and end apart: 17, of which 9 were waited for; matrix products, arithmetic and copies ran while one was open for 0% of the time, Pallas kernels for 9%

profile of v4, /device:TPU:1, one launch (start us, length us, event | category | flops | bytes accessed | tf_op | source)
XLA Modules:
  0.0 98.6 jit_solution(14083884522411862266)
XLA Ops:
  1.6 1.3 %fusion = (f32[3,16,1024]{2,1,0:T(8,128)S(1)}, f32[3,16,1024]{2,1,0:T(8,128)S(1)}, f32[3,16,1024]{2,1,0:T(8,128)S(1)}, f32[3,16,1024]{2,1,0:T(8,128)S(1)}) fusion(f32[8,16,1024]{2,1,0:T(8,128)} %p.3, f32[8,16,1024]{2,1,0:T(8,128)} %m.5), kind=kLoop, calls=%fused_computation.3 | loop fusion | bytes 1572864 | tf_op jit(solution)/shard_map/slice | solution.py:810
  3.0 2.5 %collective-permute-start = (f32[8,16,1024]{2,1,0:T(8,128)S(1)}, f32[8,16,1024]{2,1,0:T(8,128)S(1)}, u32[]{:S(2)}, u32[]{:S(2)}) collective-permute-start(f32[8,16,1024]{2,1,0:T(8,128)S(1)} %pad_maximum_fusion), channel_id=1, source_target_pairs={{0,8},{1,9},{2,10},{3,11},{4,12},{5,13},{6,14},{7,15},{8,16},{9,17... | collective-permute-start | bytes 1572872 | tf_op jit(solution)/shard_map/ppermute | solution.py:794
  5.6 4.4 %collective-permute-start.1 = (f32[8,16,1024]{2,1,0:T(8,128)S(1)}, f32[8,16,1024]{2,1,0:T(8,128)S(1)}, u32[]{:S(2)}, u32[]{:S(2)}) collective-permute-start(f32[8,16,1024]{2,1,0:T(8,128)S(1)} %pad_maximum_fusion.1), channel_id=1, source_target_pairs={{0,120},{1,121},{2,122},{3,123},{4,124},{5,125},{6,126},{7,127},{8... | collective-permute-start | bytes 1572872 | tf_op jit(solution)/shard_map/ppermute | solution.py:794
  10.1 2.1 %collective-permute-start.2 = (f32[8,8,1024]{2,1,0:T(8,128)S(1)}, f32[8,8,1024]{2,1,0:T(8,128)S(1)}, u32[]{:S(2)}, u32[]{:S(2)}) collective-permute-start(f32[8,8,1024]{2,1,0:T(8,128)S(1)} %get-tuple-element.60), channel_id=1, source_target_pairs={{0,1},{1,2},{2,3},{3,4},{4,5},{5,6},{6,7},{7,0},{8,9},{9,10},{10,1... | collective-permute-start | bytes 786440 | tf_op jit(solution)/shard_map/ppermute | solution.py:794
  12.2 3.3 %collective-permute-done.2.nleft = f32[8,8,1024]{2,1,0:T(8,128)S(1)} collective-permute-done((f32[8,8,1024]{2,1,0:T(8,128)S(1)}, f32[8,8,1024]{2,1,0:T(8,128)S(1)}, u32[]{:S(2)}, u32[]{:S(2)}) %collective-permute-start.2) | collective-permute-done | bytes 262176 | tf_op jit(solution)/shard_map/ppermute | solution.py:794
  15.5 2.8 %collective-permute-done.3.nright = f32[8,8,1024]{2,1,0:T(8,128)S(1)} collective-permute-done((f32[8,8,1024]{2,1,0:T(8,128)S(1)}, f32[8,8,1024]{2,1,0:T(8,128)S(1)}, u32[]{:S(2)}, u32[]{:S(2)}) %collective-permute-start.3) | collective-permute-done | bytes 262176 | tf_op jit(solution)/shard_map/ppermute | solution.py:794
  18.3 3.2 %collective-permute-done.left = f32[8,16,1024]{2,1,0:T(8,128)S(1)} collective-permute-done((f32[8,16,1024]{2,1,0:T(8,128)S(1)}, f32[8,16,1024]{2,1,0:T(8,128)S(1)}, u32[]{:S(2)}, u32[]{:S(2)}) %collective-permute-start) | collective-permute-done | bytes 524320 | tf_op jit(solution)/shard_map/ppermute | solution.py:794
  21.6 2.4 %collective-permute-start.4 = (f32[4,8,1024]{2,1,0:T(8,128)S(1)}, f32[4,8,1024]{2,1,0:T(8,128)S(1)}, u32[]{:S(2)}, u32[]{:S(2)}) collective-permute-start(f32[4,8,1024]{2,1,0:T(8,128)S(1)} %get-tuple-element.74), channel_id=1, source_target_pairs={{0,1},{1,2},{2,3},{3,4},{4,5},{5,6},{6,7},{7,0},{8,9},{9,10},{10,1... | collective-permute-start | bytes 393224 | tf_op jit(solution)/shard_map/ppermute | solution.py:794
  24.3 1.9 %shard_map.51 = (f32[14,16,1024]{2,1,0:T(8,128)S(1)}, f32[14,16,1024]{2,1,0:T(8,128)S(1)}, f32[14,16,1024]{2,1,0:T(8,128)S(1)}, f32[14,16,1024]{2,1,0:T(8,128)S(...) custom-call(f32[8,16,1024]{2,1,0:T(8,128)S(1)} %copy-done.1, ...), custom_call_target="tpu_custom_call" | custom-call | flops 20000000 | bytes 2621440 | tf_op jit(solution)/shard_map/pallas_call | solution.py:193
  26.3 2.1 %collective-permute-done.5.nright_edge = f32[4,8,1024]{2,1,0:T(8,128)S(1)} collective-permute-done((f32[4,8,1024]{2,1,0:T(8,128)S(1)}, f32[4,8,1024]{2,1,0:T(8,128)S(1)}, u32[]{:S(2)}, u32[]{:S(2)}) %collective-permute-start.5) | collective-permute-done | bytes 131104 | tf_op jit(solution)/shard_map/ppermute | solution.py:794
  28.4 4.2 %shard_map.54 = (f32[8,16,1024]{2,1,0:T(8,128)S(1)}, f32[4,8,512]{2,1,0:T(8,128)S(1)}, f32[7,8,512]{2,1,0:T(8,128)S(1)}, f32[7,8,512]{2,1,0:T(8,128)S(1)}, f32[1...) custom-call(f32[14,16,1024]{2,1,0:T(8,128)S(1)} %get-tuple-element.6, ...), custom_call_target="tpu_custom_call" | custom-call | flops 30000000 | bytes 7274496 | tf_op jit(solution)/shard_map/pallas_call | solution.py:193
  32.6 5.0 %collective-permute-start.7 = (f32[7,8,512]{2,1,0:T(8,128)S(1)}, f32[7,8,512]{2,1,0:T(8,128)S(1)}, u32[]{:S(2)}, u32[]{:S(2)}) collective-permute-start(f32[7,8,512]{2,1,0:T(8,128)S(1)} %get-tuple-element.84), channel_id=1, source_target_pairs={{0,120},{1,121},{2,122},{3,123},{4,124},{5,125},{6,126},{7,127},{8... | collective-permute-start | bytes 344072 | tf_op jit(solution)/shard_map/ppermute | solution.py:794
  37.6 3.3 %collective-permute-done.6.left = f32[7,8,512]{2,1,0:T(8,128)S(1)} collective-permute-done((f32[7,8,512]{2,1,0:T(8,128)S(1)}, f32[7,8,512]{2,1,0:T(8,128)S(1)}, u32[]{:S(2)}, u32[]{:S(2)}) %collective-permute-start.6) | collective-permute-done | bytes 114720 | tf_op jit(solution)/shard_map/ppermute | solution.py:794
  41.7 1.8 %collective-permute-done.8.nleft = f32[10,8,512]{2,1,0:T(8,128)S(1)} collective-permute-done((f32[10,8,512]{2,1,0:T(8,128)S(1)}, f32[10,8,512]{2,1,0:T(8,128)S(1)}, u32[]{:S(2)}, u32[]{:S(2)}) %collective-permute-start.8) | collective-permute-done | bytes 163872 | tf_op jit(solution)/shard_map/ppermute | solution.py:794
  43.5 2.8 %collective-permute-done.9.nright = f32[10,8,512]{2,1,0:T(8,128)S(1)} collective-permute-done((f32[10,8,512]{2,1,0:T(8,128)S(1)}, f32[10,8,512]{2,1,0:T(8,128)S(1)}, u32[]{:S(2)}, u32[]{:S(2)}) %collective-permute-start.9) | collective-permute-done | bytes 163872 | tf_op jit(solution)/shard_map/ppermute | solution.py:794
  46.2 1.2 %shard_map.56 = (f32[4,8,512]{2,1,0:T(8,128)S(1)}, f32[2,8,128]{2,1,0:T(8,128)S(1)}, f32[8,8,1024]{2,1,0:T(8,128)S(1)}, f32[8,8,1024]{2,1,0:T(8,128)S(1)}, f32[1...) custom-call(f32[4,8,512]{2,1,0:T(8,128)S(1)} %get-tuple-element.82.s, ...), custom_call_target="tpu_custom_call" | custom-call | flops 10000000 | bytes 1212416 | tf_op jit(solution)/shard_map/pallas_call | solution.py:193
  47.5 28.4 %all_to_all.5.mine = f32[64,2,2,8,128]{4,3,2,1,0:T(8,128)S(1)} all-to-all(f32[64,2,2,8,128]{4,3,2,1,0:T(8,128)S(1)} %broadcast_in_dim.2), channel_id=1, replica_groups=mesh['wide'=16,'ny'=4,'core'=2] {'wide','ny'}, dimensions={0} | all-to-all | bytes 2097152 | tf_op jit(solution)/shard_map/all_to_all | solution.py:805
  76.1 4.7 %collective-permute-start.12 = (f32[8,8,1024]{2,1,0:T(8,128)S(1)}, f32[8,8,1024]{2,1,0:T(8,128)S(1)}, u32[]{:S(2)}, u32[]{:S(2)}) collective-permute-start(f32[8,8,1024]{2,1,0:T(8,128)S(1)} %get-tuple-element.99), channel_id=1, source_target_pairs={{0,120},{1,121},{2,122},{3,123},{4,124},{5,125},{6,126},{7,127},{8... | collective-permute-start | bytes 786440 | tf_op jit(solution)/shard_map/ppermute | solution.py:794
  80.8 1.5 %collective-permute-start.13 = (f32[5,8,1024]{2,1,0:T(8,128)S(1)}, f32[5,8,1024]{2,1,0:T(8,128)S(1)}, u32[]{:S(2)}, u32[]{:S(2)}) collective-permute-start(f32[5,8,1024]{2,1,0:T(8,128)S(1)} %get-tuple-element.100), channel_id=1, source_target_pairs={{0,1},{1,2},{2,3},{3,4},{4,5},{5,6},{6,7},{7,0},{8,9},{9,10},{10,1... | collective-permute-start | bytes 491528 | tf_op jit(solution)/shard_map/ppermute | solution.py:794
  82.2 3.0 %shard_map.57 = (f32[34,32,256]{2,1,0:T(8,128)S(1)}, f32[34,32,256]{2,1,0:T(8,128)S(1)}, f32[34,32,256]{2,1,0:T(8,128)S(1)}, f32[34,32,256]{2,1,0:T(8,128)S(1)},...) custom-call(f32[64,2,2,8,128]{4,3,2,1,0:T(8,128)S(1)} %all_to_all.5., ...), custom_call_target="tpu_custom_call" | custom-call | flops 1000 | tf_op jit(solution)/shard_map/pallas_call | solution.py:193
  85.3 2.0 %collective-permute-done.14.nright = f32[5,8,1024]{2,1,0:T(8,128)S(1)} collective-permute-done((f32[5,8,1024]{2,1,0:T(8,128)S(1)}, f32[5,8,1024]{2,1,0:T(8,128)S(1)}, u32[]{:S(2)}, u32[]{:S(2)}) %collective-permute-start.14) | collective-permute-done | bytes 163872 | tf_op jit(solution)/shard_map/ppermute | solution.py:794
  88.4 3.5 %shard_map.60.e2 = f32[6,8,256]{2,1,0:T(8,128)S(1)} custom-call(f32[16,16,128]{2,1,0:T(8,128)S(1)} %get-tuple-element.108.s3, f32[16,16,128]{2,1,0:T(8,128)S(1)} %get-tuple-element.109.c3, f32[34,32,256]{2,1,0:T(8,128)S(1)} %get-tuple-element.110.s, f32[34,32,256]{2,1,0:T(8,128)S(1)} %get-tuple-element.111.c, f32[34,32,256]{2,1,0:T(8,128)S(1)} %get-tuple-element.112.v, ...), custom_call_target="tpu_custom_call" | custom-call | flops 1000 | tf_op jit(solution)/shard_map/pallas_call | solution.py:193
  92.0 1.2 %collective-permute-done.16.nright_edge = f32[4,8,1024]{2,1,0:T(8,128)S(1)} collective-permute-done((f32[4,8,1024]{2,1,0:T(8,128)S(1)}, f32[4,8,1024]{2,1,0:T(8,128)S(1)}, u32[]{:S(2)}, u32[]{:S(2)}) %collective-permute-start.16) | collective-permute-done | bytes 131104 | tf_op jit(solution)/shard_map/ppermute | solution.py:794
  93.1 5.5 %shard_map.61 = (f32[8,16,1024]{2,1,0:T(8,128)}, f32[8,16,1024]{2,1,0:T(8,128)}) custom-call(f32[14,16,1024]{2,1,0:T(8,128)S(1)} %get-tuple-element.64.own_me, f32[14,16,1024]{2,1,0:T(8,128)S(1)} %get-tuple-element.65.own_de, f32[14,16,1024]{2,1,0:T(8,128)S(1)} %get-tuple-element.66.own_fa, f32[14,16,1024]{2,1,0:T(8,128)S(1)} %get-tuple-element.67.own_fz, ...), custom_call_target="tpu_custom_call" | custom-call | flops 30000000 | bytes 12369920 | tf_op jit(solution)/shard_map/pallas_call | solution.py:193
  (35 shorter events, 3.8 us)
Async XLA Ops:
  2.9 7.1 %copy-start = (f32[8,16,1024]{2,1,0:T(8,128)S(1)}, f32[8,16,1024]{2,1,0:T(8,128)}, u32[]{:S(2)}) copy-start(f32[8,16,1024]{2,1,0:T(8,128)} %m.5) | copy-start | bytes 1572868
  2.9 7.1 %copy-start.1 = (f32[8,16,1024]{2,1,0:T(8,128)S(1)}, f32[8,16,1024]{2,1,0:T(8,128)}, u32[]{:S(2)}) copy-start(f32[8,16,1024]{2,1,0:T(8,128)} %p.3) | copy-start | bytes 1572868
  2.9 7.1 %copy-start.2 = (f32[8,16,1024]{2,1,0:T(8,128)S(1)}, f32[8,16,1024]{2,1,0:T(8,128)}, u32[]{:S(2)}) copy-start(f32[8,16,1024]{2,1,0:T(8,128)} %d.3) | copy-start | bytes 1572868
  3.0 18.5 %collective-permute-start = (f32[8,16,1024]{2,1,0:T(8,128)S(1)}, f32[8,16,1024]{2,1,0:T(8,128)S(1)}, u32[]{:S(2)}, u32[]{:S(2)}) collective-permute-start(f32[8,16,1024]{2,1,0:T(8,128)S(1)} %pad_maximum_fusion), channel_id=1, source_target_pairs={{0,8},{1,9},{2,10},{3,11},{4,12},{5,13},{6,14},{7,15},{8,16},{9,17... | collective-permute-start | bytes 1572872 | tf_op jit(solution)/shard_map/ppermute | solution.py:794
  5.6 15.9 %collective-permute-start.1 = (f32[8,16,1024]{2,1,0:T(8,128)S(1)}, f32[8,16,1024]{2,1,0:T(8,128)S(1)}, u32[]{:S(2)}, u32[]{:S(2)}) collective-permute-start(f32[8,16,1024]{2,1,0:T(8,128)S(1)} %pad_maximum_fusion.1), channel_id=1, source_target_pairs={{0,120},{1,121},{2,122},{3,123},{4,124},{5,125},{6,126},{7,127},{8... | collective-permute-start | bytes 1572872 | tf_op jit(solution)/shard_map/ppermute | solution.py:794
  10.1 5.5 %collective-permute-start.2 = (f32[8,8,1024]{2,1,0:T(8,128)S(1)}, f32[8,8,1024]{2,1,0:T(8,128)S(1)}, u32[]{:S(2)}, u32[]{:S(2)}) collective-permute-start(f32[8,8,1024]{2,1,0:T(8,128)S(1)} %get-tuple-element.60), channel_id=1, source_target_pairs={{0,1},{1,2},{2,3},{3,4},{4,5},{5,6},{6,7},{7,0},{8,9},{9,10},{10,1... | collective-permute-start | bytes 786440 | tf_op jit(solution)/shard_map/ppermute | solution.py:794
  12.2 6.1 %collective-permute-start.3 = (f32[8,8,1024]{2,1,0:T(8,128)S(1)}, f32[8,8,1024]{2,1,0:T(8,128)S(1)}, u32[]{:S(2)}, u32[]{:S(2)}) collective-permute-start(f32[8,8,1024]{2,1,0:T(8,128)S(1)} %get-tuple-element.61), channel_id=1, source_target_pairs={{0,7},{1,0},{2,1},{3,2},{4,3},{5,4},{6,5},{7,6},{8,15},{9,8},{10,9... | collective-permute-start | bytes 786440 | tf_op jit(solution)/shard_map/ppermute | solution.py:794
  21.6 4.7 %collective-permute-start.4 = (f32[4,8,1024]{2,1,0:T(8,128)S(1)}, f32[4,8,1024]{2,1,0:T(8,128)S(1)}, u32[]{:S(2)}, u32[]{:S(2)}) collective-permute-start(f32[4,8,1024]{2,1,0:T(8,128)S(1)} %get-tuple-element.74), channel_id=1, source_target_pairs={{0,1},{1,2},{2,3},{3,4},{4,5},{5,6},{6,7},{7,0},{8,9},{9,10},{10,1... | collective-permute-start | bytes 393224 | tf_op jit(solution)/shard_map/ppermute | solution.py:794
  24.0 4.4 %collective-permute-start.5 = (f32[4,8,1024]{2,1,0:T(8,128)S(1)}, f32[4,8,1024]{2,1,0:T(8,128)S(1)}, u32[]{:S(2)}, u32[]{:S(2)}) collective-permute-start(f32[4,8,1024]{2,1,0:T(8,128)S(1)} %get-tuple-element.75), channel_id=1, source_target_pairs={{0,7},{1,0},{2,1},{3,2},{4,3},{5,4},{6,5},{7,6},{8,15},{9,8},{10,9... | collective-permute-start | bytes 393224 | tf_op jit(solution)/shard_map/ppermute | solution.py:794
  32.5 8.4 %collective-permute-start.6 = (f32[7,8,512]{2,1,0:T(8,128)S(1)}, f32[7,8,512]{2,1,0:T(8,128)S(1)}, u32[]{:S(2)}, u32[]{:S(2)}) collective-permute-start(f32[7,8,512]{2,1,0:T(8,128)S(1)} %get-tuple-element.83), channel_id=1, source_target_pairs={{0,8},{1,9},{2,10},{3,11},{4,12},{5,13},{6,14},{7,15},{8,16},{9,17... | collective-permute-start | bytes 344072 | tf_op jit(solution)/shard_map/ppermute | solution.py:794
  32.6 8.3 %collective-permute-start.7 = (f32[7,8,512]{2,1,0:T(8,128)S(1)}, f32[7,8,512]{2,1,0:T(8,128)S(1)}, u32[]{:S(2)}, u32[]{:S(2)}) collective-permute-start(f32[7,8,512]{2,1,0:T(8,128)S(1)} %get-tuple-element.84), channel_id=1, source_target_pairs={{0,120},{1,121},{2,122},{3,123},{4,124},{5,125},{6,126},{7,127},{8... | collective-permute-start | bytes 344072 | tf_op jit(solution)/shard_map/ppermute | solution.py:794
  41.0 2.5 %collective-permute-start.8 = (f32[10,8,512]{2,1,0:T(8,128)S(1)}, f32[10,8,512]{2,1,0:T(8,128)S(1)}, u32[]{:S(2)}, u32[]{:S(2)}) collective-permute-start(f32[10,8,512]{2,1,0:T(8,128)S(1)} %get-tuple-element.85), channel_id=1, source_target_pairs={{0,1},{1,2},{2,3},{3,4},{4,5},{5,6},{6,7},{7,0},{8,9},{9,10},{10,1... | collective-permute-start | bytes 491528 | tf_op jit(solution)/shard_map/ppermute | solution.py:794
  41.2 5.0 %collective-permute-start.9 = (f32[10,8,512]{2,1,0:T(8,128)S(1)}, f32[10,8,512]{2,1,0:T(8,128)S(1)}, u32[]{:S(2)}, u32[]{:S(2)}) collective-permute-start(f32[10,8,512]{2,1,0:T(8,128)S(1)} %get-tuple-element.86), channel_id=1, source_target_pairs={{0,7},{1,0},{2,1},{3,2},{4,3},{5,4},{6,5},{7,6},{8,15},{9,8},{10,9... | collective-permute-start | bytes 491528 | tf_op jit(solution)/shard_map/ppermute | solution.py:794
  75.9 6.3 %collective-permute-start.10 = (f32[64,2,2,8,128]{4,3,2,1,0:T(8,128)S(1)}, f32[64,2,2,8,128]{4,3,2,1,0:T(8,128)S(1)}, u32[]{:S(2)}, u32[]{:S(2)}) collective-permute-start(f32[64,2,2,8,128]{4,3,2,1,0:T(8,128)S(1)} %all_to_all.5.mine), channel_id=1, source_target_pairs={{0,1},{1,0},{2,3},{3,2},{4,5},{5,4},{6,7},{7,6},{8,9},{9,8},{10,11... | collective-permute-start | bytes 3145736 | tf_op jit(solution)/shard_map/ppermute | solution.py:799
  75.9 11.3 %collective-permute-start.11 = (f32[8,8,1024]{2,1,0:T(8,128)S(1)}, f32[8,8,1024]{2,1,0:T(8,128)S(1)}, u32[]{:S(2)}, u32[]{:S(2)}) collective-permute-start(f32[8,8,1024]{2,1,0:T(8,128)S(1)} %get-tuple-element.98), channel_id=1, source_target_pairs={{0,8},{1,9},{2,10},{3,11},{4,12},{5,13},{6,14},{7,15},{8,16},{9,17... | collective-permute-start | bytes 786440 | tf_op jit(solution)/shard_map/ppermute | solution.py:794
  76.1 11.2 %collective-permute-start.12 = (f32[8,8,1024]{2,1,0:T(8,128)S(1)}, f32[8,8,1024]{2,1,0:T(8,128)S(1)}, u32[]{:S(2)}, u32[]{:S(2)}) collective-permute-start(f32[8,8,1024]{2,1,0:T(8,128)S(1)} %get-tuple-element.99), channel_id=1, source_target_pairs={{0,120},{1,121},{2,122},{3,123},{4,124},{5,125},{6,126},{7,127},{8... | collective-permute-start | bytes 786440 | tf_op jit(solution)/shard_map/ppermute | solution.py:794
  80.8 4.5 %collective-permute-start.13 = (f32[5,8,1024]{2,1,0:T(8,128)S(1)}, f32[5,8,1024]{2,1,0:T(8,128)S(1)}, u32[]{:S(2)}, u32[]{:S(2)}) collective-permute-start(f32[5,8,1024]{2,1,0:T(8,128)S(1)} %get-tuple-element.100), channel_id=1, source_target_pairs={{0,1},{1,2},{2,3},{3,4},{4,5},{5,6},{6,7},{7,0},{8,9},{9,10},{10,1... | collective-permute-start | bytes 491528 | tf_op jit(solution)/shard_map/ppermute | solution.py:794
  82.2 5.0 %collective-permute-start.14 = (f32[5,8,1024]{2,1,0:T(8,128)S(1)}, f32[5,8,1024]{2,1,0:T(8,128)S(1)}, u32[]{:S(2)}, u32[]{:S(2)}) collective-permute-start(f32[5,8,1024]{2,1,0:T(8,128)S(1)} %get-tuple-element.101), channel_id=1, source_target_pairs={{0,7},{1,0},{2,1},{3,2},{4,3},{5,4},{6,5},{7,6},{8,15},{9,8},{10,9... | collective-permute-start | bytes 491528 | tf_op jit(solution)/shard_map/ppermute | solution.py:794
  87.3 4.6 %collective-permute-start.15 = (f32[4,8,1024]{2,1,0:T(8,128)S(1)}, f32[4,8,1024]{2,1,0:T(8,128)S(1)}, u32[]{:S(2)}, u32[]{:S(2)}) collective-permute-start(f32[4,8,1024]{2,1,0:T(8,128)S(1)} %get-tuple-element.106), channel_id=1, source_target_pairs={{0,1},{1,2},{2,3},{3,4},{4,5},{5,6},{6,7},{7,0},{8,9},{9,10},{10,1... | collective-permute-start | bytes 393224 | tf_op jit(solution)/shard_map/ppermute | solution.py:794
  88.4 4.7 %collective-permute-start.16 = (f32[4,8,1024]{2,1,0:T(8,128)S(1)}, f32[4,8,1024]{2,1,0:T(8,128)S(1)}, u32[]{:S(2)}, u32[]{:S(2)}) collective-permute-start(f32[4,8,1024]{2,1,0:T(8,128)S(1)} %get-tuple-element.107), channel_id=1, source_target_pairs={{0,7},{1,0},{2,1},{3,2},{4,3},{5,4},{6,5},{7,6},{8,15},{9,8},{10,9... | collective-permute-start | bytes 393224 | tf_op jit(solution)/shard_map/ppermute | solution.py:794

commit v5 on v4

--- a/solution.py
+++ b/solution.py
@@ -26,6 +26,8 @@
 
 
 def lanes(x, r, k):
+    if callable(x):
+        return x(r, k)
     if isinstance(x, tuple):
         return jnp.concatenate([lanes(part, r, k) for part in x], axis=0)
     return x[r, :, 128 * k : 128 * k + 128]
@@ -116,6 +118,10 @@
     return x[0] if len(x) == 1 else jnp.concatenate(x, axis=0)
 
 
+def level_one_row(x, r):
+    return x[6 + r // 2][:, 512 * (r % 2) : 512 * (r % 2) + 512]
+
+
 def coarse_sum(first, second, split=False):
     halves = [half_columns(x + y) for x, y in zip(first, second)]
     halves = [x + following(x, 1) for x in halves]
@@ -201,7 +207,10 @@
     )(*args)
 
 
-def coarse_coefficients(m, c1, c2):
+def coarse_coefficients(p, d, m, c1, c2, up, down):
+    for n, (x, last, first) in enumerate(((p, 5, 2), (m, 5, 2), (d, 6, 1))):
+        for t in range(2):
+            up[2 * n + t], down[2 * n + t] = x[last, 8 * t : 8 * t + 8], x[first, 8 * t : 8 * t + 8]
     for i in range(4):
         x = coarse_sum(blocks_of(m[2 * i]), blocks_of(m[2 * i + 1]))
         for k, a in enumerate(x):
@@ -209,6 +218,8 @@
     for i in range(2):
         even, odd = coarse_sum(blocks_of(c1[2 * i]), blocks_of(c1[2 * i + 1]), True)
         c2[i] = 0.125 * (even + pltpu.roll(odd, 4, 0))
+        both = jnp.concatenate([c1[2 * i], c1[2 * i + 1]], axis=1)
+        up[6 + i], down[6 + i] = both, both
 
 
 def columns_zero(vp, vm, vd, side):
@@ -232,8 +243,10 @@
     for side, out in ((0, to_left), (1, to_right)):
         tile = slice(8 * side, 8 * side + 8)
         for i in range(2):
-            out[i] = columns_zero(left[1 + i, tile], left[4 + i, tile], left[6 + i, tile], side) * low
-            out[2 + i] = columns_zero(right[i, tile], right[3 + i, tile], right[6 + i, tile], side) * high
+            nothing = jnp.zeros((8, 1024), F32)
+            vd = (left[4, tile] if i == 1 else nothing), (right[4, tile] if i == 0 else nothing)
+            out[i] = columns_zero(left[i, tile], left[2 + i, tile], vd[0], side) * low
+            out[2 + i] = columns_zero(right[i, tile], right[2 + i, tile], vd[1], side) * high
 
 
 def faces(c, rows, fa, fb, fz, w, step):
@@ -259,9 +272,9 @@
     ]
 
 
-def across(r, v, c, s, fa, fz, diagonal, left_over):
-    lane = iota((c.shape[1], 128), 1)
-    count = c.shape[2] // 128
+def across(r, v, c, s, fa, fz, diagonal, left_over, cols=slice(None)):
+    lane = iota(lanes(c, r, 0).shape, 1)
+    count = fa.shape[2] // 128
     turn = lambda x, k: pltpu.roll(lanes(x, r, k), 127, 1) if k < count else 0.0
     here, there, c_next, v_next = lanes(c, r, 0), lanes(v, r, 0), turn(c, 0), turn(v, 0)
     for k in range(count):
@@ -273,45 +286,44 @@
         if k == 0:
             z_before, flux_before = 0.5 * here, 0.5 * here * there
         above, below = 0.5 * (here + lanes(c, r + 1, k)), 0.5 * (here + lanes(c, r - 1, k))
-        fa[r, :, at], fz[r, :, at] = above, z
-        diagonal[r, :, at] = above + below + (z + jnp.where(lane == 0, z_before, z_turned))
+        fa[r, cols, at], fz[r, cols, at] = above, z
+        diagonal[r, cols, at] = above + below + (z + jnp.where(lane == 0, z_before, z_turned))
         a = above * (there - lanes(v, r + 1, k)) + below * (there - lanes(v, r - 1, k))
         a = a + (jnp.where(lane == 0, flux_before, flux_turned) - flux)
-        left_over[r, :, at] = s[r, :, at] - a
+        left_over[r, cols, at] = lanes(s, r, k) - a
         if k + 1 < count:
             here, there = lanes(c, r, k + 1), lanes(v, r, k + 1)
         c_next, v_next, z_before, flux_before = c_later, v_later, z_turned, flux_turned
 
 
-def first_face(c, fa):
-    fa[0] = 0.5 * (c[0] + c[1])
-
-
 def level_zero_own(p, d, m, left, right, v, me, de, fa, fz, diagonal, left_over):
     _, _, _, (low, high, _, _) = scalars()
-    for r in range(14):
+    for r in range(1, 13):
         a = r - 3
         if a < 0:
-            v[r], me[r] = left[r] * low, left[3 + r] * low
-            de[r] = left[5 + r] * low if r > 0 else jnp.zeros((16, 1024), F32)
+            v[r], me[r] = left[r - 1] * low, left[r + 1] * low
         elif a < 8:
             v[r], me[r], de[r] = p[a], m[a], d[a]
         else:
-            v[r], me[r] = right[a - 8] * high, right[a - 5] * high
-            de[r] = right[a - 2] * high if a < 10 else jnp.zeros((16, 1024), F32)
-    first_face(me, fa)
-    over_rows(1, 13, 2, lambda r: across(r, v, me, de, fa, fz, diagonal, left_over))
+            v[r], me[r] = right[a - 8] * high, right[a - 6] * high
+    de[2], de[11] = left[4] * low, right[4] * high
+    fa[1] = 0.5 * (me[1] + me[2])
+    over_rows(2, 12, 2, lambda r: across(r, v, me, de, fa, fz, diagonal, left_over))
 
 
 def level_zero(
-    own_v, own_me, own_de, own_fa, own_fz, own_diagonal, own_left_over, c1, nleft, nright, nleft_edge, nright_edge,
+    own_v, own_me, own_de, own_fa, own_fz, own_diagonal, own_left_over, left, right, nleft, nright,
+    nleft_edge, nright_edge,
     field, s1, up, down, me, de, fa, fz, fb, w, v, u, beside, diagonal, left_over,
 ):
-    _, _, _, (_, _, nlow, nhigh) = scalars()
+    _, _, _, (low, high, nlow, nhigh) = scalars()
     at = iota((8, 1024), 0)
-    for r in (0, 13):
-        beside[r] = me[r] = de[r] = jnp.zeros((8, 1024), F32)
-    for r in range(1, 13):
+    own, halo = slice(0, 16), slice(16, 24)
+    nothing = jnp.zeros((8, 1024), F32)
+    for r in range(14):
+        if r in (0, 13):
+            beside[r], me[r], de[r, halo] = nothing, nothing, nothing
+            continue
         if 3 <= r < 11:
             x, y = nright[r - 3] * nhigh, nleft[r - 3] * nlow
         else:
@@ -321,15 +333,42 @@
         x3, y3 = pltpu.roll(x, 5, 0), pltpu.roll(y, 3, 0)
         me[r] = jnp.where(at < 3, x3, jnp.where(at >= 5, y3, 0.0))
         x6, y6 = pltpu.roll(x, 2, 0), pltpu.roll(y, 6, 0)
-        de[r] = jnp.where(at < 2, x6, jnp.where(at >= 6, y6, 0.0))
-    first_face(me, fa)
-    pairs = [(own_v, beside), (own_me, me), (own_diagonal, diagonal), (own_left_over, left_over)]
-
-    def one(r):
-        across(r, beside, me, de, fa, fz, diagonal, left_over)
+        de[r, halo] = jnp.where(at < 2, x6, jnp.where(at >= 6, y6, 0.0))
+
+    def late(first):
+        rows = (own_v, own_me)[first // 2]
+
+        def row(r, k):
+            if r not in (0, 13):
+                return lanes(rows, r, k)
+            parts = [(left if r == 0 else right)[first + t, :, 128 * k : 128 * k + 128] for t in range(2)]
+            return jnp.concatenate(parts, axis=0) * (low if r == 0 else high)
+
+        return row
+
+    edge_v, edge_c = late(0), late(2)
+    for t in range(2):
+        de[1, 8 * t : 8 * t + 8], de[12, 8 * t : 8 * t + 8] = left[4 + t] * low, right[4 + t] * high
+    for k in range(8):
+        lane = slice(128 * k, 128 * k + 128)
+        fa[0, own, lane] = 0.5 * (edge_c(0, k) + edge_c(1, k))
+    fa[0, halo] = 0.5 * me[1]
+    de_own = lambda r, k: de[r, own, 128 * k : 128 * k + 128]
+    de_halo = lambda r, k: de[r, halo, 128 * k : 128 * k + 128]
+    for r in (1, 12):
+        across(r, edge_v, edge_c, de_own, fa, fz, diagonal, left_over, own)
+
+    def one(r, edge=False):
+        across(r, beside, me, de_halo, fa, fz, diagonal, left_over, halo)
+        if not edge:
+            de[r, own], fa[r, own], fz[r, own] = own_de[r], own_fa[r], own_fz[r]
         for k in range(8):
             lane = slice(128 * k, 128 * k + 128)
-            there, here, total, rest = [lanes(x, r, k) for x in pairs]
+            there, here = lanes((own_v, beside), r, k), lanes((own_me, me), r, k)
+            total, rest = [
+                x[r, :, lane] if edge else jnp.concatenate([y[r, :, lane], x[r, halo, lane]], axis=0)
+                for x, y in ((diagonal, own_diagonal), (left_over, own_left_over))
+            ]
             y = 0.5 * (here + following(here, 0))
             flux = y * (following(there, 0) - there)
             total = total + (y + preceding(y, 0))
@@ -337,8 +376,10 @@
             fb[r, :, lane], w[r, :, lane] = y, factor
             u[r, :, lane] = there + factor * (rest - (preceding(flux, 0) - flux))
 
-    over_rows(1, 13, 2, one)
-    me, de, fa, fz = (own_me, me), (own_de, de), (own_fa, fa), (own_fz, fz)
+    one(1, True)
+    over_rows(2, 12, 2, one)
+    one(12, True)
+    me = (own_me, me)
     sweep(u, v, de, me, fa, fb, fz, w, (2, 12), 3)
     field[...] = v[3:11, 0:16]
 
@@ -351,39 +392,38 @@
         return carry
 
     lax.fori_loop(0, 4, coarse, 0)
-    up[0:3], down[0:3] = s1[1:4], s1[0:3]
-    up[3:7], down[3:7] = c1[...], c1[...]
-
-
-def pack_one(s, c, left, right, to_left, to_right):
+    up[...], down[...] = s1[1:4], s1[0:3]
+
+
+def pack_one(s, c, left, right, c_left, c_right, to_left, to_right):
     _, _, _, (low, high, _, _) = scalars()
     at = iota((8, 512), 0)
     for r in range(1, 11):
         a = r - 4
         if a < 0:
-            vc = left[3 + r] * low
+            vc = level_one_row(c_left, r) * low
             vs = left[r - 1] * low if r > 0 else jnp.zeros_like(vc)
         elif a < 4:
             vs, vc = s[a], c[a]
         else:
-            vc = right[a - 1] * high
+            vc = level_one_row(c_right, a - 4) * high
             vs = right[a - 4] * high if a < 7 else jnp.zeros_like(vc)
         to_left[r - 1] = jnp.where(at < 4, vc, pltpu.roll(vs, 4, 0))
         to_right[r - 1] = jnp.where(at >= 4, vc, pltpu.roll(vs, 4, 0))
 
 
-def level_one(s, c, left, right, nleft, nright, f0, field, s2, up, down, se, ce, fa, fb, fz, w, v, u):
+def level_one(s, c, left, right, c_left, c_right, nleft, nright, f0, field, s2, up, down, se, ce, fa, fb, fz, w, v, u):
     _, _, _, (low, high, nlow, nhigh) = scalars()
     at = iota((8, 512), 0)
     for r in range(12):
         a = r - 4
         if a < 0:
-            ce[r, 0:8] = left[3 + r] * low
+            ce[r, 0:8] = level_one_row(c_left, r) * low
             se[r, 0:8] = left[r - 1] * low if r > 0 else jnp.zeros((8, 512), F32)
         elif a < 4:
             se[r, 0:8], ce[r, 0:8] = s[a], c[a]
         else:
-            ce[r, 0:8] = right[a - 1] * high
+            ce[r, 0:8] = level_one_row(c_right, a - 4) * high
             se[r, 0:8] = right[a - 4] * high if a < 7 else jnp.zeros((8, 512), F32)
         if r in (0, 11):
             ce[r, 8:16] = se[r, 8:16] = jnp.zeros((8, 512), F32)
@@ -443,7 +483,7 @@
 
 
 def level_up(
-    own_me, own_de, own_fa, own_fz, me, de, fa, fz, fb, w, se, ce, fa1, fb1, fz1, w1,
+    own_me, me, de, fa, fz, fb, w, se, ce, fa1, fb1, fz1, w1,
     f0, f1, left, right, nleft, nright, nleft_edge, nright_edge, e2,
     out, res, v, u, v1, u1, kept, sent,
 ):
@@ -495,10 +535,10 @@
         for t, (part, index) in enumerate(pieces):
             fine = widen(take_rows(part, index), 8)
             tile = slice(8 * t, 8 * t + 8)
-            inside = own_me[r, tile] if t < 2 else me[r]
+            inside = own_me[min(max(r, 1), 12), tile] if t < 2 else me[r]
             v[r, tile] = f[t] + jnp.where(inside > 0.0, fine, 0.0)
 
-    me, de, fa, fz = (own_me, me), (own_de, de), (own_fa, fa), (own_fz, fz)
+    me = (own_me, me)
     sweep(v, u, de, me, fa, fb, fz, w, (1, 13), 3)
     sweep(u, v, de, me, fa, fb, fz, w, (2, 12), 3)
     first = pltpu.make_async_copy(v.at[3:11, 0:16], out, sent.at[0])
@@ -806,10 +846,13 @@
 
 
 def per_device(p, d, m):
-    up = jnp.concatenate([p[5:8], m[5:8], d[6:8]], axis=0)
-    down = jnp.concatenate([p[0:3], m[0:3], d[0:2]], axis=0)
+    up = jnp.concatenate([p[6:8], m[6:8], d[7:8]], axis=0)
+    down = jnp.concatenate([p[0:2], m[0:2], d[0:1]], axis=0)
     left, right = moved(up, 1, 0), moved(down, -1, 0)
-    c1, c2 = call(coarse_coefficients, [(4, 8, 512), (2, 8, 128)], [], m)
+    c1, c2, up, down = call(
+        coarse_coefficients, [(4, 8, 512), (2, 8, 128)] + [(8, 8, 1024)] * 2, [], p, d, m
+    )
+    c_left, c_right = moved(up, 1, 0), moved(down, -1, 0)
     to_left, to_right = call(pack_zero_own, [(8, 8, 1024)] * 2, [], p, d, m)
     nleft, nright = moved(to_right, 0, 1), moved(to_left, 0, -1)
     left, right, nleft, nright = lax.optimization_barrier((left, right, nleft, nright))
@@ -819,21 +862,21 @@
     alone = call(level_zero_own, [own] * 7, [], p, d, m, left, right, flops=20_000_000)
     f0, s1, up, down, *zero = call(
         level_zero,
-        [(8, 16, 1024), (4, 8, 512)] + [(7, 8, 512)] * 2 + [halo] * 4 + [big] * 2,
-        [big] * 2 + [halo] * 3,
-        *alone, c1, nleft, nright, nleft_edge, nright_edge,
+        [(8, 16, 1024), (4, 8, 512)] + [(3, 8, 512)] * 2 + [halo] + [big] * 5,
+        [big] * 2 + [halo] + [big] * 2,
+        *alone, c_left, c_right, nleft, nright, nleft_edge, nright_edge,
         flops=30_000_000,
     )
-    zero = [*alone[1:5], *zero]
+    zero = [alone[1], *zero]
     left1, right1 = moved(up, 1, 0), moved(down, -1, 0)
-    to_left, to_right = call(pack_one, [(10, 8, 512)] * 2, [], s1, c1, left1, right1)
+    to_left, to_right = call(pack_one, [(10, 8, 512)] * 2, [], s1, c1, left1, right1, c_left, c_right)
     nleft1, nright1 = moved(to_right, 0, 1), moved(to_left, 0, -1)
     mid = (12, 16, 512)
     f1, s2, up, down, *one = call(
         level_one,
         [(4, 8, 512), (2, 8, 128)] + [(8, 8, 1024)] * 2 + [mid] * 6,
         [mid] * 2,
-        s1, c1, left1, right1, nleft1, nright1, f0,
+        s1, c1, left1, right1, c_left, c_right, nleft1, nright1, f0,
         flops=10_000_000,
     )
     hleft, hright = moved(up, 1, 0), moved(down, -1, 0)

time: 98.8 us -> 96 us (0.972)
  waiting for transfers between devices: 22.4 us -> 14.1 us
  starting transfers between devices: 24.7 us -> 30.4 us
    ppermute x16 -> x18, waiting for transfers between devices: 22.4 us -> 14.1 us  [moved(): return lax.ppermute(x, AX, pairs)]
    ppermute x16 -> x18, starting transfers between devices: 24.7 us -> 30 us  [moved(): return lax.ppermute(x, AX, pairs)]
  transfers between devices with their start and end apart: 17 -> 19, of which waited for: 9 -> 11; matrix products, arithmetic and copies ran while one was open for 0% -> 0% of each run, Pallas kernels for 9% -> 9%
where the time goes in v5:
time: 96 us; the launch traced here: 95.8 us
  starting transfers between devices  30.4 us (32%)
  blocking collectives  28.1 us (29%)
  Pallas kernels  19.8 us (21%)
  waiting for transfers between devices  14.1 us (15%)
  local copies, waits for them, and re-layouts  2.26 us (2%)
  between operations  0.97 us (1%)
    ppermute x18, starting transfers between devices, moved(): return lax.ppermute(x, AX, pairs)  30 us
    all_to_all x1, blocking collectives, gathered(): lax.all_to_all(jnp.broadcast_to(both[None], (chips,) + both.shape), ('wid...  28.1 us
    pallas_call x12, Pallas kernels, call(): pl.pallas_call(kernel, out_shape=[jax.ShapeDtypeStruct(s, F32) for s in o...  19.8 us
    ppermute x18, waiting for transfers between devices, moved(): return lax.ppermute(x, AX, pairs)  14.1 us
    slice x2, local copies, waits for them, and re-layouts, per_device(): down = jnp.concatenate([p[0:2], m[0:2], d[0:1]], axis=0)  2.13 us
  transfers between devices with their start and end apart: 19, of which 11 were waited for; matrix products, arithmetic and copies ran while one was open for 0% of the time, Pallas kernels for 9%

profile of v5, /device:TPU:1, one launch (start us, length us, event | category | flops | bytes accessed | tf_op | source)
XLA Modules:
  0.0 95.8 jit_solution(419501119231441020)
XLA Ops:
  1.7 1.1 %fusion = (f32[2,16,1024]{2,1,0:T(8,128)S(1)}, f32[2,16,1024]{2,1,0:T(8,128)S(1)}, f32[2,16,1024]{2,1,0:T(8,128)S(1)}, f32[2,16,1024]{2,1,0:T(8,128)S(1)}) fusion(f32[8,16,1024]{2,1,0:T(8,128)} %p.5, f32[8,16,1024]{2,1,0:T(8,128)} %m.5), kind=kLoop, calls=%fused_computation.3 | loop fusion | bytes 1048576 | tf_op jit(solution)/shard_map/slice | solution.py:850
  2.8 2.5 %collective-permute-start = (f32[5,16,1024]{2,1,0:T(8,128)S(1)}, f32[5,16,1024]{2,1,0:T(8,128)S(1)}, u32[]{:S(2)}, u32[]{:S(2)}) collective-permute-start(f32[5,16,1024]{2,1,0:T(8,128)S(1)} %pad_maximum_fusion), channel_id=1, source_target_pairs={{0,8},{1,9},{2,10},{3,11},{4,12},{5,13},{6,14},{7,15},{8,16},{9,17... | collective-permute-start | bytes 983048 | tf_op jit(solution)/shard_map/ppermute | solution.py:834
  5.5 2.1 %collective-permute-start.2 = (f32[8,8,1024]{2,1,0:T(8,128)S(1)}, f32[8,8,1024]{2,1,0:T(8,128)S(1)}, u32[]{:S(2)}, u32[]{:S(2)}) collective-permute-start(f32[8,8,1024]{2,1,0:T(8,128)S(1)} %get-tuple-element.62), channel_id=1, source_target_pairs={{0,1},{1,2},{2,3},{3,4},{4,5},{5,6},{6,7},{7,0},{8,9},{9,10},{10,1... | collective-permute-start | bytes 786440 | tf_op jit(solution)/shard_map/ppermute | solution.py:834
  7.6 4.1 %collective-permute-start.1 = (f32[5,16,1024]{2,1,0:T(8,128)S(1)}, f32[5,16,1024]{2,1,0:T(8,128)S(1)}, u32[]{:S(2)}, u32[]{:S(2)}) collective-permute-start(f32[5,16,1024]{2,1,0:T(8,128)S(1)} %pad_maximum_fusion.1), channel_id=1, source_target_pairs={{0,120},{1,121},{2,122},{3,123},{4,124},{5,125},{6,126},{7,127},{8... | collective-permute-start | bytes 983048 | tf_op jit(solution)/shard_map/ppermute | solution.py:834
  12.2 4.8 %collective-permute-start.5 = (f32[8,8,1024]{2,1,0:T(8,128)S(1)}, f32[8,8,1024]{2,1,0:T(8,128)S(1)}, u32[]{:S(2)}, u32[]{:S(2)}) collective-permute-start(f32[8,8,1024]{2,1,0:T(8,128)S(1)} %get-tuple-element.74), channel_id=1, source_target_pairs={{0,120},{1,121},{2,122},{3,123},{4,124},{5,125},{6,126},{7,127},{8... | collective-permute-start | bytes 786440 | tf_op jit(solution)/shard_map/ppermute | solution.py:834
  19.6 1.6 %shard_map.51 = (f32[14,16,1024]{2,1,0:T(8,128)S(1)}, f32[14,16,1024]{2,1,0:T(8,128)S(1)}, f32[14,16,1024]{2,1,0:T(8,128)S(1)}, f32[14,16,1024]{2,1,0:T(8,128)S(...) custom-call(f32[8,16,1024]{2,1,0:T(8,128)S(1)} %copy-done, ...), custom_call_target="tpu_custom_call" | custom-call | flops 20000000 | bytes 2228224 | tf_op jit(solution)/shard_map/pallas_call | solution.py:199
  21.5 1.2 %collective-permute-done.5.right.c_right = f32[8,8,1024]{2,1,0:T(8,128)S(1)} collective-permute-done((f32[8,8,1024]{2,1,0:T(8,128)S(1)}, f32[8,8,1024]{2,1,0:T(8,128)S(1)}, u32[]{:S(2)}, u32[]{:S(2)}) %collective-permute-start.5) | collective-permute-done | bytes 262176 | tf_op jit(solution)/shard_map/ppermute | solution.py:834
  22.8 1.5 %collective-permute-done.7.nright_edge = f32[4,8,1024]{2,1,0:T(8,128)S(1)} collective-permute-done((f32[4,8,1024]{2,1,0:T(8,128)S(1)}, f32[4,8,1024]{2,1,0:T(8,128)S(1)}, u32[]{:S(2)}, u32[]{:S(2)}) %collective-permute-start.7) | collective-permute-done | bytes 131104 | tf_op jit(solution)/shard_map/ppermute | solution.py:834
  24.3 4.4 %shard_map.54 = (f32[8,16,1024]{2,1,0:T(8,128)S(1)}, f32[4,8,512]{2,1,0:T(8,128)S(1)}, f32[3,8,512]{2,1,0:T(8,128)S(1)}, f32[3,8,512]{2,1,0:T(8,128)S(1)}, f32[1...) custom-call(f32[14,16,1024]{2,1,0:T(8,128)S(1)} %get-tuple-element.6, ...), custom_call_target="tpu_custom_call" | custom-call | flops 30000000 | bytes 7733248 | tf_op jit(solution)/shard_map/pallas_call | solution.py:199
  28.8 5.5 %collective-permute-start.9 = (f32[3,8,512]{2,1,0:T(8,128)S(1)}, f32[3,8,512]{2,1,0:T(8,128)S(1)}, u32[]{:S(2)}, u32[]{:S(2)}) collective-permute-start(f32[3,8,512]{2,1,0:T(8,128)S(1)} %get-tuple-element.88), channel_id=1, source_target_pairs={{0,120},{1,121},{2,122},{3,123},{4,124},{5,125},{6,126},{7,127},{8... | collective-permute-start | bytes 147464 | tf_op jit(solution)/shard_map/ppermute | solution.py:834
  34.3 1.4 %collective-permute-done.8.left = f32[3,8,512]{2,1,0:T(8,128)S(1)} collective-permute-done((f32[3,8,512]{2,1,0:T(8,128)S(1)}, f32[3,8,512]{2,1,0:T(8,128)S(1)}, u32[]{:S(2)}, u32[]{:S(2)}) %collective-permute-start.8) | collective-permute-done | bytes 49184 | tf_op jit(solution)/shard_map/ppermute | solution.py:834
  35.8 2.5 %collective-permute-start.10 = (f32[10,8,512]{2,1,0:T(8,128)S(1)}, f32[10,8,512]{2,1,0:T(8,128)S(1)}, u32[]{:S(2)}, u32[]{:S(2)}) collective-permute-start(f32[10,8,512]{2,1,0:T(8,128)S(1)} %get-tuple-element.89), channel_id=1, source_target_pairs={{0,1},{1,2},{2,3},{3,4},{4,5},{5,6},{6,7},{7,0},{8,9},{9,10},{10,1... | collective-permute-start | bytes 491528 | tf_op jit(solution)/shard_map/ppermute | solution.py:834
  38.3 2.3 %collective-permute-done.10.nleft = f32[10,8,512]{2,1,0:T(8,128)S(1)} collective-permute-done((f32[10,8,512]{2,1,0:T(8,128)S(1)}, f32[10,8,512]{2,1,0:T(8,128)S(1)}, u32[]{:S(2)}, u32[]{:S(2)}) %collective-permute-start.10) | collective-permute-done | bytes 163872 | tf_op jit(solution)/shard_map/ppermute | solution.py:834
  40.5 2.5 %collective-permute-done.11.nright = f32[10,8,512]{2,1,0:T(8,128)S(1)} collective-permute-done((f32[10,8,512]{2,1,0:T(8,128)S(1)}, f32[10,8,512]{2,1,0:T(8,128)S(1)}, u32[]{:S(2)}, u32[]{:S(2)}) %collective-permute-start.11) | collective-permute-done | bytes 163872 | tf_op jit(solution)/shard_map/ppermute | solution.py:834
  43.0 1.1 %shard_map.56 = (f32[4,8,512]{2,1,0:T(8,128)S(1)}, f32[2,8,128]{2,1,0:T(8,128)S(1)}, f32[8,8,1024]{2,1,0:T(8,128)S(1)}, f32[8,8,1024]{2,1,0:T(8,128)S(1)}, f32[1...) custom-call(f32[4,8,512]{2,1,0:T(8,128)S(1)} %get-tuple-element.85.s, ...), custom_call_target="tpu_custom_call" | custom-call | flops 10000000 | bytes 1605632 | tf_op jit(solution)/shard_map/pallas_call | solution.py:199
  44.3 28.1 %all_to_all.5.mine = f32[64,2,2,8,128]{4,3,2,1,0:T(8,128)S(1)} all-to-all(f32[64,2,2,8,128]{4,3,2,1,0:T(8,128)S(1)} %broadcast_in_dim.2), channel_id=1, replica_groups=mesh['wide'=16,'ny'=4,'core'=2] {'wide','ny'}, dimensions={0} | all-to-all | bytes 2097152 | tf_op jit(solution)/shard_map/all_to_all | solution.py:845
  73.1 4.5 %collective-permute-start.14 = (f32[8,8,1024]{2,1,0:T(8,128)S(1)}, f32[8,8,1024]{2,1,0:T(8,128)S(1)}, u32[]{:S(2)}, u32[]{:S(2)}) collective-permute-start(f32[8,8,1024]{2,1,0:T(8,128)S(1)} %get-tuple-element.103), channel_id=1, source_target_pairs={{0,120},{1,121},{2,122},{3,123},{4,124},{5,125},{6,126},{7,127},{8... | collective-permute-start | bytes 786440 | tf_op jit(solution)/shard_map/ppermute | solution.py:834
  77.6 1.0 %collective-permute-start.15 = (f32[5,8,1024]{2,1,0:T(8,128)S(1)}, f32[5,8,1024]{2,1,0:T(8,128)S(1)}, u32[]{:S(2)}, u32[]{:S(2)}) collective-permute-start(f32[5,8,1024]{2,1,0:T(8,128)S(1)} %get-tuple-element.104), channel_id=1, source_target_pairs={{0,1},{1,2},{2,3},{3,4},{4,5},{5,6},{6,7},{7,0},{8,9},{9,10},{10,1... | collective-permute-start | bytes 491528 | tf_op jit(solution)/shard_map/ppermute | solution.py:834
  78.7 3.0 %shard_map.57 = (f32[34,32,256]{2,1,0:T(8,128)S(1)}, f32[34,32,256]{2,1,0:T(8,128)S(1)}, f32[34,32,256]{2,1,0:T(8,128)S(1)}, f32[34,32,256]{2,1,0:T(8,128)S(1)},...) custom-call(f32[64,2,2,8,128]{4,3,2,1,0:T(8,128)S(1)} %all_to_all.5., ...), custom_call_target="tpu_custom_call" | custom-call | flops 1000 | tf_op jit(solution)/shard_map/pallas_call | solution.py:199
  81.8 2.0 %collective-permute-done.16.nright = f32[5,8,1024]{2,1,0:T(8,128)S(1)} collective-permute-done((f32[5,8,1024]{2,1,0:T(8,128)S(1)}, f32[5,8,1024]{2,1,0:T(8,128)S(1)}, u32[]{:S(2)}, u32[]{:S(2)}) %collective-permute-start.16) | collective-permute-done | bytes 163872 | tf_op jit(solution)/shard_map/ppermute | solution.py:834
  84.0 1.4 %collective-permute-start.17 = (f32[4,8,1024]{2,1,0:T(8,128)S(1)}, f32[4,8,1024]{2,1,0:T(8,128)S(1)}, u32[]{:S(2)}, u32[]{:S(2)}) collective-permute-start(f32[4,8,1024]{2,1,0:T(8,128)S(1)} %get-tuple-element.110), channel_id=1, source_target_pairs={{0,1},{1,2},{2,3},{3,4},{4,5},{5,6},{6,7},{7,0},{8,9},{9,10},{10,1... | collective-permute-start | bytes 393224 | tf_op jit(solution)/shard_map/ppermute | solution.py:834
  85.4 3.5 %shard_map.60.e2 = f32[6,8,256]{2,1,0:T(8,128)S(1)} custom-call(f32[16,16,128]{2,1,0:T(8,128)S(1)} %get-tuple-element.112.s3, f32[16,16,128]{2,1,0:T(8,128)S(1)} %get-tuple-element.113.c3, f32[34,32,256]{2,1,0:T(8,128)S(1)} %get-tuple-element.114.s, f32[34,32,256]{2,1,0:T(8,128)S(1)} %get-tuple-element.115.c, f32[34,32,256]{2,1,0:T(8,128)S(1)} %get-tuple-element.116.v, ...), custom_call_target="tpu_custom_call" | custom-call | flops 1000 | tf_op jit(solution)/shard_map/pallas_call | solution.py:199
  88.9 1.2 %collective-permute-done.18.nright_edge = f32[4,8,1024]{2,1,0:T(8,128)S(1)} collective-permute-done((f32[4,8,1024]{2,1,0:T(8,128)S(1)}, f32[4,8,1024]{2,1,0:T(8,128)S(1)}, u32[]{:S(2)}, u32[]{:S(2)}) %collective-permute-start.18) | collective-permute-done | bytes 131104 | tf_op jit(solution)/shard_map/ppermute | solution.py:834
  90.1 5.6 %shard_map.61 = (f32[8,16,1024]{2,1,0:T(8,128)}, f32[8,16,1024]{2,1,0:T(8,128)}) custom-call(f32[14,16,1024]{2,1,0:T(8,128)S(1)} %get-tuple-element.66.own_me, f32[14,8,1024]{2,1,0:T(8,128)S(1)} %get-tuple-element.79.me, f32[14,24,1024]{2,1,0:T(8,128)S(1)} %get-tuple-element.80.de, f32[14,24,1024]{2,1,0:T(8,128)S(1)} %get-tuple-element.81.fa, ...), custom_call_target="tpu_custom_call" | custom-call | flops 30000000 | bytes 12369920 | tf_op jit(solution)/shard_map/pallas_call | solution.py:199
  (39 shorter events, 5.7 us)
Async XLA Ops:
  0.6 4.7 %copy-start.2 = (f32[8,16,1024]{2,1,0:T(8,128)S(1)}, f32[8,16,1024]{2,1,0:T(8,128)}, u32[]{:S(2)}) copy-start(f32[8,16,1024]{2,1,0:T(8,128)} %d.5) | copy-start | bytes 1572868
  0.6 4.7 %copy-start = (f32[8,16,1024]{2,1,0:T(8,128)S(1)}, f32[8,16,1024]{2,1,0:T(8,128)}, u32[]{:S(2)}) copy-start(f32[8,16,1024]{2,1,0:T(8,128)} %p.5) | copy-start | bytes 1572868
  0.7 4.7 %copy-start.1 = (f32[8,16,1024]{2,1,0:T(8,128)S(1)}, f32[8,16,1024]{2,1,0:T(8,128)}, u32[]{:S(2)}) copy-start(f32[8,16,1024]{2,1,0:T(8,128)} %m.5) | copy-start | bytes 1572868
  2.8 15.0 %collective-permute-start = (f32[5,16,1024]{2,1,0:T(8,128)S(1)}, f32[5,16,1024]{2,1,0:T(8,128)S(1)}, u32[]{:S(2)}, u32[]{:S(2)}) collective-permute-start(f32[5,16,1024]{2,1,0:T(8,128)S(1)} %pad_maximum_fusion), channel_id=1, source_target_pairs={{0,8},{1,9},{2,10},{3,11},{4,12},{5,13},{6,14},{7,15},{8,16},{9,17... | collective-permute-start | bytes 983048 | tf_op jit(solution)/shard_map/ppermute | solution.py:834
  5.5 6.8 %collective-permute-start.2 = (f32[8,8,1024]{2,1,0:T(8,128)S(1)}, f32[8,8,1024]{2,1,0:T(8,128)S(1)}, u32[]{:S(2)}, u32[]{:S(2)}) collective-permute-start(f32[8,8,1024]{2,1,0:T(8,128)S(1)} %get-tuple-element.62), channel_id=1, source_target_pairs={{0,1},{1,2},{2,3},{3,4},{4,5},{5,6},{6,7},{7,0},{8,9},{9,10},{10,1... | collective-permute-start | bytes 786440 | tf_op jit(solution)/shard_map/ppermute | solution.py:834
  7.6 11.0 %collective-permute-start.1 = (f32[5,16,1024]{2,1,0:T(8,128)S(1)}, f32[5,16,1024]{2,1,0:T(8,128)S(1)}, u32[]{:S(2)}, u32[]{:S(2)}) collective-permute-start(f32[5,16,1024]{2,1,0:T(8,128)S(1)} %pad_maximum_fusion.1), channel_id=1, source_target_pairs={{0,120},{1,121},{2,122},{3,123},{4,124},{5,125},{6,126},{7,127},{8... | collective-permute-start | bytes 983048 | tf_op jit(solution)/shard_map/ppermute | solution.py:834
  11.8 6.1 %collective-permute-start.3 = (f32[8,8,1024]{2,1,0:T(8,128)S(1)}, f32[8,8,1024]{2,1,0:T(8,128)S(1)}, u32[]{:S(2)}, u32[]{:S(2)}) collective-permute-start(f32[8,8,1024]{2,1,0:T(8,128)S(1)} %get-tuple-element.63), channel_id=1, source_target_pairs={{0,7},{1,0},{2,1},{3,2},{4,3},{5,4},{6,5},{7,6},{8,15},{9,8},{10,9... | collective-permute-start | bytes 786440 | tf_op jit(solution)/shard_map/ppermute | solution.py:834
  12.1 9.4 %collective-permute-start.4 = (f32[8,8,1024]{2,1,0:T(8,128)S(1)}, f32[8,8,1024]{2,1,0:T(8,128)S(1)}, u32[]{:S(2)}, u32[]{:S(2)}) collective-permute-start(f32[8,8,1024]{2,1,0:T(8,128)S(1)} %get-tuple-element.73), channel_id=1, source_target_pairs={{0,8},{1,9},{2,10},{3,11},{4,12},{5,13},{6,14},{7,15},{8,16},{9,17... | collective-permute-start | bytes 786440 | tf_op jit(solution)/shard_map/ppermute | solution.py:834
  12.2 10.5 %collective-permute-start.5 = (f32[8,8,1024]{2,1,0:T(8,128)S(1)}, f32[8,8,1024]{2,1,0:T(8,128)S(1)}, u32[]{:S(2)}, u32[]{:S(2)}) collective-permute-start(f32[8,8,1024]{2,1,0:T(8,128)S(1)} %get-tuple-element.74), channel_id=1, source_target_pairs={{0,120},{1,121},{2,122},{3,123},{4,124},{5,125},{6,126},{7,127},{8... | collective-permute-start | bytes 786440 | tf_op jit(solution)/shard_map/ppermute | solution.py:834
  18.6 4.1 %collective-permute-start.6 = (f32[4,8,1024]{2,1,0:T(8,128)S(1)}, f32[4,8,1024]{2,1,0:T(8,128)S(1)}, u32[]{:S(2)}, u32[]{:S(2)}) collective-permute-start(f32[4,8,1024]{2,1,0:T(8,128)S(1)} %get-tuple-element.77), channel_id=1, source_target_pairs={{0,1},{1,2},{2,3},{3,4},{4,5},{5,6},{6,7},{7,0},{8,9},{9,10},{10,1... | collective-permute-start | bytes 393224 | tf_op jit(solution)/shard_map/ppermute | solution.py:834
  19.6 4.7 %collective-permute-start.7 = (f32[4,8,1024]{2,1,0:T(8,128)S(1)}, f32[4,8,1024]{2,1,0:T(8,128)S(1)}, u32[]{:S(2)}, u32[]{:S(2)}) collective-permute-start(f32[4,8,1024]{2,1,0:T(8,128)S(1)} %get-tuple-element.78), channel_id=1, source_target_pairs={{0,7},{1,0},{2,1},{3,2},{4,3},{5,4},{6,5},{7,6},{8,15},{9,8},{10,9... | collective-permute-start | bytes 393224 | tf_op jit(solution)/shard_map/ppermute | solution.py:834
  28.7 7.0 %collective-permute-start.8 = (f32[3,8,512]{2,1,0:T(8,128)S(1)}, f32[3,8,512]{2,1,0:T(8,128)S(1)}, u32[]{:S(2)}, u32[]{:S(2)}) collective-permute-start(f32[3,8,512]{2,1,0:T(8,128)S(1)} %get-tuple-element.87), channel_id=1, source_target_pairs={{0,8},{1,9},{2,10},{3,11},{4,12},{5,13},{6,14},{7,15},{8,16},{9,17... | collective-permute-start | bytes 147464 | tf_op jit(solution)/shard_map/ppermute | solution.py:834
  28.8 6.9 %collective-permute-start.9 = (f32[3,8,512]{2,1,0:T(8,128)S(1)}, f32[3,8,512]{2,1,0:T(8,128)S(1)}, u32[]{:S(2)}, u32[]{:S(2)}) collective-permute-start(f32[3,8,512]{2,1,0:T(8,128)S(1)} %get-tuple-element.88), channel_id=1, source_target_pairs={{0,120},{1,121},{2,122},{3,123},{4,124},{5,125},{6,126},{7,127},{8... | collective-permute-start | bytes 147464 | tf_op jit(solution)/shard_map/ppermute | solution.py:834
  35.8 4.8 %collective-permute-start.10 = (f32[10,8,512]{2,1,0:T(8,128)S(1)}, f32[10,8,512]{2,1,0:T(8,128)S(1)}, u32[]{:S(2)}, u32[]{:S(2)}) collective-permute-start(f32[10,8,512]{2,1,0:T(8,128)S(1)} %get-tuple-element.89), channel_id=1, source_target_pairs={{0,1},{1,2},{2,3},{3,4},{4,5},{5,6},{6,7},{7,0},{8,9},{9,10},{10,1... | collective-permute-start | bytes 491528 | tf_op jit(solution)/shard_map/ppermute | solution.py:834
  38.3 4.7 %collective-permute-start.11 = (f32[10,8,512]{2,1,0:T(8,128)S(1)}, f32[10,8,512]{2,1,0:T(8,128)S(1)}, u32[]{:S(2)}, u32[]{:S(2)}) collective-permute-start(f32[10,8,512]{2,1,0:T(8,128)S(1)} %get-tuple-element.90), channel_id=1, source_target_pairs={{0,7},{1,0},{2,1},{3,2},{4,3},{5,4},{6,5},{7,6},{8,15},{9,8},{10,9... | collective-permute-start | bytes 491528 | tf_op jit(solution)/shard_map/ppermute | solution.py:834
  72.4 6.3 %collective-permute-start.12 = (f32[64,2,2,8,128]{4,3,2,1,0:T(8,128)S(1)}, f32[64,2,2,8,128]{4,3,2,1,0:T(8,128)S(1)}, u32[]{:S(2)}, u32[]{:S(2)}) collective-permute-start(f32[64,2,2,8,128]{4,3,2,1,0:T(8,128)S(1)} %all_to_all.5.mine), channel_id=1, source_target_pairs={{0,1},{1,0},{2,3},{3,2},{4,5},{5,4},{6,7},{7,6},{8,9},{9,8},{10,11... | collective-permute-start | bytes 3145736 | tf_op jit(solution)/shard_map/ppermute | solution.py:839
  72.8 11.1 %collective-permute-start.13 = (f32[8,8,1024]{2,1,0:T(8,128)S(1)}, f32[8,8,1024]{2,1,0:T(8,128)S(1)}, u32[]{:S(2)}, u32[]{:S(2)}) collective-permute-start(f32[8,8,1024]{2,1,0:T(8,128)S(1)} %get-tuple-element.102), channel_id=1, source_target_pairs={{0,8},{1,9},{2,10},{3,11},{4,12},{5,13},{6,14},{7,15},{8,16},{9,17... | collective-permute-start | bytes 786440 | tf_op jit(solution)/shard_map/ppermute | solution.py:834
  73.1 10.8 %collective-permute-start.14 = (f32[8,8,1024]{2,1,0:T(8,128)S(1)}, f32[8,8,1024]{2,1,0:T(8,128)S(1)}, u32[]{:S(2)}, u32[]{:S(2)}) collective-permute-start(f32[8,8,1024]{2,1,0:T(8,128)S(1)} %get-tuple-element.103), channel_id=1, source_target_pairs={{0,120},{1,121},{2,122},{3,123},{4,124},{5,125},{6,126},{7,127},{8... | collective-permute-start | bytes 786440 | tf_op jit(solution)/shard_map/ppermute | solution.py:834
  77.6 4.1 %collective-permute-start.15 = (f32[5,8,1024]{2,1,0:T(8,128)S(1)}, f32[5,8,1024]{2,1,0:T(8,128)S(1)}, u32[]{:S(2)}, u32[]{:S(2)}) collective-permute-start(f32[5,8,1024]{2,1,0:T(8,128)S(1)} %get-tuple-element.104), channel_id=1, source_target_pairs={{0,1},{1,2},{2,3},{3,4},{4,5},{5,6},{6,7},{7,0},{8,9},{9,10},{10,1... | collective-permute-start | bytes 491528 | tf_op jit(solution)/shard_map/ppermute | solution.py:834
  78.7 5.0 %collective-permute-start.16 = (f32[5,8,1024]{2,1,0:T(8,128)S(1)}, f32[5,8,1024]{2,1,0:T(8,128)S(1)}, u32[]{:S(2)}, u32[]{:S(2)}) collective-permute-start(f32[5,8,1024]{2,1,0:T(8,128)S(1)} %get-tuple-element.105), channel_id=1, source_target_pairs={{0,7},{1,0},{2,1},{3,2},{4,3},{5,4},{6,5},{7,6},{8,15},{9,8},{10,9... | collective-permute-start | bytes 491528 | tf_op jit(solution)/shard_map/ppermute | solution.py:834
  84.0 5.0 %collective-permute-start.17 = (f32[4,8,1024]{2,1,0:T(8,128)S(1)}, f32[4,8,1024]{2,1,0:T(8,128)S(1)}, u32[]{:S(2)}, u32[]{:S(2)}) collective-permute-start(f32[4,8,1024]{2,1,0:T(8,128)S(1)} %get-tuple-element.110), channel_id=1, source_target_pairs={{0,1},{1,2},{2,3},{3,4},{4,5},{5,6},{6,7},{7,0},{8,9},{9,10},{10,1... | collective-permute-start | bytes 393224 | tf_op jit(solution)/shard_map/ppermute | solution.py:834
  85.4 4.7 %collective-permute-start.18 = (f32[4,8,1024]{2,1,0:T(8,128)S(1)}, f32[4,8,1024]{2,1,0:T(8,128)S(1)}, u32[]{:S(2)}, u32[]{:S(2)}) collective-permute-start(f32[4,8,1024]{2,1,0:T(8,128)S(1)} %get-tuple-element.111), channel_id=1, source_target_pairs={{0,7},{1,0},{2,1},{3,2},{4,3},{5,4},{6,5},{7,6},{8,15},{9,8},{10,9... | collective-permute-start | bytes 393224 | tf_op jit(solution)/shard_map/ppermute | solution.py:834

commit v6 on v5

--- a/solution.py
+++ b/solution.py
@@ -207,7 +207,8 @@
     )(*args)
 
 
-def coarse_coefficients(p, d, m, c1, c2, up, down):
+def before_exchange(p, d, m, c1, c2, up, down, to_left, to_right):
+    pack_zero_own(p, d, m, to_left, to_right)
     for n, (x, last, first) in enumerate(((p, 5, 2), (m, 5, 2), (d, 6, 1))):
         for t in range(2):
             up[2 * n + t], down[2 * n + t] = x[last, 8 * t : 8 * t + 8], x[first, 8 * t : 8 * t + 8]
@@ -377,7 +378,7 @@
             u[r, :, lane] = there + factor * (rest - (preceding(flux, 0) - flux))
 
     one(1, True)
-    over_rows(2, 12, 2, one)
+    over_rows(2, 12, 5, one)
     one(12, True)
     me = (own_me, me)
     sweep(u, v, de, me, fa, fb, fz, w, (2, 12), 3)
@@ -849,11 +850,10 @@
     up = jnp.concatenate([p[6:8], m[6:8], d[7:8]], axis=0)
     down = jnp.concatenate([p[0:2], m[0:2], d[0:1]], axis=0)
     left, right = moved(up, 1, 0), moved(down, -1, 0)
-    c1, c2, up, down = call(
-        coarse_coefficients, [(4, 8, 512), (2, 8, 128)] + [(8, 8, 1024)] * 2, [], p, d, m
+    c1, c2, up, down, to_left, to_right = call(
+        before_exchange, [(4, 8, 512), (2, 8, 128)] + [(8, 8, 1024)] * 4, [], p, d, m
     )
     c_left, c_right = moved(up, 1, 0), moved(down, -1, 0)
-    to_left, to_right = call(pack_zero_own, [(8, 8, 1024)] * 2, [], p, d, m)
     nleft, nright = moved(to_right, 0, 1), moved(to_left, 0, -1)
     left, right, nleft, nright = lax.optimization_barrier((left, right, nleft, nright))
     to_left, to_right = call(pack_zero_edge, [(4, 8, 1024)] * 2, [], left, right)

time: 96 us -> 95.7 us (level)
    pallas_call x12 -> x11, Pallas kernels: 19.8 us -> 19.8 us  [call(): pl.pallas_call(kernel, out_shape=[jax.ShapeDtypeStruct(s, F32) for s in o...]
  transfers between devices with their start and end apart: 19 -> 19, of which waited for: 11 -> 9; matrix products, arithmetic and copies ran while one was open for 0% -> 0% of each run, Pallas kernels for 9% -> 9%
where the time goes in v6:
time: 95.7 us; the launch traced here: 95.5 us
  starting transfers between devices  30.1 us (31%)
  blocking collectives  28 us (29%)
  Pallas kernels  19.8 us (21%)
  waiting for transfers between devices  14.3 us (15%)
  local copies, waits for them, and re-layouts  2.26 us (2%)
  between operations  0.97 us (1%)
    ppermute x18, starting transfers between devices, moved(): return lax.ppermute(x, AX, pairs)  30 us
    all_to_all x1, blocking collectives, gathered(): lax.all_to_all(jnp.broadcast_to(both[None], (chips,) + both.shape), ('wid...  28 us
    pallas_call x11, Pallas kernels, call(): pl.pallas_call(kernel, out_shape=[jax.ShapeDtypeStruct(s, F32) for s in o...  19.8 us
    ppermute x18, waiting for transfers between devices, moved(): return lax.ppermute(x, AX, pairs)  14.3 us
    slice x2, local copies, waits for them, and re-layouts, per_device(): down = jnp.concatenate([p[0:2], m[0:2], d[0:1]], axis=0)  2.13 us
  transfers between devices with their start and end apart: 19, of which 9 were waited for; matrix products, arithmetic and copies ran while one was open for 0% of the time, Pallas kernels for 9%

profile of v6, /device:TPU:1, one launch (start us, length us, event | category | flops | bytes accessed | tf_op | source)
XLA Modules:
  0.0 95.5 jit_solution(16927225159333091184)
XLA Ops:
  1.7 1.1 %fusion = (f32[2,16,1024]{2,1,0:T(8,128)S(1)}, f32[2,16,1024]{2,1,0:T(8,128)S(1)}, f32[2,16,1024]{2,1,0:T(8,128)S(1)}, f32[2,16,1024]{2,1,0:T(8,128)S(1)}) fusion(f32[8,16,1024]{2,1,0:T(8,128)} %p.3, f32[8,16,1024]{2,1,0:T(8,128)} %m.3), kind=kLoop, calls=%fused_computation.3 | loop fusion | bytes 1048576 | tf_op jit(solution)/shard_map/slice | solution.py:851
  2.8 2.5 %collective-permute-start = (f32[5,16,1024]{2,1,0:T(8,128)S(1)}, f32[5,16,1024]{2,1,0:T(8,128)S(1)}, u32[]{:S(2)}, u32[]{:S(2)}) collective-permute-start(f32[5,16,1024]{2,1,0:T(8,128)S(1)} %pad_maximum_fusion), channel_id=1, source_target_pairs={{0,8},{1,9},{2,10},{3,11},{4,12},{5,13},{6,14},{7,15},{8,16},{9,17... | collective-permute-start | bytes 983048 | tf_op jit(solution)/shard_map/ppermute | solution.py:835
  5.8 2.1 %collective-permute-start.2 = (f32[8,8,1024]{2,1,0:T(8,128)S(1)}, f32[8,8,1024]{2,1,0:T(8,128)S(1)}, u32[]{:S(2)}, u32[]{:S(2)}) collective-permute-start(f32[8,8,1024]{2,1,0:T(8,128)S(1)} %get-tuple-element.62), channel_id=1, source_target_pairs={{0,1},{1,2},{2,3},{3,4},{4,5},{5,6},{6,7},{7,0},{8,9},{9,10},{10,1... | collective-permute-start | bytes 786440 | tf_op jit(solution)/shard_map/ppermute | solution.py:835
  8.0 4.1 %collective-permute-start.1 = (f32[5,16,1024]{2,1,0:T(8,128)S(1)}, f32[5,16,1024]{2,1,0:T(8,128)S(1)}, u32[]{:S(2)}, u32[]{:S(2)}) collective-permute-start(f32[5,16,1024]{2,1,0:T(8,128)S(1)} %pad_maximum_fusion.1), channel_id=1, source_target_pairs={{0,120},{1,121},{2,122},{3,123},{4,124},{5,125},{6,126},{7,127},{8... | collective-permute-start | bytes 983048 | tf_op jit(solution)/shard_map/ppermute | solution.py:835
  12.1 4.8 %collective-permute-start.5 = (f32[8,8,1024]{2,1,0:T(8,128)S(1)}, f32[8,8,1024]{2,1,0:T(8,128)S(1)}, u32[]{:S(2)}, u32[]{:S(2)}) collective-permute-start(f32[8,8,1024]{2,1,0:T(8,128)S(1)} %get-tuple-element.74), channel_id=1, source_target_pairs={{0,120},{1,121},{2,122},{3,123},{4,124},{5,125},{6,126},{7,127},{8... | collective-permute-start | bytes 786440 | tf_op jit(solution)/shard_map/ppermute | solution.py:835
  16.9 1.3 %collective-permute-done.3.nright = f32[8,8,1024]{2,1,0:T(8,128)S(1)} collective-permute-done((f32[8,8,1024]{2,1,0:T(8,128)S(1)}, f32[8,8,1024]{2,1,0:T(8,128)S(1)}, u32[]{:S(2)}, u32[]{:S(2)}) %collective-permute-start.3) | collective-permute-done | bytes 262176 | tf_op jit(solution)/shard_map/ppermute | solution.py:835
  19.9 1.6 %shard_map.51 = (f32[14,16,1024]{2,1,0:T(8,128)S(1)}, f32[14,16,1024]{2,1,0:T(8,128)S(1)}, f32[14,16,1024]{2,1,0:T(8,128)S(1)}, f32[14,16,1024]{2,1,0:T(8,128)S(...) custom-call(f32[8,16,1024]{2,1,0:T(8,128)S(1)} %copy-done, ...), custom_call_target="tpu_custom_call" | custom-call | flops 20000000 | bytes 2228224 | tf_op jit(solution)/shard_map/pallas_call | solution.py:199
  21.5 2.0 %collective-permute-done.5.right.c_right = f32[8,8,1024]{2,1,0:T(8,128)S(1)} collective-permute-done((f32[8,8,1024]{2,1,0:T(8,128)S(1)}, f32[8,8,1024]{2,1,0:T(8,128)S(1)}, u32[]{:S(2)}, u32[]{:S(2)}) %collective-permute-start.5) | collective-permute-done | bytes 262176 | tf_op jit(solution)/shard_map/ppermute | solution.py:835
  24.5 4.4 %shard_map.53 = (f32[8,16,1024]{2,1,0:T(8,128)S(1)}, f32[4,8,512]{2,1,0:T(8,128)S(1)}, f32[3,8,512]{2,1,0:T(8,128)S(1)}, f32[3,8,512]{2,1,0:T(8,128)S(1)}, f32[1...) custom-call(f32[14,16,1024]{2,1,0:T(8,128)S(1)} %get-tuple-element.6, ...), custom_call_target="tpu_custom_call" | custom-call | flops 30000000 | bytes 7733248 | tf_op jit(solution)/shard_map/pallas_call | solution.py:199
  29.0 5.6 %collective-permute-start.9 = (f32[3,8,512]{2,1,0:T(8,128)S(1)}, f32[3,8,512]{2,1,0:T(8,128)S(1)}, u32[]{:S(2)}, u32[]{:S(2)}) collective-permute-start(f32[3,8,512]{2,1,0:T(8,128)S(1)} %get-tuple-element.88), channel_id=1, source_target_pairs={{0,120},{1,121},{2,122},{3,123},{4,124},{5,125},{6,126},{7,127},{8... | collective-permute-start | bytes 147464 | tf_op jit(solution)/shard_map/ppermute | solution.py:835
  34.6 1.4 %collective-permute-done.8.left = f32[3,8,512]{2,1,0:T(8,128)S(1)} collective-permute-done((f32[3,8,512]{2,1,0:T(8,128)S(1)}, f32[3,8,512]{2,1,0:T(8,128)S(1)}, u32[]{:S(2)}, u32[]{:S(2)}) %collective-permute-start.8) | collective-permute-done | bytes 49184 | tf_op jit(solution)/shard_map/ppermute | solution.py:835
  36.0 2.5 %collective-permute-start.10 = (f32[10,8,512]{2,1,0:T(8,128)S(1)}, f32[10,8,512]{2,1,0:T(8,128)S(1)}, u32[]{:S(2)}, u32[]{:S(2)}) collective-permute-start(f32[10,8,512]{2,1,0:T(8,128)S(1)} %get-tuple-element.89), channel_id=1, source_target_pairs={{0,1},{1,2},{2,3},{3,4},{4,5},{5,6},{6,7},{7,0},{8,9},{9,10},{10,1... | collective-permute-start | bytes 491528 | tf_op jit(solution)/shard_map/ppermute | solution.py:835
  38.5 2.3 %collective-permute-done.10.nleft = f32[10,8,512]{2,1,0:T(8,128)S(1)} collective-permute-done((f32[10,8,512]{2,1,0:T(8,128)S(1)}, f32[10,8,512]{2,1,0:T(8,128)S(1)}, u32[]{:S(2)}, u32[]{:S(2)}) %collective-permute-start.10) | collective-permute-done | bytes 163872 | tf_op jit(solution)/shard_map/ppermute | solution.py:835
  40.8 2.5 %collective-permute-done.11.nright = f32[10,8,512]{2,1,0:T(8,128)S(1)} collective-permute-done((f32[10,8,512]{2,1,0:T(8,128)S(1)}, f32[10,8,512]{2,1,0:T(8,128)S(1)}, u32[]{:S(2)}, u32[]{:S(2)}) %collective-permute-start.11) | collective-permute-done | bytes 163872 | tf_op jit(solution)/shard_map/ppermute | solution.py:835
  43.3 1.1 %shard_map.55 = (f32[4,8,512]{2,1,0:T(8,128)S(1)}, f32[2,8,128]{2,1,0:T(8,128)S(1)}, f32[8,8,1024]{2,1,0:T(8,128)S(1)}, f32[8,8,1024]{2,1,0:T(8,128)S(1)}, f32[1...) custom-call(f32[4,8,512]{2,1,0:T(8,128)S(1)} %get-tuple-element.85.s, ...), custom_call_target="tpu_custom_call" | custom-call | flops 10000000 | bytes 1605632 | tf_op jit(solution)/shard_map/pallas_call | solution.py:199
  44.6 28.0 %all_to_all.5.mine = f32[64,2,2,8,128]{4,3,2,1,0:T(8,128)S(1)} all-to-all(f32[64,2,2,8,128]{4,3,2,1,0:T(8,128)S(1)} %broadcast_in_dim.2), channel_id=1, replica_groups=mesh['wide'=16,'ny'=4,'core'=2] {'wide','ny'}, dimensions={0} | all-to-all | bytes 2097152 | tf_op jit(solution)/shard_map/all_to_all | solution.py:846
  72.7 4.8 %collective-permute-start.14 = (f32[8,8,1024]{2,1,0:T(8,128)S(1)}, f32[8,8,1024]{2,1,0:T(8,128)S(1)}, u32[]{:S(2)}, u32[]{:S(2)}) collective-permute-start(f32[8,8,1024]{2,1,0:T(8,128)S(1)} %get-tuple-element.103), channel_id=1, source_target_pairs={{0,120},{1,121},{2,122},{3,123},{4,124},{5,125},{6,126},{7,127},{8... | collective-permute-start | bytes 786440 | tf_op jit(solution)/shard_map/ppermute | solution.py:835
  77.5 1.2 %collective-permute-start.15 = (f32[5,8,1024]{2,1,0:T(8,128)S(1)}, f32[5,8,1024]{2,1,0:T(8,128)S(1)}, u32[]{:S(2)}, u32[]{:S(2)}) collective-permute-start(f32[5,8,1024]{2,1,0:T(8,128)S(1)} %get-tuple-element.104), channel_id=1, source_target_pairs={{0,1},{1,2},{2,3},{3,4},{4,5},{5,6},{6,7},{7,0},{8,9},{9,10},{10,1... | collective-permute-start | bytes 491528 | tf_op jit(solution)/shard_map/ppermute | solution.py:835
  78.7 3.0 %shard_map.56 = (f32[34,32,256]{2,1,0:T(8,128)S(1)}, f32[34,32,256]{2,1,0:T(8,128)S(1)}, f32[34,32,256]{2,1,0:T(8,128)S(1)}, f32[34,32,256]{2,1,0:T(8,128)S(1)},...) custom-call(f32[64,2,2,8,128]{4,3,2,1,0:T(8,128)S(1)} %all_to_all.5., ...), custom_call_target="tpu_custom_call" | custom-call | flops 1000 | tf_op jit(solution)/shard_map/pallas_call | solution.py:199
  81.8 2.0 %collective-permute-done.16.nright = f32[5,8,1024]{2,1,0:T(8,128)S(1)} collective-permute-done((f32[5,8,1024]{2,1,0:T(8,128)S(1)}, f32[5,8,1024]{2,1,0:T(8,128)S(1)}, u32[]{:S(2)}, u32[]{:S(2)}) %collective-permute-start.16) | collective-permute-done | bytes 163872 | tf_op jit(solution)/shard_map/ppermute | solution.py:835
  83.8 1.3 %collective-permute-start.17 = (f32[4,8,1024]{2,1,0:T(8,128)S(1)}, f32[4,8,1024]{2,1,0:T(8,128)S(1)}, u32[]{:S(2)}, u32[]{:S(2)}) collective-permute-start(f32[4,8,1024]{2,1,0:T(8,128)S(1)} %get-tuple-element.110), channel_id=1, source_target_pairs={{0,1},{1,2},{2,3},{3,4},{4,5},{5,6},{6,7},{7,0},{8,9},{9,10},{10,1... | collective-permute-start | bytes 393224 | tf_op jit(solution)/shard_map/ppermute | solution.py:835
  85.1 3.5 %shard_map.59.e2 = f32[6,8,256]{2,1,0:T(8,128)S(1)} custom-call(f32[16,16,128]{2,1,0:T(8,128)S(1)} %get-tuple-element.112.s3, f32[16,16,128]{2,1,0:T(8,128)S(1)} %get-tuple-element.113.c3, f32[34,32,256]{2,1,0:T(8,128)S(1)} %get-tuple-element.114.s, f32[34,32,256]{2,1,0:T(8,128)S(1)} %get-tuple-element.115.c, f32[34,32,256]{2,1,0:T(8,128)S(1)} %get-tuple-element.116.v, ...), custom_call_target="tpu_custom_call" | custom-call | flops 1000 | tf_op jit(solution)/shard_map/pallas_call | solution.py:199
  88.6 1.2 %collective-permute-done.18.nright_edge = f32[4,8,1024]{2,1,0:T(8,128)S(1)} collective-permute-done((f32[4,8,1024]{2,1,0:T(8,128)S(1)}, f32[4,8,1024]{2,1,0:T(8,128)S(1)}, u32[]{:S(2)}, u32[]{:S(2)}) %collective-permute-start.18) | collective-permute-done | bytes 131104 | tf_op jit(solution)/shard_map/ppermute | solution.py:835
  89.8 5.6 %shard_map.60 = (f32[8,16,1024]{2,1,0:T(8,128)}, f32[8,16,1024]{2,1,0:T(8,128)}) custom-call(f32[14,16,1024]{2,1,0:T(8,128)S(1)} %get-tuple-element.66.own_me, f32[14,8,1024]{2,1,0:T(8,128)S(1)} %get-tuple-element.79.me, f32[14,24,1024]{2,1,0:T(8,128)S(1)} %get-tuple-element.80.de, f32[14,24,1024]{2,1,0:T(8,128)S(1)} %get-tuple-element.81.fa, ...), custom_call_target="tpu_custom_call" | custom-call | flops 30000000 | bytes 12369920 | tf_op jit(solution)/shard_map/pallas_call | solution.py:199
  (38 shorter events, 4.6 us)
Async XLA Ops:
  0.6 4.7 %copy-start.2 = (f32[8,16,1024]{2,1,0:T(8,128)S(1)}, f32[8,16,1024]{2,1,0:T(8,128)}, u32[]{:S(2)}) copy-start(f32[8,16,1024]{2,1,0:T(8,128)} %d.3) | copy-start | bytes 1572868
  0.6 4.7 %copy-start = (f32[8,16,1024]{2,1,0:T(8,128)S(1)}, f32[8,16,1024]{2,1,0:T(8,128)}, u32[]{:S(2)}) copy-start(f32[8,16,1024]{2,1,0:T(8,128)} %p.3) | copy-start | bytes 1572868
  0.7 4.7 %copy-start.1 = (f32[8,16,1024]{2,1,0:T(8,128)S(1)}, f32[8,16,1024]{2,1,0:T(8,128)}, u32[]{:S(2)}) copy-start(f32[8,16,1024]{2,1,0:T(8,128)} %m.3) | copy-start | bytes 1572868
  2.8 15.4 %collective-permute-start = (f32[5,16,1024]{2,1,0:T(8,128)S(1)}, f32[5,16,1024]{2,1,0:T(8,128)S(1)}, u32[]{:S(2)}, u32[]{:S(2)}) collective-permute-start(f32[5,16,1024]{2,1,0:T(8,128)S(1)} %pad_maximum_fusion), channel_id=1, source_target_pairs={{0,8},{1,9},{2,10},{3,11},{4,12},{5,13},{6,14},{7,15},{8,16},{9,17... | collective-permute-start | bytes 983048 | tf_op jit(solution)/shard_map/ppermute | solution.py:835
  5.8 6.3 %collective-permute-start.2 = (f32[8,8,1024]{2,1,0:T(8,128)S(1)}, f32[8,8,1024]{2,1,0:T(8,128)S(1)}, u32[]{:S(2)}, u32[]{:S(2)}) collective-permute-start(f32[8,8,1024]{2,1,0:T(8,128)S(1)} %get-tuple-element.62), channel_id=1, source_target_pairs={{0,1},{1,2},{2,3},{3,4},{4,5},{5,6},{6,7},{7,0},{8,9},{9,10},{10,1... | collective-permute-start | bytes 786440 | tf_op jit(solution)/shard_map/ppermute | solution.py:835
  8.0 11.0 %collective-permute-start.1 = (f32[5,16,1024]{2,1,0:T(8,128)S(1)}, f32[5,16,1024]{2,1,0:T(8,128)S(1)}, u32[]{:S(2)}, u32[]{:S(2)}) collective-permute-start(f32[5,16,1024]{2,1,0:T(8,128)S(1)} %pad_maximum_fusion.1), channel_id=1, source_target_pairs={{0,120},{1,121},{2,122},{3,123},{4,124},{5,125},{6,126},{7,127},{8... | collective-permute-start | bytes 983048 | tf_op jit(solution)/shard_map/ppermute | solution.py:835
  12.1 6.1 %collective-permute-start.3 = (f32[8,8,1024]{2,1,0:T(8,128)S(1)}, f32[8,8,1024]{2,1,0:T(8,128)S(1)}, u32[]{:S(2)}, u32[]{:S(2)}) collective-permute-start(f32[8,8,1024]{2,1,0:T(8,128)S(1)} %get-tuple-element.63), channel_id=1, source_target_pairs={{0,7},{1,0},{2,1},{3,2},{4,3},{5,4},{6,5},{7,6},{8,15},{9,8},{10,9... | collective-permute-start | bytes 786440 | tf_op jit(solution)/shard_map/ppermute | solution.py:835
  12.1 9.4 %collective-permute-start.4 = (f32[8,8,1024]{2,1,0:T(8,128)S(1)}, f32[8,8,1024]{2,1,0:T(8,128)S(1)}, u32[]{:S(2)}, u32[]{:S(2)}) collective-permute-start(f32[8,8,1024]{2,1,0:T(8,128)S(1)} %get-tuple-element.73), channel_id=1, source_target_pairs={{0,8},{1,9},{2,10},{3,11},{4,12},{5,13},{6,14},{7,15},{8,16},{9,17... | collective-permute-start | bytes 786440 | tf_op jit(solution)/shard_map/ppermute | solution.py:835
  12.1 11.4 %collective-permute-start.5 = (f32[8,8,1024]{2,1,0:T(8,128)S(1)}, f32[8,8,1024]{2,1,0:T(8,128)S(1)}, u32[]{:S(2)}, u32[]{:S(2)}) collective-permute-start(f32[8,8,1024]{2,1,0:T(8,128)S(1)} %get-tuple-element.74), channel_id=1, source_target_pairs={{0,120},{1,121},{2,122},{3,123},{4,124},{5,125},{6,126},{7,127},{8... | collective-permute-start | bytes 786440 | tf_op jit(solution)/shard_map/ppermute | solution.py:835
  19.0 4.5 %collective-permute-start.6 = (f32[4,8,1024]{2,1,0:T(8,128)S(1)}, f32[4,8,1024]{2,1,0:T(8,128)S(1)}, u32[]{:S(2)}, u32[]{:S(2)}) collective-permute-start(f32[4,8,1024]{2,1,0:T(8,128)S(1)} %get-tuple-element.77), channel_id=1, source_target_pairs={{0,1},{1,2},{2,3},{3,4},{4,5},{5,6},{6,7},{7,0},{8,9},{9,10},{10,1... | collective-permute-start | bytes 393224 | tf_op jit(solution)/shard_map/ppermute | solution.py:835
  19.9 4.6 %collective-permute-start.7 = (f32[4,8,1024]{2,1,0:T(8,128)S(1)}, f32[4,8,1024]{2,1,0:T(8,128)S(1)}, u32[]{:S(2)}, u32[]{:S(2)}) collective-permute-start(f32[4,8,1024]{2,1,0:T(8,128)S(1)} %get-tuple-element.78), channel_id=1, source_target_pairs={{0,7},{1,0},{2,1},{3,2},{4,3},{5,4},{6,5},{7,6},{8,15},{9,8},{10,9... | collective-permute-start | bytes 393224 | tf_op jit(solution)/shard_map/ppermute | solution.py:835
  28.9 7.1 %collective-permute-start.8 = (f32[3,8,512]{2,1,0:T(8,128)S(1)}, f32[3,8,512]{2,1,0:T(8,128)S(1)}, u32[]{:S(2)}, u32[]{:S(2)}) collective-permute-start(f32[3,8,512]{2,1,0:T(8,128)S(1)} %get-tuple-element.87), channel_id=1, source_target_pairs={{0,8},{1,9},{2,10},{3,11},{4,12},{5,13},{6,14},{7,15},{8,16},{9,17... | collective-permute-start | bytes 147464 | tf_op jit(solution)/shard_map/ppermute | solution.py:835
  29.0 7.0 %collective-permute-start.9 = (f32[3,8,512]{2,1,0:T(8,128)S(1)}, f32[3,8,512]{2,1,0:T(8,128)S(1)}, u32[]{:S(2)}, u32[]{:S(2)}) collective-permute-start(f32[3,8,512]{2,1,0:T(8,128)S(1)} %get-tuple-element.88), channel_id=1, source_target_pairs={{0,120},{1,121},{2,122},{3,123},{4,124},{5,125},{6,126},{7,127},{8... | collective-permute-start | bytes 147464 | tf_op jit(solution)/shard_map/ppermute | solution.py:835
  36.0 4.8 %collective-permute-start.10 = (f32[10,8,512]{2,1,0:T(8,128)S(1)}, f32[10,8,512]{2,1,0:T(8,128)S(1)}, u32[]{:S(2)}, u32[]{:S(2)}) collective-permute-start(f32[10,8,512]{2,1,0:T(8,128)S(1)} %get-tuple-element.89), channel_id=1, source_target_pairs={{0,1},{1,2},{2,3},{3,4},{4,5},{5,6},{6,7},{7,0},{8,9},{9,10},{10,1... | collective-permute-start | bytes 491528 | tf_op jit(solution)/shard_map/ppermute | solution.py:835
  38.5 4.7 %collective-permute-start.11 = (f32[10,8,512]{2,1,0:T(8,128)S(1)}, f32[10,8,512]{2,1,0:T(8,128)S(1)}, u32[]{:S(2)}, u32[]{:S(2)}) collective-permute-start(f32[10,8,512]{2,1,0:T(8,128)S(1)} %get-tuple-element.90), channel_id=1, source_target_pairs={{0,7},{1,0},{2,1},{3,2},{4,3},{5,4},{6,5},{7,6},{8,15},{9,8},{10,9... | collective-permute-start | bytes 491528 | tf_op jit(solution)/shard_map/ppermute | solution.py:835
  72.6 6.1 %collective-permute-start.12 = (f32[64,2,2,8,128]{4,3,2,1,0:T(8,128)S(1)}, f32[64,2,2,8,128]{4,3,2,1,0:T(8,128)S(1)}, u32[]{:S(2)}, u32[]{:S(2)}) collective-permute-start(f32[64,2,2,8,128]{4,3,2,1,0:T(8,128)S(1)} %all_to_all.5.mine), channel_id=1, source_target_pairs={{0,1},{1,0},{2,3},{3,2},{4,5},{5,4},{6,7},{7,6},{8,9},{9,8},{10,11... | collective-permute-start | bytes 3145736 | tf_op jit(solution)/shard_map/ppermute | solution.py:840
  72.7 11.1 %collective-permute-start.13 = (f32[8,8,1024]{2,1,0:T(8,128)S(1)}, f32[8,8,1024]{2,1,0:T(8,128)S(1)}, u32[]{:S(2)}, u32[]{:S(2)}) collective-permute-start(f32[8,8,1024]{2,1,0:T(8,128)S(1)} %get-tuple-element.102), channel_id=1, source_target_pairs={{0,8},{1,9},{2,10},{3,11},{4,12},{5,13},{6,14},{7,15},{8,16},{9,17... | collective-permute-start | bytes 786440 | tf_op jit(solution)/shard_map/ppermute | solution.py:835
  72.7 11.0 %collective-permute-start.14 = (f32[8,8,1024]{2,1,0:T(8,128)S(1)}, f32[8,8,1024]{2,1,0:T(8,128)S(1)}, u32[]{:S(2)}, u32[]{:S(2)}) collective-permute-start(f32[8,8,1024]{2,1,0:T(8,128)S(1)} %get-tuple-element.103), channel_id=1, source_target_pairs={{0,120},{1,121},{2,122},{3,123},{4,124},{5,125},{6,126},{7,127},{8... | collective-permute-start | bytes 786440 | tf_op jit(solution)/shard_map/ppermute | solution.py:835
  77.5 4.3 %collective-permute-start.15 = (f32[5,8,1024]{2,1,0:T(8,128)S(1)}, f32[5,8,1024]{2,1,0:T(8,128)S(1)}, u32[]{:S(2)}, u32[]{:S(2)}) collective-permute-start(f32[5,8,1024]{2,1,0:T(8,128)S(1)} %get-tuple-element.104), channel_id=1, source_target_pairs={{0,1},{1,2},{2,3},{3,4},{4,5},{5,6},{6,7},{7,0},{8,9},{9,10},{10,1... | collective-permute-start | bytes 491528 | tf_op jit(solution)/shard_map/ppermute | solution.py:835
  78.7 5.0 %collective-permute-start.16 = (f32[5,8,1024]{2,1,0:T(8,128)S(1)}, f32[5,8,1024]{2,1,0:T(8,128)S(1)}, u32[]{:S(2)}, u32[]{:S(2)}) collective-permute-start(f32[5,8,1024]{2,1,0:T(8,128)S(1)} %get-tuple-element.105), channel_id=1, source_target_pairs={{0,7},{1,0},{2,1},{3,2},{4,3},{5,4},{6,5},{7,6},{8,15},{9,8},{10,9... | collective-permute-start | bytes 491528 | tf_op jit(solution)/shard_map/ppermute | solution.py:835
  83.8 4.8 %collective-permute-start.17 = (f32[4,8,1024]{2,1,0:T(8,128)S(1)}, f32[4,8,1024]{2,1,0:T(8,128)S(1)}, u32[]{:S(2)}, u32[]{:S(2)}) collective-permute-start(f32[4,8,1024]{2,1,0:T(8,128)S(1)} %get-tuple-element.110), channel_id=1, source_target_pairs={{0,1},{1,2},{2,3},{3,4},{4,5},{5,6},{6,7},{7,0},{8,9},{9,10},{10,1... | collective-permute-start | bytes 393224 | tf_op jit(solution)/shard_map/ppermute | solution.py:835
  85.1 4.7 %collective-permute-start.18 = (f32[4,8,1024]{2,1,0:T(8,128)S(1)}, f32[4,8,1024]{2,1,0:T(8,128)S(1)}, u32[]{:S(2)}, u32[]{:S(2)}) collective-permute-start(f32[4,8,1024]{2,1,0:T(8,128)S(1)} %get-tuple-element.111), channel_id=1, source_target_pairs={{0,7},{1,0},{2,1},{3,2},{4,3},{5,4},{6,5},{7,6},{8,15},{9,8},{10,9... | collective-permute-start | bytes 393224 | tf_op jit(solution)/shard_map/ppermute | solution.py:835
